TPU v7x, 32 devices: a whole 2x2x4 slice. The times are simulated.
32 devices in a mesh: layer: 4 (over z), feat: 8 (over y, x, core).
Axes of the slice: x: 2, y: 2, z: 4, core: 2. Of those that a mesh axis runs over, the one named last changes fastest.
Arguments:
- resid: bfloat16 [8, 256, 4096], P('layer', None, 'feat'), may hold values from -6 to 6
- enc: bfloat16 [8, 4096, 4096], P('layer', None, 'feat'), may hold values from -0.09375 to 0.09375
- enc_bias: float32 [8, 4096], P('layer', 'feat'), may hold values from -3 to 3
- fire: int32 [8, 256, 4096], P('layer', None, 'feat'), may hold values 0 or 1
- dec: bfloat16 [36, 4096, 4096], P('layer', 'feat'), may hold values from -0.125 to 0.125
- dec_bias: bfloat16 [8, 4096], P('layer', 'feat'), may hold values from -2 to 2
- target: bfloat16 [8, 256, 4096], P('layer', None, 'feat'), may hold values from -6 to 6
Outputs:
- error: bfloat16 [8, 256, 4096], P('layer', None, 'feat')
- act_grad: float32 [8, 256, 4096], P('layer', None, 'feat')
All inputs are finite; a program needn't handle non-finite values. No bound on the sum of `fire` on one device may be relied on, other than what follows from the above.
Results may differ from a plain program's by a relative error of at most 0.0085.
Values may be sent and summed in bfloat16 or wider, within the bound.
No kernel may reach another device: no remote copies, remote signals or barrier semaphores. Data moves between devices by JAX's collectives and lax.ppermute only.
A program may use at most 192 MiB of HBM per device.

v0:
```python
import jax
import jax.numpy as jnp
from jax import lax
from jax.sharding import PartitionSpec as P

LAYERS = 8


def on_device(resid, enc, enc_bias, fire, dec, dec_bias, target):
    group = lax.axis_index("layer")
    half = LAYERS // 2
    pre = jnp.einsum(
        "ltd,ldf->ltf",
        lax.all_gather(resid, "feat", axis=2, tiled=True),
        enc,
        preferred_element_type=jnp.float32,
    )
    acts = (fire.astype(jnp.float32) * (pre + enc_bias[:, None, :])).astype(jnp.bfloat16)
    every = lax.all_gather(acts, "layer", axis=0, tiled=True)
    order = jnp.arange(LAYERS + 1, dtype=jnp.int32)
    early = order <= group
    source_ids = jnp.where(early, order, order - group - 1)
    chosen = jnp.take(every, source_ids, axis=0)
    lead_mask = early[:half].astype(jnp.bfloat16)[:, None, None]
    lead_acts = chosen[:half]
    low = jnp.einsum(
        "ktf,kfd->td", lead_acts * lead_mask, dec[:half], preferred_element_type=jnp.float32
    )
    high = jnp.einsum(
        "ktf,kfd->td", lead_acts * (1 - lead_mask), dec[:half], preferred_element_type=jnp.float32
    )
    high = high + jnp.einsum(
        "ktf,kfd->td", chosen[half:], dec[half:], preferred_element_type=jnp.float32
    )
    partial_value = jnp.stack([low, high])
    recon = lax.psum(partial_value, "feat")
    whole_target, whole_bias = (
        lax.all_gather(target, "feat", axis=2, tiled=True),
        lax.all_gather(dec_bias, "feat", axis=1, tiled=True),
    )
    wide_error = (
        recon + whole_bias.astype(jnp.float32)[:, None, :] - whole_target.astype(jnp.float32)
    ).astype(jnp.bfloat16)
    columns = target.shape[2]
    error = lax.dynamic_slice_in_dim(wide_error, lax.axis_index("feat") * columns, columns, 2)
    lead_error = jnp.where(early[:half, None, None], wide_error[0][None], wide_error[1][None])
    grads_lead = jnp.einsum(
        "ktd,kfd->ktf", lead_error, dec[:half], preferred_element_type=jnp.float32
    )
    grads_rest = jnp.einsum(
        "td,kfd->ktf", wide_error[1], dec[half:], preferred_element_type=jnp.float32
    )
    pair_grads = jnp.concatenate([grads_lead, grads_rest], axis=0)
    one_hot = (source_ids[:, None] == jnp.arange(LAYERS, dtype=jnp.int32)[None, :]).astype(
        jnp.float32
    )
    grad_terms = jnp.einsum("ks,ktf->stf", one_hot, pair_grads, precision=lax.Precision.HIGHEST)
    summed = lax.psum_scatter(
        grad_terms.astype(jnp.bfloat16), "layer", scatter_dimension=0, tiled=True
    ).astype(jnp.float32)
    act_grad = fire.astype(jnp.float32) * summed
    return (error, act_grad)


def solution(mesh):
    placed = (
        P("layer", None, "feat"),
        P("layer", None, "feat"),
        P("layer", "feat"),
        P("layer", None, "feat"),
        P("layer", "feat", None),
        P("layer", "feat"),
        P("layer", None, "feat"),
    )
    return jax.shard_map(
        on_device,
        mesh=mesh,
        in_specs=placed,
        out_specs=(P("layer", None, "feat"), P("layer", None, "feat")),
        check_vma=False,
    )
```

profile of v0, /device:TPU:10, one launch (start us, length us, event | category | flops | bytes accessed | tf_op | source)
XLA Modules:
  0.0 361.6 jit_solution(1028037676478747829)
XLA Ops:
  7.2 0.0 all-gather.4.cloned.1.call-start
  7.2 0.7 all-gather.4.cloned.1.call-update
  7.9 0.0 all-gather.6.cloned.1.call-start
  7.9 40.5 %all-gather.4.cloned.1.call-done = bf16[2,256,4096]{2,1,0:T(8,128)(2,1)} async-done(((bf16[2,256,512]{2,1,0:T(8,128)(2,1)}), bf16[2,256,4096]{2,1,0:T(8,128)(2,1)}) %all-gather.4.cloned.1.call-update) | async-done | bytes 4194320 | tf_op jit(solution)/shard_map/all_gather | solution.py:14
  48.5 7.9 %fusion.36 = bf16[2,256,512]{2,1,0:T(8,128)(2,1)} fusion(bf16[2,256,4096]{2,1,0:T(8,128)(2,1)} %all-gather.4.cloned.1.call-done, bf16[2,4096,512]{2,1,0:T(8,128)(2,1)} %param.8, s32[2,256,512]{2,1,0:T(8,128)} %param.10, f32[2,512]{1,0:T(2,128)} %param.9), kind=kOutput, calls=%fused_computation.35 | convolution fusion | flops 2148532224 | bytes 14159872 | tf_op jit(solution)/shard_map/ltd,ldf->ltf/dot_general | solution.py:12
  56.4 0.0 all-gather.6.cloned.1.call-update
  56.4 0.0 all-gather.8.cloned.1.call-start
  56.5 0.7 all-gather.8.cloned.1.call-update
  57.2 0.0 all-reduce.2.cloned.1.call-start
  57.3 43.6 %all-gather.6.cloned.1.call-done = bf16[8,256,512]{2,1,0:T(8,128)(2,1)} async-done(((bf16[2,256,512]{2,1,0:T(8,128)(2,1)}), bf16[8,256,512]{2,1,0:T(8,128)(2,1)}) %all-gather.6.cloned.1.call-update) | async-done | bytes 2097168 | tf_op jit(solution)/shard_map/all_gather | solution.py:19
  100.9 2.3 gather_fusion
  103.2 0.3 broadcast_select_fusion
  103.5 0.0 copy-start.1
  103.5 9.1 %fusion.19 = f32[1,256,4096]{2,1,0:T(8,128)S(1)} fusion(bf16[9,512,4096]{2,1,0:T(8,128)(2,1)} %param.11, bf16[9,256,512]{2,1,0:T(8,128)(2,1)S(1)} %broadcast_select_fusion, bf16[4]{0:T(256)(128)(2,1)S(1)} %get-tuple-element.5), kind=kOutput, calls=%fused_computation.20 | convolution fusion | flops 4295491584 | bytes 22020608 | tf_op jit(solution)/shard_map/ktf,kfd->td/dot_general | solution.py:26
  112.6 0.0 copy-done.1
  112.6 11.5 %fusion.16 = f32[256,4096]{1,0:T(8,128)} fusion(bf16[9,256,512]{2,1,0:T(8,128)(2,1)S(1)} %broadcast_select_fusion, bf16[9,512,4096]{2,1,0:T(8,128)(2,1)} %param.11), kind=kOutput, calls=%fused_computation.19 | convolution fusion | flops 5368709120 | bytes 27525120 | tf_op jit(solution)/shard_map/ktf,kfd->td/dot_general | solution.py:32
  124.1 12.5 %fusion.28 = f32[1,256,4096]{2,1,0:T(8,128)S(1)} fusion(f32[256,4096]{1,0:T(8,128)} %fusion.16, bf16[9,512,4096]{2,1,0:T(8,128)(2,1)} %param.11, bf16[9,256,512]{2,1,0:T(8,128)(2,1)} %copy-done.1, bf16[4]{0:T(256)(128)(2,1)S(1)} %broadcast_subtract_fusion), kind=kOutput, calls=%fused_computation.23 | convolution fusion | flops 4296540160 | bytes 26214408 | tf_op jit(solution)/shard_map/ktf,kfd->td/dot_general | solution.py:29
  136.6 4.2 %pad_maximum_fusion = f32[2,256,4096]{2,1,0:T(8,128)} fusion(f32[1,256,4096]{2,1,0:T(8,128)S(1)} %fusion.28, f32[1,256,4096]{2,1,0:T(8,128)S(1)} %fusion.19), kind=kLoop, calls=%fused_computation.11 | loop fusion | flops 2097152 | bytes 16777216 | tf_op jit(solution)/shard_map/stack | solution.py:35
  140.9 0.0 copy-start.3
  140.9 0.0 all-reduce.2.cloned.1.call-update
  140.9 0.0 reduce-scatter.2.cloned.1.call-start
  140.9 0.6 copy-done.3
  141.5 8.9 %all_gather.14 = bf16[2,4096]{1,0:T(2,128)(2,1)S(1)} all-gather(bf16[2,512]{1,0:T(2,128)(2,1)S(1)} %copy-done.3), channel_id=1, replica_groups=mesh['layer'=4,'feat'=8] {'feat'}, dimensions={1}, use_global_device_ids=true | all-gather | bytes 18432 | tf_op jit(solution)/shard_map/all_gather | solution.py:39
  150.4 0.0 all-gather.8.cloned.1.call-done
  150.5 119.9 %all-reduce.2.cloned.1.call-done = f32[2,256,4096]{2,1,0:T(8,128)} async-done(((f32[2,256,4096]{2,1,0:T(8,128)}), f32[2,256,4096]{2,1,0:T(8,128)}) %all-reduce.2.cloned.1.call-update) | async-done | bytes 8388624 | tf_op jit(solution)/shard_map/psum | solution.py:36
  270.4 6.1 %subtract_convert_fusion = bf16[2,256,4096]{2,1,0:T(8,128)(2,1)S(1)} fusion(bf16[2,256,4096]{2,1,0:T(8,128)(2,1)} %all-gather.8.cloned.1.call-done, f32[2,256,4096]{2,1,0:T(8,128)} %all-reduce.2.cloned.1.call-done, f32[2,4096]{1,0:T(2,128)S(1)} %convert_element_type.29), kind=kLoop, calls=%fused_computation.17 | loop fusion | flops 8388608 | bytes 16809984 | tf_op jit(solution)/shard_map/convert_element_type | solution.py:43
  276.4 0.0 copy-start
  276.5 2.4 slice_bitcast_fusion
  278.9 0.8 copy-done
  279.7 9.9 %fusion = f32[256,5,512]{2,0,1:T(8,128)S(1)} fusion(bf16[9,512,4096]{2,1,0:T(8,128)(2,1)} %param.11, bf16[2,256,4096]{2,1,0:T(8,128)(2,1)S(1)} %subtract_convert_fusion), kind=kOutput, calls=%fused_computation.1 | convolution fusion | flops 5368709120 | bytes 25690112 | tf_op jit(solution)/shard_map/td,kfd->ktf/dot_general | solution.py:50
  289.6 10.3 %fusion.4 = f32[4,256,512]{2,1,0:T(8,128)} fusion(bf16[9,512,4096]{2,1,0:T(8,128)(2,1)} %param.11, pred[4]{0:T(512)(128)(4,1)S(1)} %get-tuple-element.4, bf16[256,4096]{1,0:T(8,128)(2,1)} %get-tuple-element.3, bf16[256,4096]{1,0:T(8,128)(2,1)} %get-tuple-element.2), kind=kOutput, calls=%fused_computation.5 | convolution fusion | flops 4299161600 | bytes 23068676 | tf_op jit(solution)/shard_map/ktd,kfd->ktf/dot_general | solution.py:47
  299.9 2.9 copy.11
  302.9 1.6 copy.16
  304.5 4.2 %fusion.10 = bf16[8,256,512]{2,0,1:T(8,128)(2,1)S(1)} fusion(f32[5,256,512]{2,0,1:T(8,128)S(1)} %bitcast.31, f32[4,256,512]{2,0,1:T(4,128)S(1)} %copy.11, s32[9]{0:T(128)S(1)} %add_select_fusion), kind=kOutput, calls=%fused_computation.12 | convolution fusion | flops 114425928 | bytes 6815780 | tf_op jit(solution)/shard_map/ks,ktf->stf/dot_general | solution.py:57
  308.7 0.0 copy-start.2
  308.7 2.1 copy.15
  310.8 0.0 reduce-scatter.2.cloned.1.call-update
  310.8 1.9 constant_dynamic-slice_fusion
  312.7 40.2 %reduce-scatter.2.cloned.1.call-done = bf16[2,256,512]{2,1,0:T(8,128)(2,1)} async-done(((bf16[8,256,512]{2,1,0:T(8,128)(2,1)}), bf16[2,256,512]{2,1,0:T(8,128)(2,1)}) %reduce-scatter.2.cloned.1.call-update) | async-done | bytes 524304 | tf_op jit(solution)/shard_map/reduce_scatter | solution.py:58
  352.9 0.0 copy-done.2
  352.9 2.2 convert_multiply_fusion
  (7 shorter events, 0.1 us)
Async XLA Ops:
  7.2 41.3 %all-gather.4.cloned.1.call-start = ((), (), s32[]{:S(2)}) async-start(), calls=%async_computation.1 | async-start | bytes 4718592 | tf_op jit(solution)/shard_map/all_gather | solution.py:14
  7.9 93.0 %all-gather.6.cloned.1.call-start = ((), (), s32[]{:S(2)}) async-start(), calls=%async_computation.2 | async-start | bytes 2621440 | tf_op jit(solution)/shard_map/all_gather | solution.py:19
  56.4 94.0 %all-gather.8.cloned.1.call-start = ((), (), s32[]{:S(2)}) async-start(), calls=%async_computation.4 | async-start | bytes 4718592 | tf_op jit(solution)/shard_map/all_gather | solution.py:38
  57.2 213.2 %all-reduce.2.cloned.1.call-start = ((), (), s32[]{:S(2)}) async-start(), calls=%async_computation.3 | async-start | bytes 16777216 | tf_op jit(solution)/shard_map/psum | solution.py:36
  103.5 9.1 %copy-start.1 = (bf16[9,256,512]{2,1,0:T(8,128)(2,1)}, bf16[9,256,512]{2,1,0:T(8,128)(2,1)S(1)}, u32[]{:S(2)}) copy-start(bf16[9,256,512]{2,1,0:T(8,128)(2,1)S(1)} %broadcast_select_fusion) | copy-start | bytes 7077892
  140.9 0.7 copy-start.3
  140.9 212.0 %reduce-scatter.2.cloned.1.call-start = ((), (), s32[]{:S(2)}) async-start(), calls=%async_computation.5 | async-start | bytes 2621440 | tf_op jit(solution)/shard_map/reduce_scatter | solution.py:58
  276.4 3.3 copy-start
  308.7 44.2 %copy-start.2 = (s32[2,256,512]{2,1,0:T(8,128)S(1)}, s32[2,256,512]{2,1,0:T(8,128)}, u32[]{:S(2)}) copy-start(s32[2,256,512]{2,1,0:T(8,128)} %param.10) | copy-start | bytes 3145732
Sparse Core Ops, SparseCore 0:
  9.9 38.5 all-gather.3
  56.6 44.3 all-gather.5
  102.8 37.7 all-gather.7
  143.9 126.4 all-reduce.1
  310.9 41.9 reduce-scatter.1
where the time goes:
time: 366 us; the launch traced here: 362 us
  waiting for transfers between devices  246 us (67%)
  matrix products  65.4 us (18%)
  local copies, waits for them, and re-layouts  14.6 us (4%)
  between operations  13.9 us (4%)
  other arithmetic  12.8 us (3%)
  blocking collectives  8.87 us (2%)
    psum x1, waiting for transfers between devices, on_device(): recon = lax.psum(partial_value, 'feat')  120 us
    all_gather x1, waiting for transfers between devices, on_device(): every = lax.all_gather(acts, 'layer', axis=0, tiled=True)  43.6 us
    all_gather x1, waiting for transfers between devices, on_device(): lax.all_gather(resid, 'feat', axis=2, tiled=True)  40.5 us
    reduce_scatter x1, waiting for transfers between devices, on_device(): lax.psum_scatter(grad_terms.astype(jnp.bfloat16), 'layer', scatter_dimens...  40.2 us
    dot_general x1, matrix products, on_device(): jnp.einsum('ktf,kfd->td', lead_acts * (1 - lead_mask), dec[:half], prefer...  12.5 us
    dot_general x1, matrix products, on_device(): jnp.einsum('ktf,kfd->td', chosen[half:], dec[half:], preferred_element_ty...  11.5 us
    dot_general x1, matrix products, on_device(): jnp.einsum('ktd,kfd->ktf', lead_error, dec[:half], preferred_element_type...  10.3 us
    dot_general x1, matrix products, on_device(): jnp.einsum('td,kfd->ktf', wide_error[1], dec[half:], preferred_element_ty...  9.9 us
  transfers between devices with their start and end apart: 5, of which 4 were waited for; matrix products, arithmetic and copies ran while one was open for 12% of the time, Pallas kernels for 0%

commit v1 on v0

--- a/solution.py
+++ b/solution.py
@@ -1,12 +1,18 @@
 import jax
 import jax.numpy as jnp
 from jax import lax
+from jax.experimental import pallas as pl
+from jax.experimental.pallas import tpu as pltpu
 from jax.sharding import PartitionSpec as P
 
 LAYERS = 8
-
-
-def on_device(resid, enc, enc_bias, fire, dec, dec_bias, target):
+CHUNKS = 1
+VMEM = pl.BlockSpec(memory_space=pltpu.VMEM)
+SMEM = pl.BlockSpec(memory_space=pltpu.SMEM)
+LIMIT = 48 * 2**20
+
+
+def plain(resid, enc, enc_bias, fire, dec, dec_bias, target):
     group = lax.axis_index("layer")
     half = LAYERS // 2
     pre = jnp.einsum(
@@ -62,6 +68,217 @@
     return (error, act_grad)
 
 
+def pre_kernel(order, *refs):
+    *blocks, enc, bias, fire, out, acc = refs
+    width = blocks[0].shape[2]
+    layer = pl.program_id(0)
+    for i, block in enumerate(blocks):
+        rows = pl.ds(pl.multiple_of(order[i] * width, width), width)
+        term = jnp.dot(block[layer], enc[0, rows, :], preferred_element_type=jnp.float32)
+        if i == 0:
+            acc[...] = term
+        else:
+            acc[...] += term
+    out[0] = (fire[0].astype(jnp.float32) * (acc[...] + bias[0])).astype(jnp.bfloat16)
+
+
+def encode(order, blocks, enc, bias, fire, chunk):
+    layers, tokens, _ = blocks[0].shape
+    _, depth, feats = enc.shape
+    part = feats // 2
+    return pl.pallas_call(
+        pre_kernel,
+        grid=(layers, feats // part),
+        in_specs=[SMEM]
+        + [VMEM] * len(blocks)
+        + [
+            pl.BlockSpec((1, depth, part), lambda l, h: (l, 0, h)),
+            pl.BlockSpec((1, 1, part), lambda l, h: (l, 0, h)),
+            pl.BlockSpec((1, tokens, part), lambda l, h: (l, chunk, h)),
+        ],
+        out_specs=pl.BlockSpec((1, tokens, part), lambda l, h: (l, 0, h)),
+        out_shape=jax.ShapeDtypeStruct((layers, tokens, feats), jnp.bfloat16),
+        scratch_shapes=[pltpu.VMEM((tokens, part), jnp.float32)],
+        compiler_params=pltpu.CompilerParams(vmem_limit_bytes=LIMIT),
+        cost_estimate=pl.CostEstimate(
+            flops=2 * layers * tokens * depth * feats, bytes_accessed=2 * enc.size, transcendentals=0
+        ),
+        name="encode",
+    )(order, *blocks, enc, bias, fire)
+
+
+def rec_kernel(cols, rows, edge, *refs):
+    *sources, dec, keep, send, held, acc = refs
+    k = pl.program_id(0)
+    width = keep.shape[3]
+    layers = keep.shape[1]
+    quarter = dec.shape[2] // 4
+
+    @pl.when(k == 0)
+    def _():
+        for i, source in enumerate(sources):
+            held[layers * i : layers * (i + 1)] = source[...]
+        acc[...] = jnp.zeros_like(acc)
+
+    slot = (k >= edge[0]).astype(jnp.int32)
+    acts = held[rows[k]]
+    for j in range(4):
+        part = slice(j * quarter, (j + 1) * quarter)
+        acc[slot, :, part] += jnp.dot(acts, dec[0, :, part], preferred_element_type=jnp.float32)
+
+    @pl.when(k == pl.num_programs(0) - 1)
+    def _():
+        for i in range(8):
+            place = pl.ds(pl.multiple_of(cols[i] * width, width), width)
+            for s in range(layers):
+                value = acc[s, :, place].astype(jnp.bfloat16)
+                if i < 4:
+                    keep[i, s] = value
+                else:
+                    send[i - 4, s] = value
+
+
+def reconstruct(cols, rows, edge, sources, dec):
+    layers, tokens, feats = sources[0].shape
+    pairs, _, depth = dec.shape
+    out = jax.ShapeDtypeStruct((4, layers, tokens, depth // 8), jnp.bfloat16)
+    return pl.pallas_call(
+        rec_kernel,
+        grid=(pairs,),
+        in_specs=[SMEM] * 3
+        + [VMEM] * len(sources)
+        + [pl.BlockSpec((1, feats, depth), lambda k: (k, 0, 0))],
+        out_specs=[VMEM, VMEM],
+        out_shape=[out, out],
+        scratch_shapes=[
+            pltpu.VMEM((layers * len(sources), tokens, feats), jnp.bfloat16),
+            pltpu.VMEM((layers, tokens, depth), jnp.float32),
+        ],
+        compiler_params=pltpu.CompilerParams(vmem_limit_bytes=LIMIT),
+        cost_estimate=pl.CostEstimate(
+            flops=2 * tokens * dec.size, bytes_accessed=2 * dec.size, transcendentals=0
+        ),
+        name="reconstruct",
+    )(cols, rows, edge, *sources, dec)
+
+
+def grad_kernel(cols, rows, edge, *refs):
+    blocks, dec, outs, error, total = refs[:8], refs[8], refs[9:-2], refs[-2], refs[-1]
+    k = pl.program_id(0)
+    width = blocks[0].shape[2]
+    layers = blocks[0].shape[0]
+
+    @pl.when(k == 0)
+    def _():
+        for i, block in enumerate(blocks):
+            place = pl.ds(pl.multiple_of(cols[i] * width, width), width)
+            error[:, :, place] = block[...]
+        total[...] = jnp.zeros_like(total)
+
+    slot = (k >= edge[0]).astype(jnp.int32)
+    total[rows[k]] += lax.dot_general(
+        error[slot], dec[0], (((1,), (1,)), ((), ())), preferred_element_type=jnp.float32
+    )
+
+    @pl.when(k == pl.num_programs(0) - 1)
+    def _():
+        for i, out in enumerate(outs):
+            out[...] = total[layers * i : layers * (i + 1)].astype(out.dtype)
+
+
+def gradients(cols, rows, edge, blocks, dec):
+    layers, tokens, _ = blocks[0].shape
+    pairs, feats, depth = dec.shape
+    return pl.pallas_call(
+        grad_kernel,
+        grid=(pairs,),
+        in_specs=[SMEM] * 3
+        + [VMEM] * len(blocks)
+        + [pl.BlockSpec((1, feats, depth), lambda k: (k, 0, 0))],
+        out_specs=[VMEM] * 7,
+        out_shape=[
+            jax.ShapeDtypeStruct((layers, tokens, feats), jnp.bfloat16 if i else jnp.float32)
+            for i in range(7)
+        ],
+        scratch_shapes=[
+            pltpu.VMEM((layers, tokens, depth), jnp.bfloat16),
+            pltpu.VMEM((layers * 7, tokens, feats), jnp.float32),
+        ],
+        compiler_params=pltpu.CompilerParams(vmem_limit_bytes=LIMIT),
+        cost_estimate=pl.CostEstimate(
+            flops=2 * tokens * dec.size, bytes_accessed=2 * dec.size, transcendentals=0
+        ),
+        name="gradients",
+    )(cols, rows, edge, *blocks, dec)
+
+
+FLIP = [(i, i ^ 1) for i in range(8)]
+FIRST = [(i, i ^ (4 if i & 1 else 2)) for i in range(8)]
+SECOND = [(i, i ^ (2 if i & 1 else 4)) for i in range(8)]
+UP = [(i, i + 1) for i in range(3)]
+DOWN = [(i + 1, i) for i in range(3)]
+
+
+def gather(own):
+    first = lax.ppermute(own, "feat", FIRST)
+    second = lax.ppermute(own, "feat", SECOND)
+    both = lax.ppermute(first, "feat", SECOND)
+    mine = [own, first, second, both]
+    return mine + [lax.ppermute(b, "feat", FLIP) for b in mine]
+
+
+def on_device(resid, enc, enc_bias, fire, dec, dec_bias, target):
+    group = lax.axis_index("layer")
+    me = lax.axis_index("feat")
+    core = me & 1
+    one, two = 2 + 2 * core, 4 - 2 * core
+    gathered = jnp.stack([0 * core, one, two, 0 * core + 6, 0 * core + 1, two ^ 1, one ^ 1, 0 * core + 7])
+    columns = (me ^ gathered).astype(jnp.int32)
+    scattered = columns
+    k = jnp.arange(LAYERS + 1, dtype=jnp.int32)
+    source = jnp.where(k <= group, k, k - group - 1)
+    away = source // 2 - group
+    place = jnp.where(away >= 0, away, 3 - away)
+    rows = (2 * place + source % 2).astype(jnp.int32)
+    edge = (group + 1).astype(jnp.int32)[None]
+    bias3 = enc_bias[:, None, :]
+    tokens = resid.shape[1] // CHUNKS
+    errors, grads = [], []
+    for c in range(CHUNKS):
+        span = slice(c * tokens, (c + 1) * tokens)
+        blocks = gather(resid[:, span])
+        acts = encode(columns, blocks, enc, bias3, fire, c)
+        above1 = lax.ppermute(acts, "layer", DOWN)
+        below1 = lax.ppermute(acts, "layer", UP)
+        above2 = lax.ppermute(above1, "layer", [(1, 0), (2, 1)])
+        below2 = lax.ppermute(below1, "layer", [(1, 2), (2, 3)])
+        above3 = lax.ppermute(acts, "layer", [(3, 0)])
+        below3 = lax.ppermute(acts, "layer", [(0, 3)])
+        keep, send = reconstruct(
+            scattered, rows, edge, [acts, above1, above2, above3, below1, below2, below3], dec
+        )
+        other = lax.ppermute(send, "feat", FLIP)
+        f32 = jnp.float32
+        pair = keep.astype(f32) + other.astype(f32)
+        far = lax.ppermute(pair[2:].astype(jnp.bfloat16), "feat", SECOND).astype(f32)
+        near = lax.ppermute((pair[1] + far[1]).astype(jnp.bfloat16), "feat", FIRST).astype(f32)
+        recon = pair[0] + far[0] + near
+        error = (
+            recon + dec_bias.astype(f32)[:, None, :] - target[:, span].astype(f32)
+        ).astype(jnp.bfloat16)
+        errors.append(error)
+        own, up1, up2, up3, down1, down2, down3 = gradients(columns, rows, edge, gather(error), dec)
+        up3 = lax.ppermute(up3, "layer", [(0, 3)])
+        down3 = lax.ppermute(down3, "layer", [(3, 0)])
+        up2 = lax.ppermute(up2, "layer", [(0, 1), (1, 2)]).astype(f32)
+        down2 = lax.ppermute(down2, "layer", [(3, 2), (2, 1)]).astype(f32)
+        up1 = lax.ppermute((up1.astype(f32) + up2).astype(jnp.bfloat16), "layer", UP)
+        down1 = lax.ppermute((down1.astype(f32) + down2).astype(jnp.bfloat16), "layer", DOWN)
+        total = own + up1.astype(f32) + down1.astype(f32) + up3.astype(f32) + down3.astype(f32)
+        grads.append(fire[:, span].astype(f32) * total)
+    return jnp.concatenate(errors, axis=1), jnp.concatenate(grads, axis=1)
+
+
 def solution(mesh):
     placed = (
         P("layer", None, "feat"),
@@ -72,8 +289,9 @@
         P("layer", "feat"),
         P("layer", None, "feat"),
     )
+    blocks = mesh.shape["feat"] == 8 and mesh.shape["layer"] == 4
     return jax.shard_map(
-        on_device,
+        on_device if blocks else plain,
         mesh=mesh,
         in_specs=placed,
         out_specs=(P("layer", None, "feat"), P("layer", None, "feat")),

time: 366 us -> 224 us (0.61)
  waiting for transfers between devices: 246 us -> 124 us
  matrix products: 65.4 us -> 0 us
  Pallas kernels: 0 us -> 46.2 us
  starting transfers between devices: 0.2 us -> 40 us
  between operations: 13.9 us -> 0.93 us
  blocking collectives: 8.87 us -> 0 us
  local copies, waits for them, and re-layouts: 14.6 us -> 5.82 us
  other arithmetic: 12.8 us -> 4.49 us
    ppermute x0 -> x29, waiting for transfers between devices: none -> 124 us  [the longest x2 25.1 us: gather(): first = lax.ppermute(own, 'feat', FIRST)]
    psum x1 -> x0, waiting for transfers between devices: 120 us -> none  [on_device(): recon = lax.psum(partial_value, 'feat')]
    all_gather x3 -> x0, waiting for transfers between devices: 84.2 us -> none  [the longest x1 43.6 us: on_device(): every = lax.all_gather(acts, 'layer', axis=0, tiled=True)]
    dot_general x7 -> x0, matrix products: 65.4 us -> none  [the longest x1 12.5 us: on_device(): jnp.einsum('ktf,kfd->td', lead_acts * (1 - lead_mask), dec[:half], prefer...]
    pallas_call x0 -> x3, Pallas kernels: none -> 46.2 us  [the longest x1 20.3 us: gradients(): pl.pallas_call(grad_kernel, grid=(pairs,), in_specs=[SMEM] * 3 + [VMEM] *...]
    reduce_scatter x1 -> x0, waiting for transfers between devices: 40.2 us -> none  [on_device(): lax.psum_scatter(grad_terms.astype(jnp.bfloat16), 'layer', scatter_dimens...]
    ppermute x0 -> x29, starting transfers between devices: none -> 40 us  [the longest x1 13.9 us: on_device(): below2 = lax.ppermute(below1, 'layer', [(1, 2), (2, 3)])]
    all_gather x1 -> x0, blocking collectives: 8.87 us -> none  [on_device(): lax.all_gather(dec_bias, 'feat', axis=1, tiled=True)]
  transfers between devices with their start and end apart: 5 -> 29, of which waited for: 4 -> 16; matrix products, arithmetic and copies ran while one was open for 12% -> 0% of each run, Pallas kernels for 0% -> 0%
where the time goes in v1:
time: 224 us; the launch traced here: 222 us
  waiting for transfers between devices  124 us (55%)
  Pallas kernels  46.2 us (21%)
  starting transfers between devices  40 us (18%)
  local copies, waits for them, and re-layouts  5.82 us (3%)
  other arithmetic  4.49 us (2%)
    ppermute x2, waiting for transfers between devices, gather(): first = lax.ppermute(own, 'feat', FIRST)  25.1 us
    pallas_call x1, Pallas kernels, gradients(): pl.pallas_call(grad_kernel, grid=(pairs,), in_specs=[SMEM] * 3 + [VMEM] *...  20.3 us
    pallas_call x1, Pallas kernels, reconstruct(): pl.pallas_call(rec_kernel, grid=(pairs,), in_specs=[SMEM] * 3 + [VMEM] *...  20.3 us
    ppermute x2, waiting for transfers between devices, gather(): both = lax.ppermute(first, 'feat', SECOND)  14.7 us
    ppermute x1, waiting for transfers between devices, on_device(): lax.ppermute(pair[2:].astype(jnp.bfloat16), 'feat', SECOND).astype(f32)  14.1 us
    ppermute x1, starting transfers between devices, on_device(): below2 = lax.ppermute(below1, 'layer', [(1, 2), (2, 3)])  13.9 us
    ppermute x1, waiting for transfers between devices, on_device(): up2 = lax.ppermute(up2, 'layer', [(0, 1), (1, 2)]).astype(f32)  12 us
    ppermute x1, waiting for transfers between devices, on_device(): down2 = lax.ppermute(down2, 'layer', [(3, 2), (2, 1)]).astype(f32)  10.3 us
  transfers between devices with their start and end apart: 29, of which 16 were waited for; matrix products, arithmetic and copies ran while one was open for 0% of the time, Pallas kernels for 0%

profile of v1, /device:TPU:10, one launch (start us, length us, event | category | flops | bytes accessed | tf_op | source)
XLA Modules:
  0.0 221.6 jit_solution(11412226949010780780)
XLA Ops:
  0.6 0.6 collective-permute-start
  1.2 1.5 collective-permute-start.1
  2.7 12.8 %collective-permute-done.refs_1_ = bf16[2,256,512]{2,1,0:T(8,128)(2,1)S(1)} collective-permute-done((bf16[2,256,512]{2,1,0:T(8,128)(2,1)}, bf16[2,256,512]{2,1,0:T(8,128)(2,1)S(1)}, u32[]{:S(2)}, u32[]{:S(2)}) %collective-permute-start) | collective-permute-done | bytes 524320 | tf_op jit(solution)/shard_map/ppermute | solution.py:223
  15.6 0.7 collective-permute-start.2
  16.3 0.5 collective-permute-start.4
  16.8 7.9 %collective-permute-done.2.refs_3_ = bf16[2,256,512]{2,1,0:T(8,128)(2,1)S(1)} collective-permute-done((bf16[2,256,512]{2,1,0:T(8,128)(2,1)S(1)}, bf16[2,256,512]{2,1,0:T(8,128)(2,1)S(1)}, u32[]{:S(2)}, u32[]{:S(2)}) %collective-permute-start.2) | collective-permute-done | bytes 524320 | tf_op jit(solution)/shard_map/ppermute | solution.py:225
  24.8 0.7 broadcast_in_dim.8.refs_9_
  25.6 0.8 copy-done.4
  26.8 1.2 copy-done
  28.0 1.0 copy-done.3
  29.1 1.0 copy-done.5
  30.1 5.7 %encode.1.refs_0_ = bf16[2,256,512]{2,1,0:T(8,128)(2,1)S(1)} custom-call(s32[8]{0:T(128)S(1)} %broadcast_xor_fusion.order.cols, bf16[2,256,512]{2,1,0:T(8,128)(2,1)S(1)} %copy-done.3, bf16[2,256,512]{2,1,0:T(8,128)(2,1)S(1)} %collective-permute-done.refs_1_, bf16[2,256,512]{2,1,0:T(8,128)(2,1)S(1)} %collective-permute-done.1.refs_2_, ...), custom_call_target="tpu_custom_call" | custom-call | flops 2147483648 | bytes 8388608 | tf_op jit(solution)/shard_map/encode/pallas_call | solution.py:89
  35.8 3.5 %collective-permute-start.10 = (bf16[2,256,512]{2,1,0:T(8,128)(2,1)S(1)}, bf16[2,256,512]{2,1,0:T(8,128)(2,1)S(1)}, u32[]{:S(2)}, u32[]{:S(2)}) collective-permute-start(bf16[2,256,512]{2,1,0:T(8,128)(2,1)S(1)} %encode.1.refs_0_), channel_id=1, source_target_pairs={{0,8},{8,16},{16,24},{1,9},{9,17},{17,25},{2,10},{10,18},{18,26},{... | collective-permute-start | bytes 1572872 | tf_op jit(solution)/shard_map/ppermute | solution.py:252
  39.3 2.4 %collective-permute-start.7 = (bf16[2,256,512]{2,1,0:T(8,128)(2,1)S(1)}, bf16[2,256,512]{2,1,0:T(8,128)(2,1)S(1)}, u32[]{:S(2)}, u32[]{:S(2)}) collective-permute-start(bf16[2,256,512]{2,1,0:T(8,128)(2,1)S(1)} %encode.1.refs_0_), channel_id=1, source_target_pairs={{8,0},{16,8},{24,16},{9,1},{17,9},{25,17},{10,2},{18,10},{26,18},{... | collective-permute-start | bytes 1572872 | tf_op jit(solution)/shard_map/ppermute | solution.py:251
  41.7 0.7 collective-permute-start.12
  42.4 0.7 collective-permute-start.9
  43.1 9.4 %collective-permute-done.10.refs_4_ = bf16[2,256,512]{2,1,0:T(8,128)(2,1)S(1)} collective-permute-done((bf16[2,256,512]{2,1,0:T(8,128)(2,1)S(1)}, bf16[2,256,512]{2,1,0:T(8,128)(2,1)S(1)}, u32[]{:S(2)}, u32[]{:S(2)}) %collective-permute-start.10) | collective-permute-done | bytes 524320 | tf_op jit(solution)/shard_map/ppermute | solution.py:252
  52.5 13.9 %collective-permute-start.11 = (bf16[2,256,512]{2,1,0:T(8,128)(2,1)S(1)}, bf16[2,256,512]{2,1,0:T(8,128)(2,1)S(1)}, u32[]{:S(2)}, u32[]{:S(2)}) collective-permute-start(bf16[2,256,512]{2,1,0:T(8,128)(2,1)S(1)} %collective-permute-done.10.refs_4_), channel_id=1, source_target_pairs={{8,16},{16,24},{9,17},{17,25},{10,18},{18,26},{11,19},{19,27},{12,... | collective-permute-start | bytes 1572872 | tf_op jit(solution)/shard_map/ppermute | solution.py:254
  66.4 1.9 collective-permute-start.8
  68.4 4.8 %collective-permute-done.11.refs_5_ = bf16[2,256,512]{2,1,0:T(8,128)(2,1)S(1)} collective-permute-done((bf16[2,256,512]{2,1,0:T(8,128)(2,1)S(1)}, bf16[2,256,512]{2,1,0:T(8,128)(2,1)S(1)}, u32[]{:S(2)}, u32[]{:S(2)}) %collective-permute-start.11) | collective-permute-done | bytes 524320 | tf_op jit(solution)/shard_map/ppermute | solution.py:254
  73.2 5.2 %collective-permute-done.8.refs_2_ = bf16[2,256,512]{2,1,0:T(8,128)(2,1)} collective-permute-done((bf16[2,256,512]{2,1,0:T(8,128)(2,1)S(1)}, bf16[2,256,512]{2,1,0:T(8,128)(2,1)}, u32[]{:S(2)}, u32[]{:S(2)}) %collective-permute-start.8) | collective-permute-done | bytes 524320 | tf_op jit(solution)/shard_map/ppermute | solution.py:253
  78.5 20.3 %reconstruct.1 = (bf16[4,2,256,512]{3,2,1,0:T(8,128)(2,1)S(1)}, bf16[4,2,256,512]{3,2,1,0:T(8,128)(2,1)}) custom-call(s32[8]{0:T(128)S(1)} %broadcast_xor_fusion.order.cols, s32[9]{0:T(128)S(1)} %fusion.7.rows, s32[1]{0:T(128)} %bitcast.4.edge, bf16[2,256,512]{2,1,0:T(8,128)(2,1)S(1)} %encode.1.refs_0_, ...), custom_call_target="tpu_custom_call" | custom-call | flops 9663676416 | bytes 37748736 | tf_op jit(solution)/shard_map/reconstruct/pallas_call | solution.py:145
  98.7 4.4 %collective-permute-done.13 = bf16[4,2,256,512]{3,2,1,0:T(8,128)(2,1)S(1)} collective-permute-done((bf16[4,2,256,512]{3,2,1,0:T(8,128)(2,1)}, bf16[4,2,256,512]{3,2,1,0:T(8,128)(2,1)S(1)}, u32[]{:S(2)}, u32[]{:S(2)}) %collective-permute-start.13) | collective-permute-done | bytes 2097184 | tf_op jit(solution)/shard_map/ppermute | solution.py:260
  103.1 0.6 convert_add_fusion
  103.9 0.8 collective-permute-start.14
  104.7 14.1 %collective-permute-done.14 = bf16[2,2,256,512]{3,2,1,0:T(8,128)(2,1)S(1)} collective-permute-done((bf16[2,2,256,512]{3,2,1,0:T(8,128)(2,1)S(1)}, bf16[2,2,256,512]{3,2,1,0:T(8,128)(2,1)S(1)}, u32[]{:S(2)}, u32[]{:S(2)}) %collective-permute-start.14) | collective-permute-done | bytes 1048608 | tf_op jit(solution)/shard_map/ppermute | solution.py:263
  119.3 0.6 collective-permute-start.15
  119.9 8.6 %collective-permute-done.15 = bf16[2,256,512]{2,1,0:T(8,128)(2,1)S(1)} collective-permute-done((bf16[2,256,512]{2,1,0:T(8,128)(2,1)S(1)}, bf16[2,256,512]{2,1,0:T(8,128)(2,1)S(1)}, u32[]{:S(2)}, u32[]{:S(2)}) %collective-permute-start.15) | collective-permute-done | bytes 524320 | tf_op jit(solution)/shard_map/ppermute | solution.py:264
  128.9 0.6 collective-permute-start.16
  129.5 0.7 collective-permute-start.17
  130.3 12.2 %collective-permute-done.16.refs_1_ = bf16[2,256,512]{2,1,0:T(8,128)(2,1)S(1)} collective-permute-done((bf16[2,256,512]{2,1,0:T(8,128)(2,1)S(1)}, bf16[2,256,512]{2,1,0:T(8,128)(2,1)S(1)}, u32[]{:S(2)}, u32[]{:S(2)}) %collective-permute-start.16) | collective-permute-done | bytes 524320 | tf_op jit(solution)/shard_map/ppermute | solution.py:223
  142.5 1.9 collective-permute-start.18
  144.4 0.5 collective-permute-start.20
  144.9 6.8 %collective-permute-done.18.refs_3_ = bf16[2,256,512]{2,1,0:T(8,128)(2,1)S(1)} collective-permute-done((bf16[2,256,512]{2,1,0:T(8,128)(2,1)S(1)}, bf16[2,256,512]{2,1,0:T(8,128)(2,1)S(1)}, u32[]{:S(2)}, u32[]{:S(2)}) %collective-permute-start.18) | collective-permute-done | bytes 524320 | tf_op jit(solution)/shard_map/ppermute | solution.py:225
  151.7 1.9 collective-permute-done.22.refs_7_
  153.6 0.8 copy-done.8
  154.4 20.3 %gradients.1 = (f32[2,256,512]{2,1,0:T(8,128)}, bf16[2,256,512]{2,1,0:T(8,128)(2,1)S(1)}, bf16[2,256,512]{2,1,0:T(8,128)(2,1)S(1)}, bf16[2,256,512]{2,1,0:T(8,12...) custom-call(s32[8]{0:T(128)S(1)} %broadcast_xor_fusion.order.cols, ...), custom_call_target="tpu_custom_call" | custom-call | flops 9663676416 | bytes 37748736 | tf_op jit(solution)/shard_map/gradients/pallas_call | solution.py:192
  174.7 1.9 collective-permute-start.23
  176.6 1.3 collective-permute-start.25
  177.9 0.7 collective-permute-start.27
  178.6 0.7 collective-permute-start.28
  179.3 12.0 %collective-permute-done.23 = bf16[2,256,512]{2,1,0:T(8,128)(2,1)S(1)} collective-permute-done((bf16[2,256,512]{2,1,0:T(8,128)(2,1)S(1)}, bf16[2,256,512]{2,1,0:T(8,128)(2,1)S(1)}, u32[]{:S(2)}, u32[]{:S(2)}) %collective-permute-start.23) | collective-permute-done | bytes 524320 | tf_op jit(solution)/shard_map/ppermute | solution.py:273
  191.5 1.9 collective-permute-start.24
  193.4 10.3 %collective-permute-done.25 = bf16[2,256,512]{2,1,0:T(8,128)(2,1)S(1)} collective-permute-done((bf16[2,256,512]{2,1,0:T(8,128)(2,1)S(1)}, bf16[2,256,512]{2,1,0:T(8,128)(2,1)S(1)}, u32[]{:S(2)}, u32[]{:S(2)}) %collective-permute-start.25) | collective-permute-done | bytes 524320 | tf_op jit(solution)/shard_map/ppermute | solution.py:274
  203.8 1.9 collective-permute-start.26
  205.8 7.3 %collective-permute-done.24 = bf16[2,256,512]{2,1,0:T(8,128)(2,1)S(1)} collective-permute-done((bf16[2,256,512]{2,1,0:T(8,128)(2,1)S(1)}, bf16[2,256,512]{2,1,0:T(8,128)(2,1)S(1)}, u32[]{:S(2)}, u32[]{:S(2)}) %collective-permute-start.24) | collective-permute-done | bytes 524320 | tf_op jit(solution)/shard_map/ppermute | solution.py:275
  213.0 5.8 %collective-permute-done.26 = bf16[2,256,512]{2,1,0:T(8,128)(2,1)S(1)} collective-permute-done((bf16[2,256,512]{2,1,0:T(8,128)(2,1)S(1)}, bf16[2,256,512]{2,1,0:T(8,128)(2,1)S(1)}, u32[]{:S(2)}, u32[]{:S(2)}) %collective-permute-start.26) | collective-permute-done | bytes 524320 | tf_op jit(solution)/shard_map/ppermute | solution.py:276
  218.9 2.7 %add_multiply_fusion = f32[2,256,512]{2,1,0:T(8,128)} fusion(bf16[2,256,512]{2,1,0:T(8,128)(2,1)S(1)} %collective-permute-done.28, bf16[2,256,512]{2,1,0:T(8,128)(2,1)S(1)} %collective-permute-done.27, bf16[2,256,512]{2,1,0:T(8,128)(2,1)S(1)} %collective-permute-done.26, f32[2,256,512]{2,1,0:T(8,128)} %get-tuple-element.13, ...), kind=kLoop, calls=%fused_computation.10 | loop fusion | flops 2621440 | bytes 5242880 | tf_op jit(solution)/shard_map/mul | solution.py:278
  (48 shorter events, 1.9 us)
Async XLA Ops:
  0.6 15.0 %collective-permute-start = (bf16[2,256,512]{2,1,0:T(8,128)(2,1)}, bf16[2,256,512]{2,1,0:T(8,128)(2,1)S(1)}, u32[]{:S(2)}, u32[]{:S(2)}) collective-permute-start(bf16[2,256,512]{2,1,0:T(8,128)(2,1)} %refs_0_.1), channel_id=1, source_target_pairs={{0,2},{1,5},{2,0},{3,7},{4,6},{5,1},{6,4},{7,3},{8,10},{9,13},{10,... | collective-permute-start | bytes 1572872 | tf_op jit(solution)/shard_map/ppermute | solution.py:223
  1.2 15.6 %collective-permute-start.1 = (bf16[2,256,512]{2,1,0:T(8,128)(2,1)}, bf16[2,256,512]{2,1,0:T(8,128)(2,1)S(1)}, u32[]{:S(2)}, u32[]{:S(2)}) collective-permute-start(bf16[2,256,512]{2,1,0:T(8,128)(2,1)} %refs_0_.1), channel_id=1, source_target_pairs={{0,4},{1,3},{2,6},{3,1},{4,0},{5,7},{6,2},{7,5},{8,12},{9,11},{10,... | collective-permute-start | bytes 1572872 | tf_op jit(solution)/shard_map/ppermute | solution.py:224
  15.6 9.2 %collective-permute-start.2 = (bf16[2,256,512]{2,1,0:T(8,128)(2,1)S(1)}, bf16[2,256,512]{2,1,0:T(8,128)(2,1)S(1)}, u32[]{:S(2)}, u32[]{:S(2)}) collective-permute-start(bf16[2,256,512]{2,1,0:T(8,128)(2,1)S(1)} %collective-permute-done.refs_1_), channel_id=1, source_target_pairs={{0,4},{1,3},{2,6},{3,1},{4,0},{5,7},{6,2},{7,5},{8,12},{9,11},{10,... | collective-permute-start | bytes 1572872 | tf_op jit(solution)/shard_map/ppermute | solution.py:225
  16.3 9.2 %collective-permute-start.3 = (bf16[2,256,512]{2,1,0:T(8,128)(2,1)}, bf16[2,256,512]{2,1,0:T(8,128)(2,1)S(1)}, u32[]{:S(2)}, u32[]{:S(2)}) collective-permute-start(bf16[2,256,512]{2,1,0:T(8,128)(2,1)} %refs_0_.1), channel_id=1, source_target_pairs={{0,1},{1,0},{2,3},{3,2},{4,5},{5,4},{6,7},{7,6},{8,9},{9,8},{10,11... | collective-permute-start | bytes 1572872 | tf_op jit(solution)/shard_map/ppermute | solution.py:227
  16.3 9.2 %collective-permute-start.4 = (bf16[2,256,512]{2,1,0:T(8,128)(2,1)S(1)}, bf16[2,256,512]{2,1,0:T(8,128)(2,1)S(1)}, u32[]{:S(2)}, u32[]{:S(2)}) collective-permute-start(bf16[2,256,512]{2,1,0:T(8,128)(2,1)S(1)} %collective-permute-done.refs_1_), channel_id=1, source_target_pairs={{0,1},{1,0},{2,3},{3,2},{4,5},{5,4},{6,7},{7,6},{8,9},{9,8},{10,11... | collective-permute-start | bytes 1572872 | tf_op jit(solution)/shard_map/ppermute | solution.py:227
  16.8 8.7 %collective-permute-start.5 = (bf16[2,256,512]{2,1,0:T(8,128)(2,1)S(1)}, bf16[2,256,512]{2,1,0:T(8,128)(2,1)S(1)}, u32[]{:S(2)}, u32[]{:S(2)}) collective-permute-start(bf16[2,256,512]{2,1,0:T(8,128)(2,1)S(1)} %collective-permute-done.1.refs_2_), channel_id=1, source_target_pairs={{0,1},{1,0},{2,3},{3,2},{4,5},{5,4},{6,7},{7,6},{8,9},{9,8},{10,11... | collective-permute-start | bytes 1572872 | tf_op jit(solution)/shard_map/ppermute | solution.py:227
  24.8 2.0 collective-permute-start.6
  25.6 0.8 copy-start.4
  26.8 1.2 copy-start
  28.0 1.0 copy-start.3
  29.1 1.0 copy-start.5
  35.8 16.7 %collective-permute-start.10 = (bf16[2,256,512]{2,1,0:T(8,128)(2,1)S(1)}, bf16[2,256,512]{2,1,0:T(8,128)(2,1)S(1)}, u32[]{:S(2)}, u32[]{:S(2)}) collective-permute-start(bf16[2,256,512]{2,1,0:T(8,128)(2,1)S(1)} %encode.1.refs_0_), channel_id=1, source_target_pairs={{0,8},{8,16},{16,24},{1,9},{9,17},{17,25},{2,10},{10,18},{18,26},{... | collective-permute-start | bytes 1572872 | tf_op jit(solution)/shard_map/ppermute | solution.py:252
  39.3 27.1 %collective-permute-start.7 = (bf16[2,256,512]{2,1,0:T(8,128)(2,1)S(1)}, bf16[2,256,512]{2,1,0:T(8,128)(2,1)S(1)}, u32[]{:S(2)}, u32[]{:S(2)}) collective-permute-start(bf16[2,256,512]{2,1,0:T(8,128)(2,1)S(1)} %encode.1.refs_0_), channel_id=1, source_target_pairs={{8,0},{16,8},{24,16},{9,1},{17,9},{25,17},{10,2},{18,10},{26,18},{... | collective-permute-start | bytes 1572872 | tf_op jit(solution)/shard_map/ppermute | solution.py:251
  41.7 26.7 %collective-permute-start.12 = (bf16[2,256,512]{2,1,0:T(8,128)(2,1)S(1)}, bf16[2,256,512]{2,1,0:T(8,128)(2,1)S(1)}, u32[]{:S(2)}, u32[]{:S(2)}) collective-permute-start(bf16[2,256,512]{2,1,0:T(8,128)(2,1)S(1)} %encode.1.refs_0_), channel_id=1, source_target_pairs={{0,24},{1,25},{2,26},{3,27},{4,28},{5,29},{6,30},{7,31}} | collective-permute-start | bytes 1572872 | tf_op jit(solution)/shard_map/ppermute | solution.py:256
  42.4 26.0 %collective-permute-start.9 = (bf16[2,256,512]{2,1,0:T(8,128)(2,1)S(1)}, bf16[2,256,512]{2,1,0:T(8,128)(2,1)S(1)}, u32[]{:S(2)}, u32[]{:S(2)}) collective-permute-start(bf16[2,256,512]{2,1,0:T(8,128)(2,1)S(1)} %encode.1.refs_0_), channel_id=1, source_target_pairs={{24,0},{25,1},{26,2},{27,3},{28,4},{29,5},{30,6},{31,7}} | collective-permute-start | bytes 1572872 | tf_op jit(solution)/shard_map/ppermute | solution.py:255
  52.5 20.8 %collective-permute-start.11 = (bf16[2,256,512]{2,1,0:T(8,128)(2,1)S(1)}, bf16[2,256,512]{2,1,0:T(8,128)(2,1)S(1)}, u32[]{:S(2)}, u32[]{:S(2)}) collective-permute-start(bf16[2,256,512]{2,1,0:T(8,128)(2,1)S(1)} %collective-permute-done.10.refs_4_), channel_id=1, source_target_pairs={{8,16},{16,24},{9,17},{17,25},{10,18},{18,26},{11,19},{19,27},{12,... | collective-permute-start | bytes 1572872 | tf_op jit(solution)/shard_map/ppermute | solution.py:254
  66.4 12.0 %collective-permute-start.8 = (bf16[2,256,512]{2,1,0:T(8,128)(2,1)S(1)}, bf16[2,256,512]{2,1,0:T(8,128)(2,1)}, u32[]{:S(2)}, u32[]{:S(2)}) collective-permute-start(bf16[2,256,512]{2,1,0:T(8,128)(2,1)S(1)} %collective-permute-done.7.refs_1_), channel_id=1, source_target_pairs={{8,0},{16,8},{9,1},{17,9},{10,2},{18,10},{11,3},{19,11},{12,4},{20... | collective-permute-start | bytes 1572872 | tf_op jit(solution)/shard_map/ppermute | solution.py:253
  98.7 4.4 %collective-permute-start.13 = (bf16[4,2,256,512]{3,2,1,0:T(8,128)(2,1)}, bf16[4,2,256,512]{3,2,1,0:T(8,128)(2,1)S(1)}, u32[]{:S(2)}, u32[]{:S(2)}) collective-permute-start(bf16[4,2,256,512]{3,2,1,0:T(8,128)(2,1)} %get-tuple-element.12), channel_id=1, source_target_pairs={{0,1},{1,0},{2,3},{3,2},{4,5},{5,4},{6,7},{7,6},{8,9},{9,8},{10,11... | collective-permute-start | bytes 6291464 | tf_op jit(solution)/shard_map/ppermute | solution.py:260
  103.7 16.2 %copy-start.10 = (bf16[2,512]{1,0:T(2,128)(2,1)S(1)}, bf16[2,512]{1,0:T(2,128)(2,1)}, u32[]{:S(2)}) copy-start(bf16[2,512]{1,0:T(2,128)(2,1)} %param.12) | copy-start | bytes 6148
  103.7 24.8 %copy-start.9 = (bf16[2,256,512]{2,1,0:T(8,128)(2,1)S(1)}, bf16[2,256,512]{2,1,0:T(8,128)(2,1)}, u32[]{:S(2)}) copy-start(bf16[2,256,512]{2,1,0:T(8,128)(2,1)} %param.13) | copy-start | bytes 1572868
  103.9 14.9 %collective-permute-start.14 = (bf16[2,2,256,512]{3,2,1,0:T(8,128)(2,1)S(1)}, bf16[2,2,256,512]{3,2,1,0:T(8,128)(2,1)S(1)}, u32[]{:S(2)}, u32[]{:S(2)}) collective-permute-start(bf16[2,2,256,512]{3,2,1,0:T(8,128)(2,1)S(1)} %slice.47), channel_id=1, source_target_pairs={{0,4},{1,3},{2,6},{3,1},{4,0},{5,7},{6,2},{7,5},{8,12},{9,11},{10,... | collective-permute-start | bytes 3145736 | tf_op jit(solution)/shard_map/ppermute | solution.py:263
  119.3 9.2 %collective-permute-start.15 = (bf16[2,256,512]{2,1,0:T(8,128)(2,1)S(1)}, bf16[2,256,512]{2,1,0:T(8,128)(2,1)S(1)}, u32[]{:S(2)}, u32[]{:S(2)}) collective-permute-start(bf16[2,256,512]{2,1,0:T(8,128)(2,1)S(1)} %fusion.6), channel_id=1, source_target_pairs={{0,2},{1,5},{2,0},{3,7},{4,6},{5,1},{6,4},{7,3},{8,10},{9,13},{10,... | collective-permute-start | bytes 1572872 | tf_op jit(solution)/shard_map/ppermute | solution.py:264
  128.9 45.8 %copy-start.2 = (bf16[2,256,512]{2,1,0:T(8,128)(2,1)}, bf16[2,256,512]{2,1,0:T(8,128)(2,1)S(1)}, u32[]{:S(2)}) copy-start(bf16[2,256,512]{2,1,0:T(8,128)(2,1)S(1)} %fusion.5.refs_0_) | copy-start | bytes 1572868
  128.9 89.9 %copy-start.1 = (s32[2,256,512]{2,1,0:T(8,128)S(1)}, s32[2,256,512]{2,1,0:T(8,128)}, u32[]{:S(2)}) copy-start(s32[2,256,512]{2,1,0:T(8,128)} %refs_10_.1) | copy-start | bytes 3145732
  128.9 13.6 %collective-permute-start.16 = (bf16[2,256,512]{2,1,0:T(8,128)(2,1)S(1)}, bf16[2,256,512]{2,1,0:T(8,128)(2,1)S(1)}, u32[]{:S(2)}, u32[]{:S(2)}) collective-permute-start(bf16[2,256,512]{2,1,0:T(8,128)(2,1)S(1)} %fusion.5.refs_0_), channel_id=1, source_target_pairs={{0,2},{1,5},{2,0},{3,7},{4,6},{5,1},{6,4},{7,3},{8,10},{9,13},{10,... | collective-permute-start | bytes 1572872 | tf_op jit(solution)/shard_map/ppermute | solution.py:223
  129.5 15.4 %collective-permute-start.17 = (bf16[2,256,512]{2,1,0:T(8,128)(2,1)S(1)}, bf16[2,256,512]{2,1,0:T(8,128)(2,1)S(1)}, u32[]{:S(2)}, u32[]{:S(2)}) collective-permute-start(bf16[2,256,512]{2,1,0:T(8,128)(2,1)S(1)} %fusion.5.refs_0_), channel_id=1, source_target_pairs={{0,4},{1,3},{2,6},{3,1},{4,0},{5,7},{6,2},{7,5},{8,12},{9,11},{10,... | collective-permute-start | bytes 1572872 | tf_op jit(solution)/shard_map/ppermute | solution.py:224
  142.5 9.2 %collective-permute-start.18 = (bf16[2,256,512]{2,1,0:T(8,128)(2,1)S(1)}, bf16[2,256,512]{2,1,0:T(8,128)(2,1)S(1)}, u32[]{:S(2)}, u32[]{:S(2)}) collective-permute-start(bf16[2,256,512]{2,1,0:T(8,128)(2,1)S(1)} %collective-permute-done.16.refs_1_), channel_id=1, source_target_pairs={{0,4},{1,3},{2,6},{3,1},{4,0},{5,7},{6,2},{7,5},{8,12},{9,11},{10,... | collective-permute-start | bytes 1572872 | tf_op jit(solution)/shard_map/ppermute | solution.py:225
  144.4 7.3 %collective-permute-start.19 = (bf16[2,256,512]{2,1,0:T(8,128)(2,1)S(1)}, bf16[2,256,512]{2,1,0:T(8,128)(2,1)S(1)}, u32[]{:S(2)}, u32[]{:S(2)}) collective-permute-start(bf16[2,256,512]{2,1,0:T(8,128)(2,1)S(1)} %fusion.5.refs_0_), channel_id=1, source_target_pairs={{0,1},{1,0},{2,3},{3,2},{4,5},{5,4},{6,7},{7,6},{8,9},{9,8},{10,11... | collective-permute-start | bytes 1572872 | tf_op jit(solution)/shard_map/ppermute | solution.py:227
  144.4 7.3 %collective-permute-start.20 = (bf16[2,256,512]{2,1,0:T(8,128)(2,1)S(1)}, bf16[2,256,512]{2,1,0:T(8,128)(2,1)S(1)}, u32[]{:S(2)}, u32[]{:S(2)}) collective-permute-start(bf16[2,256,512]{2,1,0:T(8,128)(2,1)S(1)} %collective-permute-done.16.refs_1_), channel_id=1, source_target_pairs={{0,1},{1,0},{2,3},{3,2},{4,5},{5,4},{6,7},{7,6},{8,9},{9,8},{10,11... | collective-permute-start | bytes 1572872 | tf_op jit(solution)/shard_map/ppermute | solution.py:227
  144.9 6.8 %collective-permute-start.21 = (bf16[2,256,512]{2,1,0:T(8,128)(2,1)S(1)}, bf16[2,256,512]{2,1,0:T(8,128)(2,1)S(1)}, u32[]{:S(2)}, u32[]{:S(2)}) collective-permute-start(bf16[2,256,512]{2,1,0:T(8,128)(2,1)S(1)} %collective-permute-done.17.refs_2_), channel_id=1, source_target_pairs={{0,1},{1,0},{2,3},{3,2},{4,5},{5,4},{6,7},{7,6},{8,9},{9,8},{10,11... | collective-permute-start | bytes 1572872 | tf_op jit(solution)/shard_map/ppermute | solution.py:227
  151.7 1.9 collective-permute-start.22
  151.7 1.9 copy-start.6
  151.7 1.9 copy-start.7
  153.6 0.8 copy-start.8
  174.7 16.7 %collective-permute-start.23 = (bf16[2,256,512]{2,1,0:T(8,128)(2,1)S(1)}, bf16[2,256,512]{2,1,0:T(8,128)(2,1)S(1)}, u32[]{:S(2)}, u32[]{:S(2)}) collective-permute-start(bf16[2,256,512]{2,1,0:T(8,128)(2,1)S(1)} %get-tuple-element.15), channel_id=1, source_target_pairs={{0,8},{8,16},{1,9},{9,17},{2,10},{10,18},{3,11},{11,19},{4,12},{12... | collective-permute-start | bytes 1572872 | tf_op jit(solution)/shard_map/ppermute | solution.py:273
  176.6 27.1 %collective-permute-start.25 = (bf16[2,256,512]{2,1,0:T(8,128)(2,1)S(1)}, bf16[2,256,512]{2,1,0:T(8,128)(2,1)S(1)}, u32[]{:S(2)}, u32[]{:S(2)}) collective-permute-start(bf16[2,256,512]{2,1,0:T(8,128)(2,1)S(1)} %get-tuple-element.17), channel_id=1, source_target_pairs={{24,16},{16,8},{25,17},{17,9},{26,18},{18,10},{27,19},{19,11},{28,... | collective-permute-start | bytes 1572872 | tf_op jit(solution)/shard_map/ppermute | solution.py:274
  177.9 27.9 %collective-permute-start.27 = (bf16[2,256,512]{2,1,0:T(8,128)(2,1)S(1)}, bf16[2,256,512]{2,1,0:T(8,128)(2,1)S(1)}, u32[]{:S(2)}, u32[]{:S(2)}) collective-permute-start(bf16[2,256,512]{2,1,0:T(8,128)(2,1)S(1)} %get-tuple-element.18), channel_id=1, source_target_pairs={{0,24},{1,25},{2,26},{3,27},{4,28},{5,29},{6,30},{7,31}} | collective-permute-start | bytes 1572872 | tf_op jit(solution)/shard_map/ppermute | solution.py:271
  178.6 27.2 %collective-permute-start.28 = (bf16[2,256,512]{2,1,0:T(8,128)(2,1)S(1)}, bf16[2,256,512]{2,1,0:T(8,128)(2,1)S(1)}, u32[]{:S(2)}, u32[]{:S(2)}) collective-permute-start(bf16[2,256,512]{2,1,0:T(8,128)(2,1)S(1)} %get-tuple-element.19), channel_id=1, source_target_pairs={{24,0},{25,1},{26,2},{27,3},{28,4},{29,5},{30,6},{31,7}} | collective-permute-start | bytes 1572872 | tf_op jit(solution)/shard_map/ppermute | solution.py:272
  191.5 21.6 %collective-permute-start.24 = (bf16[2,256,512]{2,1,0:T(8,128)(2,1)S(1)}, bf16[2,256,512]{2,1,0:T(8,128)(2,1)S(1)}, u32[]{:S(2)}, u32[]{:S(2)}) collective-permute-start(bf16[2,256,512]{2,1,0:T(8,128)(2,1)S(1)} %add_convert_fusion.1), channel_id=1, source_target_pairs={{0,8},{8,16},{16,24},{1,9},{9,17},{17,25},{2,10},{10,18},{18,26},{... | collective-permute-start | bytes 1572872 | tf_op jit(solution)/shard_map/ppermute | solution.py:275
  203.8 15.0 %collective-permute-start.26 = (bf16[2,256,512]{2,1,0:T(8,128)(2,1)S(1)}, bf16[2,256,512]{2,1,0:T(8,128)(2,1)S(1)}, u32[]{:S(2)}, u32[]{:S(2)}) collective-permute-start(bf16[2,256,512]{2,1,0:T(8,128)(2,1)S(1)} %add_convert_fusion), channel_id=1, source_target_pairs={{8,0},{16,8},{24,16},{9,1},{17,9},{25,17},{10,2},{18,10},{26,18},{... | collective-permute-start | bytes 1572872 | tf_op jit(solution)/shard_map/ppermute | solution.py:276

commit v2 on v0

--- a/solution.py
+++ b/solution.py
@@ -1,12 +1,24 @@
+import functools
+
 import jax
 import jax.numpy as jnp
+import numpy as np
 from jax import lax
+from jax.experimental import pallas as pl
+from jax.experimental.pallas import tpu as pltpu
 from jax.sharding import PartitionSpec as P
 
 LAYERS = 8
-
-
-def on_device(resid, enc, enc_bias, fire, dec, dec_bias, target):
+GROUPS = 4
+VMEM = pl.BlockSpec(memory_space=pltpu.VMEM)
+SMEM = pl.BlockSpec(memory_space=pltpu.SMEM)
+HBM = pl.BlockSpec(memory_space=pltpu.HBM)
+SLOTS = 3
+CHUNKS = 2
+LIMIT = 48 * 2**20
+
+
+def plain(resid, enc, enc_bias, fire, dec, dec_bias, target):
     group = lax.axis_index("layer")
     half = LAYERS // 2
     pre = jnp.einsum(
@@ -62,6 +74,391 @@
     return (error, act_grad)
 
 
+ONE = [(0, 1), (1, 0), (2, 3)]
+MIDDLE = [(1, 2), (2, 1)]
+TWO = [(0, 2), (2, 0), (1, 3), (3, 1)]
+RELAY = [(2, 3), (1, 0)]
+BUFFER = [[0, 1, 3, 4], [1, 0, 2, 3], [3, 2, 0, 1], [4, 3, 1, 0]]
+MIX = [(0, 1), (3, 2), (2, 0), (1, 3)]
+ENDS = [(0, 3), (3, 0)]
+BACK_ONE = [(0, 1), (1, 0), (3, 2)]
+FLIP = [(i, i ^ 1) for i in range(8)]
+FIRST = [(i, i ^ (4 if i & 1 else 2)) for i in range(8)]
+SECOND = [(i, i ^ (2 if i & 1 else 4)) for i in range(8)]
+
+
+def pairs_of(group):
+    return [(k, k, 0) if k <= group else (k, k - group - 1, 1) for k in range(LAYERS + 1)]
+
+
+def table(entries):
+    out = np.zeros((GROUPS, 1 + max(len(e) for e in entries), 4), np.int32)
+    for g, rows in enumerate(entries):
+        out[g, 0, 0] = len(rows)
+        slots = [slot for _, _, slot in rows]
+        for i, row in enumerate(rows):
+            out[g, i + 1] = (*row, slots.index(row[2]) == i)
+    return out
+
+
+def reconstruct_tables():
+    early, late = [], []
+    for g in range(GROUPS):
+        rows = ([], [])
+        for k, source, slot in pairs_of(g):
+            buffer, odd = BUFFER[g][source // 2], source % 2
+            if odd and buffer:
+                rows[1].append((k, buffer - 1, slot))
+            else:
+                rows[0].append((k, 0 if odd else buffer + 1, slot))
+        early.append(rows[0])
+        late.append(rows[1])
+    return table(early), table(late)
+
+
+def gradient_tables():
+    first, rest = [], []
+    for g in range(GROUPS):
+        rows = ([], [])
+        for k, source, slot in pairs_of(g):
+            place, odd = source // 2 ^ g, source % 2
+            if place == 2 or (place == 3 and g < 2):
+                rows[0].append((k, 2 * (place - 2) + odd, slot))
+            else:
+                rows[1].append((k, 2 * (1, 3, 0).index(place) + odd, slot))
+        first.append(sorted(rows[0], key=lambda r: r[1]))
+        rest.append(sorted(rows[1], key=lambda r: r[1]))
+    return table(first), table(rest)
+
+
+def bring(sources, places, sems):
+    copies = [
+        pltpu.make_async_copy(source, place, sems.at[i])
+        for i, (source, place) in enumerate(zip(sources, places))
+    ]
+    for copy in copies:
+        copy.start()
+    return copies
+
+
+def encode_kernel(layer, order, bias, *refs):
+    *blocks, enc, fire, out, held, weight, mask, acc, sems, wsems, fsem = refs
+    width = blocks[0].shape[1]
+    rows = [pl.ds(pl.multiple_of(order[i] * width, width), width) for i in range(8)]
+    weights = bring([enc.at[layer, r, :] for r in rows], [weight.at[i] for i in range(8)], wsems)
+    values = bring(blocks, [held.at[i] for i in range(8)], sems)
+    fired = pltpu.make_async_copy(fire.at[layer], mask, fsem)
+    fired.start()
+    for i in range(8):
+        values[i].wait()
+        weights[i].wait()
+        term = jnp.dot(held[i], weight[i], preferred_element_type=jnp.float32)
+        if i == 0:
+            acc[...] = term
+        else:
+            acc[...] += term
+    fired.wait()
+    value = acc[...] + bias[layer : layer + 1, :]
+    out[...] = (mask[...].astype(jnp.float32) * value).astype(jnp.bfloat16)
+
+
+def encode(order, blocks, enc, bias, fire, layer):
+    tokens, width = blocks[0].shape
+    _, depth, feats = enc.shape
+    return pl.pallas_call(
+        functools.partial(encode_kernel, layer),
+        in_specs=[SMEM, VMEM] + [HBM] * 10,
+        out_specs=VMEM,
+        out_shape=jax.ShapeDtypeStruct((tokens, feats), jnp.bfloat16),
+        scratch_shapes=[
+            pltpu.VMEM((8, tokens, width), jnp.bfloat16),
+            pltpu.VMEM((8, width, feats), jnp.bfloat16),
+            pltpu.VMEM((tokens, feats), jnp.int32),
+            pltpu.VMEM((tokens, feats), jnp.float32),
+            pltpu.SemaphoreType.DMA((8,)),
+            pltpu.SemaphoreType.DMA((8,)),
+            pltpu.SemaphoreType.DMA(()),
+        ],
+        compiler_params=pltpu.CompilerParams(vmem_limit_bytes=LIMIT),
+        cost_estimate=cost(1),
+        name="encode",
+    )(order, bias, *blocks, enc, fire)
+
+
+def fetch(entries, dec, ring, sems, i):
+    slot = i % SLOTS
+    return pltpu.make_async_copy(dec.at[entries[i + 1, 0]], ring.at[slot], sems.at[slot])
+
+
+def open_stream(entries, dec, ring, sems):
+    for i in range(SLOTS):
+
+        @pl.when(i < entries[0, 0])
+        def _():
+            fetch(entries, dec, ring, sems, i).start()
+
+
+def run_stream(entries, dec, ring, sems, use):
+    count = entries[0, 0]
+
+    def step(i, carry):
+        fetch(entries, dec, ring, sems, i).wait()
+        use(i + 1, ring.at[i % SLOTS])
+
+        @pl.when(i + SLOTS < count)
+        def _():
+            fetch(entries, dec, ring, sems, i + SLOTS).start()
+
+        return carry
+
+    lax.fori_loop(0, count, step, 0)
+
+
+def stream_scratch(dec):
+    return [pltpu.VMEM((SLOTS, *dec.shape[1:]), dec.dtype), pltpu.SemaphoreType.DMA((SLOTS,))]
+
+
+def cost(weight):
+    return pl.CostEstimate(flops=weight * 10**9, bytes_accessed=weight * 2**20, transcendentals=0)
+
+
+def add_pair(acc, slot, acts, dec):
+    quarter = dec.shape[1] // 4
+    for j in range(4):
+        part = slice(j * quarter, (j + 1) * quarter)
+        acc[slot, :, part] += jnp.dot(acts, dec[:, part], preferred_element_type=jnp.float32)
+
+
+def early_kernel(entries, *refs):
+    *sources, dec, out, held, acc, hsems, ring, sems = refs
+    copies = bring(sources, [held.at[i] for i in range(len(sources))], hsems)
+    open_stream(entries, dec, ring, sems)
+    acc[...] = jnp.zeros_like(acc)
+    for copy in copies:
+        copy.wait()
+
+    def use(e, block):
+        add_pair(acc, entries[e, 2], held[entries[e, 1]], block)
+
+    run_stream(entries, dec, ring, sems, use)
+    out[...] = acc[...].astype(out.dtype)
+
+
+def reconstruct_early(entries, sources, dec):
+    tokens, feats = sources[0].shape
+    depth = dec.shape[2]
+    return pl.pallas_call(
+        early_kernel,
+        in_specs=[SMEM] + [HBM] * len(sources) + [HBM],
+        out_specs=VMEM,
+        scratch_shapes=[
+            pltpu.VMEM((len(sources), tokens, feats), jnp.bfloat16),
+            pltpu.VMEM((2, tokens, depth), jnp.float32),
+            pltpu.SemaphoreType.DMA((len(sources),)),
+        ]
+        + stream_scratch(dec),
+        out_shape=jax.ShapeDtypeStruct((2, tokens, depth), jnp.bfloat16),
+        compiler_params=pltpu.CompilerParams(vmem_limit_bytes=LIMIT),
+        cost_estimate=cost(10),
+        name="reconstruct_early",
+    )(entries, *sources, dec)
+
+
+def late_kernel(entries, cols, *refs):
+    *sources, before, dec, keep0, send0, keep1, send1, held, acc, earlier, hsems, ring, sems = refs
+    copies = bring([*sources, before], [held.at[i] for i in range(len(sources))] + [earlier], hsems)
+    open_stream(entries, dec, ring, sems)
+    acc[...] = jnp.zeros_like(acc)
+    tokens, width = keep0.shape[2:]
+    for copy in copies[:-1]:
+        copy.wait()
+
+    def use(e, block):
+        add_pair(acc, entries[e, 2], held[entries[e, 1]], block)
+
+    run_stream(entries, dec, ring, sems, use)
+    copies[-1].wait()
+    for c, (keep, send) in enumerate(((keep0, send0), (keep1, send1))):
+        rows = slice(c * tokens, (c + 1) * tokens)
+        for i in range(8):
+            place = pl.ds(pl.multiple_of(cols[i] * width, width), width)
+            out = keep if i < 4 else send
+            for s in range(2):
+                value = acc[s, rows, place] + earlier[s, rows, place].astype(jnp.float32)
+                out[i % 4, s] = value.astype(jnp.bfloat16)
+
+
+def reconstruct_late(entries, cols, sources, before, dec):
+    tokens, feats = sources[0].shape
+    depth = dec.shape[2]
+    out = jax.ShapeDtypeStruct((4, 2, tokens // CHUNKS, depth // 8), jnp.bfloat16)
+    return pl.pallas_call(
+        late_kernel,
+        in_specs=[SMEM] * 2 + [HBM] * len(sources) + [HBM, HBM],
+        out_specs=[VMEM] * 4,
+        scratch_shapes=[
+            pltpu.VMEM((len(sources), tokens, feats), jnp.bfloat16),
+            pltpu.VMEM((2, tokens, depth), jnp.float32),
+            pltpu.VMEM((2, tokens, depth), jnp.bfloat16),
+            pltpu.SemaphoreType.DMA((len(sources) + 1,)),
+        ]
+        + stream_scratch(dec),
+        out_shape=[out] * 4,
+        compiler_params=pltpu.CompilerParams(vmem_limit_bytes=LIMIT),
+        cost_estimate=cost(10),
+        name="reconstruct_late",
+    )(entries, cols, *sources, before, dec)
+
+
+def add_term(entries, e, error, total, block):
+    total[entries[e, 1]] += lax.dot_general(
+        error[entries[e, 2]], block[...], (((1,), (1,)), ((), ())), preferred_element_type=jnp.float32
+    )
+
+
+def first_kernel(entries, cols, *refs):
+    *blocks, dec, two, three, error, total, bsems, ring, sems = refs
+    tokens, width = blocks[0].shape[1:]
+    places = [pl.ds(pl.multiple_of(cols[j] * width, width), width) for j in range(8)]
+    copies = bring(
+        blocks,
+        [error.at[:, c * tokens : (c + 1) * tokens, p] for c in range(len(blocks) // 8) for p in places],
+        bsems,
+    )
+    open_stream(entries, dec, ring, sems)
+    total[...] = jnp.zeros_like(total)
+    for copy in copies:
+        copy.wait()
+    run_stream(
+        entries, dec, ring, sems, lambda e, block: add_term(entries, e, error, total, block)
+    )
+    two[...] = total[:2].astype(two.dtype)
+    three[...] = total[2:]
+
+
+def first_gradients(entries, cols, blocks, dec):
+    tokens = blocks[0].shape[1] * (len(blocks) // 8)
+    _, feats, depth = dec.shape
+    return pl.pallas_call(
+        first_kernel,
+        in_specs=[SMEM] * 2 + [HBM] * len(blocks) + [HBM],
+        out_specs=[VMEM] * 3,
+        scratch_shapes=[
+            pltpu.VMEM((4, tokens, feats), jnp.float32),
+            pltpu.SemaphoreType.DMA((len(blocks),)),
+        ]
+        + stream_scratch(dec),
+        out_shape=[
+            jax.ShapeDtypeStruct((2, tokens, feats), jnp.bfloat16),
+            jax.ShapeDtypeStruct((2, tokens, feats), jnp.float32),
+            jax.ShapeDtypeStruct((2, tokens, depth), jnp.bfloat16),
+        ],
+        compiler_params=pltpu.CompilerParams(vmem_limit_bytes=LIMIT),
+        cost_estimate=cost(10),
+        name="first_gradients",
+    )(entries, cols, *blocks, dec)
+
+
+def rest_kernel(entries, whole, begun, dec, one, three, own, error, total, esem, tsem, ring, sems):
+    copy = pltpu.make_async_copy(whole, error, esem)
+    copy.start()
+    more = pltpu.make_async_copy(begun, total.at[2:4], tsem)
+    more.start()
+    open_stream(entries, dec, ring, sems)
+    total[0:2] = jnp.zeros_like(total[0:2])
+    total[4:6] = jnp.zeros_like(total[4:6])
+    copy.wait()
+    more.wait()
+    run_stream(
+        entries, dec, ring, sems, lambda e, block: add_term(entries, e, error, total, block)
+    )
+    for i, out in enumerate((one, three, own)):
+        out[...] = total[2 * i : 2 * i + 2].astype(out.dtype)
+
+
+def rest_gradients(entries, whole, begun, dec):
+    _, tokens, depth = whole.shape
+    feats = dec.shape[1]
+    return pl.pallas_call(
+        rest_kernel,
+        in_specs=[SMEM, HBM, HBM, HBM],
+        out_specs=[VMEM] * 3,
+        scratch_shapes=[
+            pltpu.VMEM((2, tokens, depth), jnp.bfloat16),
+            pltpu.VMEM((6, tokens, feats), jnp.float32),
+            pltpu.SemaphoreType.DMA(()),
+            pltpu.SemaphoreType.DMA(()),
+        ]
+        + stream_scratch(dec),
+        out_shape=[
+            jax.ShapeDtypeStruct((2, tokens, feats), t)
+            for t in (jnp.bfloat16, jnp.bfloat16, jnp.float32)
+        ],
+        compiler_params=pltpu.CompilerParams(vmem_limit_bytes=LIMIT),
+        cost_estimate=cost(10),
+        name="rest_gradients",
+    )(entries, whole, begun, dec)
+
+
+def gather(own):
+    first = lax.ppermute(own, "feat", FIRST)
+    second = lax.ppermute(own, "feat", SECOND)
+    both = lax.ppermute(first, "feat", SECOND)
+    mine = [own, first, second, both]
+    return mine + [lax.ppermute(b, "feat", FLIP) for b in mine]
+
+
+def on_device(resid, enc, enc_bias, fire, dec, dec_bias, target):
+    f32, bf16 = jnp.float32, jnp.bfloat16
+    group = lax.axis_index("layer")
+    me = lax.axis_index("feat")
+    core = me & 1
+    one, two = 2 + 2 * core, 4 - 2 * core
+    none = 0 * core
+    near = jnp.stack([none, one, two, none + 6, none + 1, two ^ 1, one ^ 1, none + 7])
+    columns = (me ^ near).astype(jnp.int32)
+    early_table, late_table = (jnp.asarray(t)[group] for t in reconstruct_tables())
+    first_table, rest_table = (jnp.asarray(t)[group] for t in gradient_tables())
+
+    masks = pltpu.with_memory_space_constraint(fire, pltpu.HBM)
+    ways = []
+    for layer in range(2):
+        acts = encode(columns, gather(resid[layer]), enc, enc_bias, masks, layer)
+        two_away = lax.ppermute(acts, "layer", TWO)
+        nearest = lax.ppermute(acts, "layer", ONE)
+        middle = lax.ppermute(acts, "layer", MIDDLE)
+        relayed = lax.ppermute(two_away, "layer", RELAY)
+        ways.append((acts, nearest, middle, two_away, relayed))
+    a, b = ways
+    before = reconstruct_early(early_table, [b[0], *a], dec)
+    halves = reconstruct_late(late_table, columns, b[1:], before, dec)
+
+    tokens = resid.shape[1] // CHUNKS
+    errors, blocks = [], []
+    for c in range(CHUNKS):
+        span = slice(c * tokens, (c + 1) * tokens)
+        keep, send = halves[2 * c : 2 * c + 2]
+        pair = keep.astype(f32) + lax.ppermute(send, "feat", FLIP).astype(f32)
+        far = lax.ppermute(pair[2:].astype(bf16), "feat", SECOND).astype(f32)
+        close = lax.ppermute((pair[1] + far[1]).astype(bf16), "feat", FIRST).astype(f32)
+        recon = pair[0] + far[0] + close
+        error = recon + dec_bias.astype(f32)[:, None, :] - target[:, span].astype(f32)
+        errors.append(error.astype(bf16))
+        blocks += gather(errors[c])
+
+    two_away, begun, whole = first_gradients(first_table, columns, blocks, dec)
+    mixed = lax.ppermute(two_away, "layer", MIX)
+    one_away, three_away, own = rest_gradients(rest_table, whole, begun, dec)
+    ends = lax.ppermute(three_away, "layer", ENDS)
+    middle = (three_away.astype(f32) + mixed.astype(f32)).astype(bf16)
+    middle = lax.ppermute(middle, "layer", MIDDLE)
+    one_away = lax.ppermute(one_away, "layer", BACK_ONE)
+    inner = (group == 1) | (group == 2)
+    total = own + one_away.astype(f32) + middle.astype(f32)
+    total = total + jnp.where(inner, 0.0, mixed.astype(f32) + ends.astype(f32))
+    return jnp.concatenate(errors, axis=1), fire.astype(f32) * total
+
+
 def solution(mesh):
     placed = (
         P("layer", None, "feat"),
@@ -72,8 +469,9 @@
         P("layer", "feat"),
         P("layer", None, "feat"),
     )
+    blocks = mesh.shape["feat"] == 8 and mesh.shape["layer"] == GROUPS
     return jax.shard_map(
-        on_device,
+        on_device if blocks else plain,
         mesh=mesh,
         in_specs=placed,
         out_specs=(P("layer", None, "feat"), P("layer", None, "feat")),

time: 366 us -> 192 us (0.52); the launches traced: 362 us -> 192 us
  waiting for transfers between devices: 246 us -> 76.9 us
  matrix products: 65.4 us -> 0 us
  starting transfers between devices: 0.2 us -> 52.3 us
  Pallas kernels: 0 us -> 48.1 us
  between operations: 13.9 us -> 0.99 us
  blocking collectives: 8.87 us -> 0 us
  local copies, waits for them, and re-layouts: 14.6 us -> 7.08 us
  other arithmetic: 12.8 us -> 6.28 us
    psum x1 -> x0, waiting for transfers between devices: 120 us -> none  [on_device(): recon = lax.psum(partial_value, 'feat')]
    all_gather x3 -> x0, waiting for transfers between devices: 84.2 us -> none  [the longest x1 43.6 us: on_device(): every = lax.all_gather(acts, 'layer', axis=0, tiled=True)]
    ppermute x0 -> x46, waiting for transfers between devices: none -> 76.9 us  [the longest x1 17.5 us: on_device(): one_away = lax.ppermute(one_away, 'layer', BACK_ONE)]
    dot_general x7 -> x0, matrix products: 65.4 us -> none  [the longest x1 12.5 us: on_device(): jnp.einsum('ktf,kfd->td', lead_acts * (1 - lead_mask), dec[:half], prefer...]
    ppermute x0 -> x46, starting transfers between devices: none -> 52.3 us  [the longest x2 11.7 us: on_device(): relayed = lax.ppermute(two_away, 'layer', RELAY)]
    pallas_call x0 -> x6, Pallas kernels: none -> 48.1 us  [the longest x1 12 us: rest_gradients(): pl.pallas_call(rest_kernel, in_specs=[SMEM, HBM, HBM, HBM], out_specs=[VM...]
    reduce_scatter x1 -> x0, waiting for transfers between devices: 40.2 us -> none  [on_device(): lax.psum_scatter(grad_terms.astype(jnp.bfloat16), 'layer', scatter_dimens...]
    all_gather x1 -> x0, blocking collectives: 8.87 us -> none  [on_device(): lax.all_gather(dec_bias, 'feat', axis=1, tiled=True)]
  transfers between devices with their start and end apart: 5 -> 46, of which waited for: 4 -> 17; matrix products, arithmetic and copies ran while one was open for 12% -> 3% of each run, Pallas kernels for 0% -> 16%
where the time goes in v2:
time: 192 us
  waiting for transfers between devices  76.9 us (40%)
  starting transfers between devices  52.3 us (27%)
  Pallas kernels  48.1 us (25%)
  local copies, waits for them, and re-layouts  7.08 us (4%)
  other arithmetic  6.28 us (3%)
    ppermute x1, waiting for transfers between devices, on_device(): one_away = lax.ppermute(one_away, 'layer', BACK_ONE)  17.5 us
    ppermute x4, waiting for transfers between devices, gather(): first = lax.ppermute(own, 'feat', FIRST)  16 us
    ppermute x2, waiting for transfers between devices, on_device(): far = lax.ppermute(pair[2:].astype(bf16), 'feat', SECOND).astype(f32)  14.6 us
    pallas_call x1, Pallas kernels, rest_gradients(): pl.pallas_call(rest_kernel, in_specs=[SMEM, HBM, HBM, HBM], out_specs=[VM...  12 us
    ppermute x2, starting transfers between devices, on_device(): relayed = lax.ppermute(two_away, 'layer', RELAY)  11.7 us
    pallas_call x1, Pallas kernels, reconstruct_early(): pl.pallas_call(early_kernel, in_specs=[SMEM] + [HBM] * len(sources) + [HB...  11.1 us
    ppermute x4, waiting for transfers between devices, gather(): both = lax.ppermute(first, 'feat', SECOND)  9.53 us
    pallas_call x1, Pallas kernels, first_gradients(): pl.pallas_call(first_kernel, in_specs=[SMEM] * 2 + [HBM] * len(blocks) +...  9.28 us
  transfers between devices with their start and end apart: 46, of which 17 were waited for; matrix products, arithmetic and copies ran while one was open for 3% of the time, Pallas kernels for 16%

profile of v2, /device:TPU:10, one launch (start us, length us, event | category | flops | bytes accessed | tf_op | source)
XLA Modules:
  0.0 191.7 jit_solution(8390489284934423559)
XLA Ops:
  0.6 1.1 slice_bitcast_fusion
  2.3 1.5 collective-permute-start.12
  3.8 1.5 collective-permute-start
  5.3 5.5 %collective-permute-done.11.refs_1_ = bf16[256,512]{1,0:T(8,128)(2,1)S(1)} collective-permute-done((bf16[256,512]{1,0:T(8,128)(2,1)S(1)}, bf16[256,512]{1,0:T(8,128)(2,1)S(1)}, u32[]{:S(2)}, u32[]{:S(2)}) %collective-permute-start.11) | collective-permute-done | bytes 262176 | tf_op jit(solution)/shard_map/ppermute | solution.py:404
  11.6 1.3 collective-permute-start.1
  13.4 3.1 %collective-permute-done.refs_1_ = bf16[256,512]{1,0:T(8,128)(2,1)S(1)} collective-permute-done((bf16[256,512]{1,0:T(8,128)(2,1)S(1)}, bf16[256,512]{1,0:T(8,128)(2,1)S(1)}, u32[]{:S(2)}, u32[]{:S(2)}) %collective-permute-start) | collective-permute-done | bytes 262176 | tf_op jit(solution)/shard_map/ppermute | solution.py:404
  16.5 0.8 collective-permute-done.13.refs_3_
  17.3 2.7 %collective-permute-done.1.refs_2_ = bf16[256,512]{1,0:T(8,128)(2,1)S(1)} collective-permute-done((bf16[256,512]{1,0:T(8,128)(2,1)S(1)}, bf16[256,512]{1,0:T(8,128)(2,1)S(1)}, u32[]{:S(2)}, u32[]{:S(2)}) %collective-permute-start.1) | collective-permute-done | bytes 262176 | tf_op jit(solution)/shard_map/ppermute | solution.py:405
  20.6 2.2 %collective-permute-done.2.refs_3_ = bf16[256,512]{1,0:T(8,128)(2,1)S(1)} collective-permute-done((bf16[256,512]{1,0:T(8,128)(2,1)S(1)}, bf16[256,512]{1,0:T(8,128)(2,1)S(1)}, u32[]{:S(2)}, u32[]{:S(2)}) %collective-permute-start.2) | collective-permute-done | bytes 262176 | tf_op jit(solution)/shard_map/ppermute | solution.py:406
  23.5 3.4 %encode.3.refs_1_ = bf16[256,512]{1,0:T(8,128)(2,1)S(1)} custom-call(s32[8]{0:T(128)S(1)} %broadcast_xor_fusion.order.cols, f32[2,512]{1,0:T(2,128)S(1)} %copy-done.1, bf16[256,512]{1,0:T(8,128)(2,1)S(1)} %get-tuple-element.24.refs_0_, bf16[256,512]{1,0:T(8,128)(2,1)S(1)} %collective-permute-done.11.refs_1_, ...), custom_call_target="tpu_custom_call" | custom-call | flops 1000000000 | bytes 1048576 | tf_op jit(solution)/shard_map/encode/pallas_call | solution.py:168
  26.9 2.7 %collective-permute-start.20 = (bf16[256,512]{1,0:T(8,128)(2,1)S(1)}, bf16[256,512]{1,0:T(8,128)(2,1)S(1)}, u32[]{:S(2)}, u32[]{:S(2)}) collective-permute-start(bf16[256,512]{1,0:T(8,128)(2,1)S(1)} %encode.3.refs_1_), channel_id=1, source_target_pairs={{0,16},{16,0},{8,24},{24,8},{1,17},{17,1},{9,25},{25,9},{2,18},{18... | collective-permute-start | bytes 786440 | tf_op jit(solution)/shard_map/ppermute | solution.py:427
  29.6 2.3 %collective-permute-start.18 = (bf16[256,512]{1,0:T(8,128)(2,1)S(1)}, bf16[256,512]{1,0:T(8,128)(2,1)S(1)}, u32[]{:S(2)}, u32[]{:S(2)}) collective-permute-start(bf16[256,512]{1,0:T(8,128)(2,1)S(1)} %encode.3.refs_1_), channel_id=1, source_target_pairs={{0,8},{8,0},{16,24},{1,9},{9,1},{17,25},{2,10},{10,2},{18,26},{3,1... | collective-permute-start | bytes 786440 | tf_op jit(solution)/shard_map/ppermute | solution.py:428
  32.0 3.4 %encode.2.refs_0_ = bf16[256,512]{1,0:T(8,128)(2,1)S(1)} custom-call(s32[8]{0:T(128)S(1)} %broadcast_xor_fusion.order.cols, f32[2,512]{1,0:T(2,128)S(1)} %copy-done.1, bf16[256,512]{1,0:T(8,128)(2,1)S(1)} %get-tuple-element.25.refs_0_, bf16[256,512]{1,0:T(8,128)(2,1)S(1)} %collective-permute-done.refs_1_, ...), custom_call_target="tpu_custom_call" | custom-call | flops 1000000000 | bytes 1048576 | tf_op jit(solution)/shard_map/encode/pallas_call | solution.py:168
  35.5 4.9 %collective-permute-start.19 = (bf16[256,512]{1,0:T(8,128)(2,1)S(1)}, bf16[256,512]{1,0:T(8,128)(2,1)S(1)}, u32[]{:S(2)}, u32[]{:S(2)}) collective-permute-start(bf16[256,512]{1,0:T(8,128)(2,1)S(1)} %encode.3.refs_1_), channel_id=1, source_target_pairs={{8,16},{16,8},{9,17},{17,9},{10,18},{18,10},{11,19},{19,11},{12,20... | collective-permute-start | bytes 786440 | tf_op jit(solution)/shard_map/ppermute | solution.py:429
  40.4 1.2 collective-permute-done.20.refs_4_
  41.6 9.0 %collective-permute-start.21 = (bf16[256,512]{1,0:T(8,128)(2,1)S(1)}, bf16[256,512]{1,0:T(8,128)(2,1)S(1)}, u32[]{:S(2)}, u32[]{:S(2)}) collective-permute-start(bf16[256,512]{1,0:T(8,128)(2,1)S(1)} %collective-permute-done.20.refs_4_), channel_id=1, source_target_pairs={{16,24},{8,0},{17,25},{9,1},{18,26},{10,2},{19,27},{11,3},{20,28},... | collective-permute-start | bytes 786440 | tf_op jit(solution)/shard_map/ppermute | solution.py:430
  52.2 1.9 collective-permute-start.7
  54.2 1.9 %collective-permute-start.8 = (bf16[256,512]{1,0:T(8,128)(2,1)S(1)}, bf16[256,512]{1,0:T(8,128)(2,1)S(1)}, u32[]{:S(2)}, u32[]{:S(2)}) collective-permute-start(bf16[256,512]{1,0:T(8,128)(2,1)S(1)} %encode.2.refs_0_), channel_id=1, source_target_pairs={{8,16},{16,8},{9,17},{17,9},{10,18},{18,10},{11,19},{19,11},{12,20... | collective-permute-start | bytes 786440 | tf_op jit(solution)/shard_map/ppermute | solution.py:429
  56.1 2.7 %collective-permute-start.10 = (bf16[256,512]{1,0:T(8,128)(2,1)S(1)}, bf16[256,512]{1,0:T(8,128)(2,1)S(1)}, u32[]{:S(2)}, u32[]{:S(2)}) collective-permute-start(bf16[256,512]{1,0:T(8,128)(2,1)S(1)} %collective-permute-done.9.refs_2_), channel_id=1, source_target_pairs={{16,24},{8,0},{17,25},{9,1},{18,26},{10,2},{19,27},{11,3},{20,28},... | collective-permute-start | bytes 786440 | tf_op jit(solution)/shard_map/ppermute | solution.py:430
  58.8 11.1 %reconstruct_early.1.refs_4_ = bf16[2,256,4096]{2,1,0:T(8,128)(2,1)S(1)} custom-call(s32[7,4]{1,0:T(8,128)S(1)} %copy.13.entries, bf16[256,512]{1,0:T(8,128)(2,1)S(1)} %encode.2.refs_0_, bf16[256,512]{1,0:T(8,128)(2,1)S(1)} %encode.3.refs_1_, bf16[256,512]{1,0:T(8,128)(2,1)S(1)} %collective-permute-done.18.refs_2_, ...), custom_call_target="tpu_custom_call" | custom-call | flops 10000000000 | bytes 10485760 | tf_op jit(solution)/shard_map/reconstruct_early/pallas_call | solution.py:250
  69.9 2.0 %copy-done = bf16[2,256,4096]{2,1,0:T(8,128)(2,1)} copy-done((bf16[2,256,4096]{2,1,0:T(8,128)(2,1)}, bf16[2,256,4096]{2,1,0:T(8,128)(2,1)S(1)}, u32[]{:S(2)}) %copy-start) | copy-done | bytes 4194328
  71.9 8.9 %reconstruct_late.1 = (bf16[4,2,128,512]{3,2,1,0:T(8,128)(2,1)S(1)}, bf16[4,2,128,512]{3,2,1,0:T(8,128)(2,1)S(1)}, bf16[4,2,128,512]{3,2,1,0:T(8,128)(2,1)S(1)}, bf16[4,2,128,512]{3,2,1,0:T(8,128)(2,1)S(1)}) custom-call(s32[5,4]{1,0:T(8,128)S(1)} %copy.14.entries, s32[8]{0:T(128)S(1)} %broadcast_xor_fusion.order.cols, ...), custom_call_target="tpu_custom_call" | custom-call | flops 10000000000 | bytes 10485760 | tf_op jit(solution)/shard_map/reconstruct_late/pallas_call | solution.py:295
  81.3 2.1 %collective-permute-done.25 = bf16[4,2,128,512]{3,2,1,0:T(8,128)(2,1)S(1)} collective-permute-done((bf16[4,2,128,512]{3,2,1,0:T(8,128)(2,1)S(1)}, bf16[4,2,128,512]{3,2,1,0:T(8,128)(2,1)S(1)}, u32[]{:S(2)}, u32[]{:S(2)}) %collective-permute-start.25) | collective-permute-done | bytes 1048608 | tf_op jit(solution)/shard_map/ppermute | solution.py:441
  83.9 0.8 collective-permute-start.26
  85.4 1.0 collective-permute-start.23
  86.4 6.7 %collective-permute-done.26 = bf16[2,2,128,512]{3,2,1,0:T(8,128)(2,1)S(1)} collective-permute-done((bf16[2,2,128,512]{3,2,1,0:T(8,128)(2,1)S(1)}, bf16[2,2,128,512]{3,2,1,0:T(8,128)(2,1)S(1)}, u32[]{:S(2)}, u32[]{:S(2)}) %collective-permute-start.26) | collective-permute-done | bytes 524320 | tf_op jit(solution)/shard_map/ppermute | solution.py:442
  93.7 7.8 %collective-permute-done.23 = bf16[2,2,128,512]{3,2,1,0:T(8,128)(2,1)S(1)} collective-permute-done((bf16[2,2,128,512]{3,2,1,0:T(8,128)(2,1)S(1)}, bf16[2,2,128,512]{3,2,1,0:T(8,128)(2,1)S(1)}, u32[]{:S(2)}, u32[]{:S(2)}) %collective-permute-start.23) | collective-permute-done | bytes 524320 | tf_op jit(solution)/shard_map/ppermute | solution.py:442
  102.1 6.1 %collective-permute-done.24 = bf16[2,128,512]{2,1,0:T(8,128)(2,1)S(1)} collective-permute-done((bf16[2,128,512]{2,1,0:T(8,128)(2,1)S(1)}, bf16[2,128,512]{2,1,0:T(8,128)(2,1)S(1)}, u32[]{:S(2)}, u32[]{:S(2)}) %collective-permute-start.24) | collective-permute-done | bytes 262176 | tf_op jit(solution)/shard_map/ppermute | solution.py:443
  108.9 1.7 collective-permute-start.35
  110.6 0.7 collective-permute-start.29
  111.4 1.3 collective-permute-start.36
  112.7 4.6 %collective-permute-done.28.refs_1_ = bf16[2,128,512]{2,1,0:T(8,128)(2,1)S(1)} collective-permute-done((bf16[2,128,512]{2,1,0:T(8,128)(2,1)S(1)}, bf16[2,128,512]{2,1,0:T(8,128)(2,1)S(1)}, u32[]{:S(2)}, u32[]{:S(2)}) %collective-permute-start.28) | collective-permute-done | bytes 262176 | tf_op jit(solution)/shard_map/ppermute | solution.py:404
  117.3 2.8 %collective-permute-done.35.refs_9_ = bf16[2,128,512]{2,1,0:T(8,128)(2,1)S(1)} collective-permute-done((bf16[2,128,512]{2,1,0:T(8,128)(2,1)S(1)}, bf16[2,128,512]{2,1,0:T(8,128)(2,1)S(1)}, u32[]{:S(2)}, u32[]{:S(2)}) %collective-permute-start.35) | collective-permute-done | bytes 262176 | tf_op jit(solution)/shard_map/ppermute | solution.py:404
  120.1 0.7 collective-permute-start.30
  120.8 1.3 collective-permute-start.37
  122.7 3.7 %collective-permute-done.30.refs_3_ = bf16[2,128,512]{2,1,0:T(8,128)(2,1)S(1)} collective-permute-done((bf16[2,128,512]{2,1,0:T(8,128)(2,1)S(1)}, bf16[2,128,512]{2,1,0:T(8,128)(2,1)S(1)}, u32[]{:S(2)}, u32[]{:S(2)}) %collective-permute-start.30) | collective-permute-done | bytes 262176 | tf_op jit(solution)/shard_map/ppermute | solution.py:406
  126.4 2.8 %collective-permute-done.37.refs_11_ = bf16[2,128,512]{2,1,0:T(8,128)(2,1)S(1)} collective-permute-done((bf16[2,128,512]{2,1,0:T(8,128)(2,1)S(1)}, bf16[2,128,512]{2,1,0:T(8,128)(2,1)S(1)}, u32[]{:S(2)}, u32[]{:S(2)}) %collective-permute-start.37) | collective-permute-done | bytes 262176 | tf_op jit(solution)/shard_map/ppermute | solution.py:406
  131.4 9.3 %first_gradients.1 = (bf16[2,256,512]{2,1,0:T(8,128)(2,1)S(1)}, f32[2,256,512]{2,1,0:T(8,128)S(1)}, bf16[2,256,4096]{2,1,0:T(8,128)(2,1)}) custom-call(s32[5,4]{1,0:T(8,128)S(1)} %copy.15.entries, s32[8]{0:T(128)S(1)} %broadcast_xor_fusion.order.cols, bf16[2,128,512]{2,1,0:T(8,128)(2,1)S(1)} %get-tuple-element.22.refs_0_, ...), custom_call_target="tpu_custom_call" | custom-call | flops 10000000000 | bytes 10485760 | tf_op jit(solution)/shard_map/first_gradients/pallas_call | solution.py:342
  140.6 4.4 %collective-permute-start.43 = (bf16[2,256,512]{2,1,0:T(8,128)(2,1)S(1)}, bf16[2,256,512]{2,1,0:T(8,128)(2,1)S(1)}, u32[]{:S(2)}, u32[]{:S(2)}) collective-permute-start(bf16[2,256,512]{2,1,0:T(8,128)(2,1)S(1)} %get-tuple-element.21), channel_id=1, source_target_pairs={{0,8},{24,16},{16,0},{8,24},{1,9},{25,17},{17,1},{9,25},{2,10},{26... | collective-permute-start | bytes 1572872 | tf_op jit(solution)/shard_map/ppermute | solution.py:450
  145.1 12.0 %rest_gradients.1 = (bf16[2,256,512]{2,1,0:T(8,128)(2,1)S(1)}, bf16[2,256,512]{2,1,0:T(8,128)(2,1)S(1)}, f32[2,256,512]{2,1,0:T(8,128)S(1)}) custom-call(s32[7,4]{1,0:T(8,128)S(1)} %copy.16.entries, bf16[2,256,4096]{2,1,0:T(8,128)(2,1)} %get-tuple-element.16.whole, f32[2,256,512]{2,1,0:T(8,128)S(1)} %get-tuple-element.17.begun, bf16[9,512,4096]{2,1,0:T(8,128)(2,1)} %dec.1), custom_call_target="tpu_custom_call" | custom-call | flops 10000000000 | bytes 10485760 | tf_op jit(solution)/shard_map/rest_gradients/pallas_call | solution.py:382
  157.1 1.9 %collective-permute-start.42 = (bf16[2,256,512]{2,1,0:T(8,128)(2,1)S(1)}, bf16[2,256,512]{2,1,0:T(8,128)(2,1)}, u32[]{:S(2)}, u32[]{:S(2)}) collective-permute-start(bf16[2,256,512]{2,1,0:T(8,128)(2,1)S(1)} %get-tuple-element.19), channel_id=1, source_target_pairs={{0,8},{8,0},{24,16},{1,9},{9,1},{25,17},{2,10},{10,2},{26,18},{3,1... | collective-permute-start | bytes 1572872 | tf_op jit(solution)/shard_map/ppermute | solution.py:455
  159.0 1.5 collective-permute-start.45
  160.5 0.9 fusion
  161.4 1.9 collective-permute-start.44
  163.4 0.8 pad_maximum_fusion
  164.2 17.5 %collective-permute-done.42 = bf16[2,256,512]{2,1,0:T(8,128)(2,1)} collective-permute-done((bf16[2,256,512]{2,1,0:T(8,128)(2,1)S(1)}, bf16[2,256,512]{2,1,0:T(8,128)(2,1)}, u32[]{:S(2)}, u32[]{:S(2)}) %collective-permute-start.42) | collective-permute-done | bytes 524320 | tf_op jit(solution)/shard_map/ppermute | solution.py:455
  181.6 6.8 %collective-permute-done.44 = bf16[2,256,512]{2,1,0:T(8,128)(2,1)} collective-permute-done((bf16[2,256,512]{2,1,0:T(8,128)(2,1)}, bf16[2,256,512]{2,1,0:T(8,128)(2,1)}, u32[]{:S(2)}, u32[]{:S(2)}) %collective-permute-start.44) | collective-permute-done | bytes 524320 | tf_op jit(solution)/shard_map/ppermute | solution.py:454
  188.5 3.2 %fusion.3 = f32[2,256,512]{2,1,0:T(8,128)} fusion(bf16[2,256,512]{2,1,0:T(8,128)(2,1)S(1)} %collective-permute-done.43, bf16[2,256,512]{2,1,0:T(8,128)(2,1)} %collective-permute-done.45, bf16[2,256,512]{2,1,0:T(8,128)(2,1)} %collective-permute-done.44, f32[2,256,512]{2,1,0:T(8,128)S(1)} %get-tuple-element.18, ...), kind=kLoop, calls=%fused_computation.7 | loop fusion | flops 2883584 | bytes 5242881 | tf_op jit(solution)/shard_map/mul | solution.py:459
  (82 shorter events, 11.0 us)
Async XLA Ops:
  1.7 9.1 %collective-permute-start.11 = (bf16[256,512]{1,0:T(8,128)(2,1)S(1)}, bf16[256,512]{1,0:T(8,128)(2,1)S(1)}, u32[]{:S(2)}, u32[]{:S(2)}) collective-permute-start(bf16[256,512]{1,0:T(8,128)(2,1)S(1)} %get-tuple-element.24.refs_0_), channel_id=1, source_target_pairs={{0,2},{1,5},{2,0},{3,7},{4,6},{5,1},{6,4},{7,3},{8,10},{9,13},{10,... | collective-permute-start | bytes 786440 | tf_op jit(solution)/shard_map/ppermute | solution.py:404
  2.3 10.6 %collective-permute-start.12 = (bf16[256,512]{1,0:T(8,128)(2,1)S(1)}, bf16[256,512]{1,0:T(8,128)(2,1)S(1)}, u32[]{:S(2)}, u32[]{:S(2)}) collective-permute-start(bf16[256,512]{1,0:T(8,128)(2,1)S(1)} %get-tuple-element.24.refs_0_), channel_id=1, source_target_pairs={{0,4},{1,3},{2,6},{3,1},{4,0},{5,7},{6,2},{7,5},{8,12},{9,11},{10,... | collective-permute-start | bytes 786440 | tf_op jit(solution)/shard_map/ppermute | solution.py:405
  3.8 9.1 %collective-permute-start.14 = (bf16[256,512]{1,0:T(8,128)(2,1)S(1)}, bf16[256,512]{1,0:T(8,128)(2,1)S(1)}, u32[]{:S(2)}, u32[]{:S(2)}) collective-permute-start(bf16[256,512]{1,0:T(8,128)(2,1)S(1)} %get-tuple-element.24.refs_0_), channel_id=1, source_target_pairs={{0,1},{1,0},{2,3},{3,2},{4,5},{5,4},{6,7},{7,6},{8,9},{9,8},{10,11... | collective-permute-start | bytes 786440 | tf_op jit(solution)/shard_map/ppermute | solution.py:408
  3.8 12.6 %collective-permute-start = (bf16[256,512]{1,0:T(8,128)(2,1)S(1)}, bf16[256,512]{1,0:T(8,128)(2,1)S(1)}, u32[]{:S(2)}, u32[]{:S(2)}) collective-permute-start(bf16[256,512]{1,0:T(8,128)(2,1)S(1)} %get-tuple-element.25.refs_0_), channel_id=1, source_target_pairs={{0,2},{1,5},{2,0},{3,7},{4,6},{5,1},{6,4},{7,3},{8,10},{9,13},{10,... | collective-permute-start | bytes 786440 | tf_op jit(solution)/shard_map/ppermute | solution.py:404
  10.8 6.4 %collective-permute-start.13 = (bf16[256,512]{1,0:T(8,128)(2,1)S(1)}, bf16[256,512]{1,0:T(8,128)(2,1)S(1)}, u32[]{:S(2)}, u32[]{:S(2)}) collective-permute-start(bf16[256,512]{1,0:T(8,128)(2,1)S(1)} %collective-permute-done.11.refs_1_), channel_id=1, source_target_pairs={{0,4},{1,3},{2,6},{3,1},{4,0},{5,7},{6,2},{7,5},{8,12},{9,11},{10,... | collective-permute-start | bytes 786440 | tf_op jit(solution)/shard_map/ppermute | solution.py:406
  11.6 8.5 %collective-permute-start.1 = (bf16[256,512]{1,0:T(8,128)(2,1)S(1)}, bf16[256,512]{1,0:T(8,128)(2,1)S(1)}, u32[]{:S(2)}, u32[]{:S(2)}) collective-permute-start(bf16[256,512]{1,0:T(8,128)(2,1)S(1)} %get-tuple-element.25.refs_0_), channel_id=1, source_target_pairs={{0,4},{1,3},{2,6},{3,1},{4,0},{5,7},{6,2},{7,5},{8,12},{9,11},{10,... | collective-permute-start | bytes 786440 | tf_op jit(solution)/shard_map/ppermute | solution.py:405
  12.9 7.2 %collective-permute-start.15 = (bf16[256,512]{1,0:T(8,128)(2,1)S(1)}, bf16[256,512]{1,0:T(8,128)(2,1)S(1)}, u32[]{:S(2)}, u32[]{:S(2)}) collective-permute-start(bf16[256,512]{1,0:T(8,128)(2,1)S(1)} %collective-permute-done.11.refs_1_), channel_id=1, source_target_pairs={{0,1},{1,0},{2,3},{3,2},{4,5},{5,4},{6,7},{7,6},{8,9},{9,8},{10,11... | collective-permute-start | bytes 786440 | tf_op jit(solution)/shard_map/ppermute | solution.py:408
  12.9 7.7 %collective-permute-start.16 = (bf16[256,512]{1,0:T(8,128)(2,1)S(1)}, bf16[256,512]{1,0:T(8,128)(2,1)S(1)}, u32[]{:S(2)}, u32[]{:S(2)}) collective-permute-start(bf16[256,512]{1,0:T(8,128)(2,1)S(1)} %collective-permute-done.12.refs_2_), channel_id=1, source_target_pairs={{0,1},{1,0},{2,3},{3,2},{4,5},{5,4},{6,7},{7,6},{8,9},{9,8},{10,11... | collective-permute-start | bytes 786440 | tf_op jit(solution)/shard_map/ppermute | solution.py:408
  16.5 6.4 %collective-permute-start.2 = (bf16[256,512]{1,0:T(8,128)(2,1)S(1)}, bf16[256,512]{1,0:T(8,128)(2,1)S(1)}, u32[]{:S(2)}, u32[]{:S(2)}) collective-permute-start(bf16[256,512]{1,0:T(8,128)(2,1)S(1)} %collective-permute-done.refs_1_), channel_id=1, source_target_pairs={{0,4},{1,3},{2,6},{3,1},{4,0},{5,7},{6,2},{7,5},{8,12},{9,11},{10,... | collective-permute-start | bytes 786440 | tf_op jit(solution)/shard_map/ppermute | solution.py:406
  17.2 5.6 %collective-permute-start.17 = (bf16[256,512]{1,0:T(8,128)(2,1)S(1)}, bf16[256,512]{1,0:T(8,128)(2,1)S(1)}, u32[]{:S(2)}, u32[]{:S(2)}) collective-permute-start(bf16[256,512]{1,0:T(8,128)(2,1)S(1)} %collective-permute-done.13.refs_3_), channel_id=1, source_target_pairs={{0,1},{1,0},{2,3},{3,2},{4,5},{5,4},{6,7},{7,6},{8,9},{9,8},{10,11... | collective-permute-start | bytes 786440 | tf_op jit(solution)/shard_map/ppermute | solution.py:408
  20.0 9.6 %collective-permute-start.3 = (bf16[256,512]{1,0:T(8,128)(2,1)S(1)}, bf16[256,512]{1,0:T(8,128)(2,1)S(1)}, u32[]{:S(2)}, u32[]{:S(2)}) collective-permute-start(bf16[256,512]{1,0:T(8,128)(2,1)S(1)} %get-tuple-element.25.refs_0_), channel_id=1, source_target_pairs={{0,1},{1,0},{2,3},{3,2},{4,5},{5,4},{6,7},{7,6},{8,9},{9,8},{10,11... | collective-permute-start | bytes 786440 | tf_op jit(solution)/shard_map/ppermute | solution.py:408
  20.0 11.9 %collective-permute-start.4 = (bf16[256,512]{1,0:T(8,128)(2,1)S(1)}, bf16[256,512]{1,0:T(8,128)(2,1)S(1)}, u32[]{:S(2)}, u32[]{:S(2)}) collective-permute-start(bf16[256,512]{1,0:T(8,128)(2,1)S(1)} %collective-permute-done.refs_1_), channel_id=1, source_target_pairs={{0,1},{1,0},{2,3},{3,2},{4,5},{5,4},{6,7},{7,6},{8,9},{9,8},{10,11... | collective-permute-start | bytes 786440 | tf_op jit(solution)/shard_map/ppermute | solution.py:408
  20.5 11.4 %collective-permute-start.5 = (bf16[256,512]{1,0:T(8,128)(2,1)S(1)}, bf16[256,512]{1,0:T(8,128)(2,1)S(1)}, u32[]{:S(2)}, u32[]{:S(2)}) collective-permute-start(bf16[256,512]{1,0:T(8,128)(2,1)S(1)} %collective-permute-done.1.refs_2_), channel_id=1, source_target_pairs={{0,1},{1,0},{2,3},{3,2},{4,5},{5,4},{6,7},{7,6},{8,9},{9,8},{10,11... | collective-permute-start | bytes 786440 | tf_op jit(solution)/shard_map/ppermute | solution.py:408
  22.8 9.2 %collective-permute-start.6 = (bf16[256,512]{1,0:T(8,128)(2,1)S(1)}, bf16[256,512]{1,0:T(8,128)(2,1)S(1)}, u32[]{:S(2)}, u32[]{:S(2)}) collective-permute-start(bf16[256,512]{1,0:T(8,128)(2,1)S(1)} %collective-permute-done.2.refs_3_), channel_id=1, source_target_pairs={{0,1},{1,0},{2,3},{3,2},{4,5},{5,4},{6,7},{7,6},{8,9},{9,8},{10,11... | collective-permute-start | bytes 786440 | tf_op jit(solution)/shard_map/ppermute | solution.py:408
  26.9 14.7 %collective-permute-start.20 = (bf16[256,512]{1,0:T(8,128)(2,1)S(1)}, bf16[256,512]{1,0:T(8,128)(2,1)S(1)}, u32[]{:S(2)}, u32[]{:S(2)}) collective-permute-start(bf16[256,512]{1,0:T(8,128)(2,1)S(1)} %encode.3.refs_1_), channel_id=1, source_target_pairs={{0,16},{16,0},{8,24},{24,8},{1,17},{17,1},{9,25},{25,9},{2,18},{18... | collective-permute-start | bytes 786440 | tf_op jit(solution)/shard_map/ppermute | solution.py:427
  29.6 24.5 %collective-permute-start.18 = (bf16[256,512]{1,0:T(8,128)(2,1)S(1)}, bf16[256,512]{1,0:T(8,128)(2,1)S(1)}, u32[]{:S(2)}, u32[]{:S(2)}) collective-permute-start(bf16[256,512]{1,0:T(8,128)(2,1)S(1)} %encode.3.refs_1_), channel_id=1, source_target_pairs={{0,8},{8,0},{16,24},{1,9},{9,1},{17,25},{2,10},{10,2},{18,26},{3,1... | collective-permute-start | bytes 786440 | tf_op jit(solution)/shard_map/ppermute | solution.py:428
  35.4 20.7 %collective-permute-start.9 = (bf16[256,512]{1,0:T(8,128)(2,1)S(1)}, bf16[256,512]{1,0:T(8,128)(2,1)S(1)}, u32[]{:S(2)}, u32[]{:S(2)}) collective-permute-start(bf16[256,512]{1,0:T(8,128)(2,1)S(1)} %encode.2.refs_0_), channel_id=1, source_target_pairs={{0,16},{16,0},{8,24},{24,8},{1,17},{17,1},{9,25},{25,9},{2,18},{18... | collective-permute-start | bytes 786440 | tf_op jit(solution)/shard_map/ppermute | solution.py:427
  35.5 23.3 %collective-permute-start.19 = (bf16[256,512]{1,0:T(8,128)(2,1)S(1)}, bf16[256,512]{1,0:T(8,128)(2,1)S(1)}, u32[]{:S(2)}, u32[]{:S(2)}) collective-permute-start(bf16[256,512]{1,0:T(8,128)(2,1)S(1)} %encode.3.refs_1_), channel_id=1, source_target_pairs={{8,16},{16,8},{9,17},{17,9},{10,18},{18,10},{11,19},{19,11},{12,20... | collective-permute-start | bytes 786440 | tf_op jit(solution)/shard_map/ppermute | solution.py:429
  41.6 17.2 %collective-permute-start.21 = (bf16[256,512]{1,0:T(8,128)(2,1)S(1)}, bf16[256,512]{1,0:T(8,128)(2,1)S(1)}, u32[]{:S(2)}, u32[]{:S(2)}) collective-permute-start(bf16[256,512]{1,0:T(8,128)(2,1)S(1)} %collective-permute-done.20.refs_4_), channel_id=1, source_target_pairs={{16,24},{8,0},{17,25},{9,1},{18,26},{10,2},{19,27},{11,3},{20,28},... | collective-permute-start | bytes 786440 | tf_op jit(solution)/shard_map/ppermute | solution.py:430
  52.2 19.7 %collective-permute-start.7 = (bf16[256,512]{1,0:T(8,128)(2,1)S(1)}, bf16[256,512]{1,0:T(8,128)(2,1)S(1)}, u32[]{:S(2)}, u32[]{:S(2)}) collective-permute-start(bf16[256,512]{1,0:T(8,128)(2,1)S(1)} %encode.2.refs_0_), channel_id=1, source_target_pairs={{0,8},{8,0},{16,24},{1,9},{9,1},{17,25},{2,10},{10,2},{18,26},{3,1... | collective-permute-start | bytes 786440 | tf_op jit(solution)/shard_map/ppermute | solution.py:428
  54.2 17.7 %collective-permute-start.8 = (bf16[256,512]{1,0:T(8,128)(2,1)S(1)}, bf16[256,512]{1,0:T(8,128)(2,1)S(1)}, u32[]{:S(2)}, u32[]{:S(2)}) collective-permute-start(bf16[256,512]{1,0:T(8,128)(2,1)S(1)} %encode.2.refs_0_), channel_id=1, source_target_pairs={{8,16},{16,8},{9,17},{17,9},{10,18},{18,10},{11,19},{19,11},{12,20... | collective-permute-start | bytes 786440 | tf_op jit(solution)/shard_map/ppermute | solution.py:429
  56.1 15.8 %collective-permute-start.10 = (bf16[256,512]{1,0:T(8,128)(2,1)S(1)}, bf16[256,512]{1,0:T(8,128)(2,1)S(1)}, u32[]{:S(2)}, u32[]{:S(2)}) collective-permute-start(bf16[256,512]{1,0:T(8,128)(2,1)S(1)} %collective-permute-done.9.refs_2_), channel_id=1, source_target_pairs={{16,24},{8,0},{17,25},{9,1},{18,26},{10,2},{19,27},{11,3},{20,28},... | collective-permute-start | bytes 786440 | tf_op jit(solution)/shard_map/ppermute | solution.py:430
  80.8 2.7 %collective-permute-start.25 = (bf16[4,2,128,512]{3,2,1,0:T(8,128)(2,1)S(1)}, bf16[4,2,128,512]{3,2,1,0:T(8,128)(2,1)S(1)}, u32[]{:S(2)}, u32[]{:S(2)}) collective-permute-start(bf16[4,2,128,512]{3,2,1,0:T(8,128)(2,1)S(1)} %get-tuple-element.15), channel_id=1, source_target_pairs={{0,1},{1,0},{2,3},{3,2},{4,5},{5,4},{6,7},{7,6},{8,9},{9,8},{10,11... | collective-permute-start | bytes 3145736 | tf_op jit(solution)/shard_map/ppermute | solution.py:441
  80.8 4.1 %collective-permute-start.22 = (bf16[4,2,128,512]{3,2,1,0:T(8,128)(2,1)S(1)}, bf16[4,2,128,512]{3,2,1,0:T(8,128)(2,1)S(1)}, u32[]{:S(2)}, u32[]{:S(2)}) collective-permute-start(bf16[4,2,128,512]{3,2,1,0:T(8,128)(2,1)S(1)} %get-tuple-element.13), channel_id=1, source_target_pairs={{0,1},{1,0},{2,3},{3,2},{4,5},{5,4},{6,7},{7,6},{8,9},{9,8},{10,11... | collective-permute-start | bytes 3145736 | tf_op jit(solution)/shard_map/ppermute | solution.py:441
  83.9 9.2 %collective-permute-start.26 = (bf16[2,2,128,512]{3,2,1,0:T(8,128)(2,1)S(1)}, bf16[2,2,128,512]{3,2,1,0:T(8,128)(2,1)S(1)}, u32[]{:S(2)}, u32[]{:S(2)}) collective-permute-start(bf16[2,2,128,512]{3,2,1,0:T(8,128)(2,1)S(1)} %slice.114), channel_id=1, source_target_pairs={{0,4},{1,3},{2,6},{3,1},{4,0},{5,7},{6,2},{7,5},{8,12},{9,11},{10,... | collective-permute-start | bytes 1572872 | tf_op jit(solution)/shard_map/ppermute | solution.py:442
  85.4 16.2 %collective-permute-start.23 = (bf16[2,2,128,512]{3,2,1,0:T(8,128)(2,1)S(1)}, bf16[2,2,128,512]{3,2,1,0:T(8,128)(2,1)S(1)}, u32[]{:S(2)}, u32[]{:S(2)}) collective-permute-start(bf16[2,2,128,512]{3,2,1,0:T(8,128)(2,1)S(1)} %slice.115), channel_id=1, source_target_pairs={{0,4},{1,3},{2,6},{3,1},{4,0},{5,7},{6,2},{7,5},{8,12},{9,11},{10,... | collective-permute-start | bytes 1572872 | tf_op jit(solution)/shard_map/ppermute | solution.py:442
  93.2 8.9 %copy-start.3 = (bf16[2,512]{1,0:T(2,128)(2,1)S(1)}, bf16[2,512]{1,0:T(2,128)(2,1)}, u32[]{:S(2)}) copy-start(bf16[2,512]{1,0:T(2,128)(2,1)} %param.16) | copy-start | bytes 6148
  93.2 15.0 %copy-start.2 = (bf16[2,256,512]{2,1,0:T(8,128)(2,1)S(1)}, bf16[2,256,512]{2,1,0:T(8,128)(2,1)}, u32[]{:S(2)}) copy-start(bf16[2,256,512]{2,1,0:T(8,128)(2,1)} %param.17) | copy-start | bytes 1572868
  93.3 8.8 %collective-permute-start.27 = (bf16[2,128,512]{2,1,0:T(8,128)(2,1)S(1)}, bf16[2,128,512]{2,1,0:T(8,128)(2,1)S(1)}, u32[]{:S(2)}, u32[]{:S(2)}) collective-permute-start(bf16[2,128,512]{2,1,0:T(8,128)(2,1)S(1)} %fusion.17), channel_id=1, source_target_pairs={{0,2},{1,5},{2,0},{3,7},{4,6},{5,1},{6,4},{7,3},{8,10},{9,13},{10,... | collective-permute-start | bytes 786440 | tf_op jit(solution)/shard_map/ppermute | solution.py:443
  101.8 6.4 %collective-permute-start.24 = (bf16[2,128,512]{2,1,0:T(8,128)(2,1)S(1)}, bf16[2,128,512]{2,1,0:T(8,128)(2,1)S(1)}, u32[]{:S(2)}, u32[]{:S(2)}) collective-permute-start(bf16[2,128,512]{2,1,0:T(8,128)(2,1)S(1)} %fusion.16), channel_id=1, source_target_pairs={{0,2},{1,5},{2,0},{3,7},{4,6},{5,1},{6,4},{7,3},{8,10},{9,13},{10,... | collective-permute-start | bytes 786440 | tf_op jit(solution)/shard_map/ppermute | solution.py:443
  108.5 8.7 %collective-permute-start.28 = (bf16[2,128,512]{2,1,0:T(8,128)(2,1)S(1)}, bf16[2,128,512]{2,1,0:T(8,128)(2,1)S(1)}, u32[]{:S(2)}, u32[]{:S(2)}) collective-permute-start(bf16[2,128,512]{2,1,0:T(8,128)(2,1)S(1)} %get-tuple-element.22.refs_0_), channel_id=1, source_target_pairs={{0,2},{1,5},{2,0},{3,7},{4,6},{5,1},{6,4},{7,3},{8,10},{9,13},{10,... | collective-permute-start | bytes 786440 | tf_op jit(solution)/shard_map/ppermute | solution.py:404
  108.9 11.2 %collective-permute-start.35 = (bf16[2,128,512]{2,1,0:T(8,128)(2,1)S(1)}, bf16[2,128,512]{2,1,0:T(8,128)(2,1)S(1)}, u32[]{:S(2)}, u32[]{:S(2)}) collective-permute-start(bf16[2,128,512]{2,1,0:T(8,128)(2,1)S(1)} %get-tuple-element.23.refs_8_), channel_id=1, source_target_pairs={{0,2},{1,5},{2,0},{3,7},{4,6},{5,1},{6,4},{7,3},{8,10},{9,13},{10,... | collective-permute-start | bytes 786440 | tf_op jit(solution)/shard_map/ppermute | solution.py:404
  110.6 10.2 %collective-permute-start.29 = (bf16[2,128,512]{2,1,0:T(8,128)(2,1)S(1)}, bf16[2,128,512]{2,1,0:T(8,128)(2,1)S(1)}, u32[]{:S(2)}, u32[]{:S(2)}) collective-permute-start(bf16[2,128,512]{2,1,0:T(8,128)(2,1)S(1)} %get-tuple-element.22.refs_0_), channel_id=1, source_target_pairs={{0,4},{1,3},{2,6},{3,1},{4,0},{5,7},{6,2},{7,5},{8,12},{9,11},{10,... | collective-permute-start | bytes 786440 | tf_op jit(solution)/shard_map/ppermute | solution.py:405
  111.4 10.7 %collective-permute-start.36 = (bf16[2,128,512]{2,1,0:T(8,128)(2,1)S(1)}, bf16[2,128,512]{2,1,0:T(8,128)(2,1)S(1)}, u32[]{:S(2)}, u32[]{:S(2)}) collective-permute-start(bf16[2,128,512]{2,1,0:T(8,128)(2,1)S(1)} %get-tuple-element.23.refs_8_), channel_id=1, source_target_pairs={{0,4},{1,3},{2,6},{3,1},{4,0},{5,7},{6,2},{7,5},{8,12},{9,11},{10,... | collective-permute-start | bytes 786440 | tf_op jit(solution)/shard_map/ppermute | solution.py:405
  112.7 9.4 %collective-permute-start.31 = (bf16[2,128,512]{2,1,0:T(8,128)(2,1)S(1)}, bf16[2,128,512]{2,1,0:T(8,128)(2,1)S(1)}, u32[]{:S(2)}, u32[]{:S(2)}) collective-permute-start(bf16[2,128,512]{2,1,0:T(8,128)(2,1)S(1)} %get-tuple-element.22.refs_0_), channel_id=1, source_target_pairs={{0,1},{1,0},{2,3},{3,2},{4,5},{5,4},{6,7},{7,6},{8,9},{9,8},{10,11... | collective-permute-start | bytes 786440 | tf_op jit(solution)/shard_map/ppermute | solution.py:408
  117.3 5.4 %collective-permute-start.38 = (bf16[2,128,512]{2,1,0:T(8,128)(2,1)S(1)}, bf16[2,128,512]{2,1,0:T(8,128)(2,1)S(1)}, u32[]{:S(2)}, u32[]{:S(2)}) collective-permute-start(bf16[2,128,512]{2,1,0:T(8,128)(2,1)S(1)} %get-tuple-element.23.refs_8_), channel_id=1, source_target_pairs={{0,1},{1,0},{2,3},{3,2},{4,5},{5,4},{6,7},{7,6},{8,9},{9,8},{10,11... | collective-permute-start | bytes 786440 | tf_op jit(solution)/shard_map/ppermute | solution.py:408
  120.1 6.4 %collective-permute-start.30 = (bf16[2,128,512]{2,1,0:T(8,128)(2,1)S(1)}, bf16[2,128,512]{2,1,0:T(8,128)(2,1)S(1)}, u32[]{:S(2)}, u32[]{:S(2)}) collective-permute-start(bf16[2,128,512]{2,1,0:T(8,128)(2,1)S(1)} %collective-permute-done.28.refs_1_), channel_id=1, source_target_pairs={{0,4},{1,3},{2,6},{3,1},{4,0},{5,7},{6,2},{7,5},{8,12},{9,11},{10,... | collective-permute-start | bytes 786440 | tf_op jit(solution)/shard_map/ppermute | solution.py:406
  120.8 8.5 %collective-permute-start.37 = (bf16[2,128,512]{2,1,0:T(8,128)(2,1)S(1)}, bf16[2,128,512]{2,1,0:T(8,128)(2,1)S(1)}, u32[]{:S(2)}, u32[]{:S(2)}) collective-permute-start(bf16[2,128,512]{2,1,0:T(8,128)(2,1)S(1)} %collective-permute-done.35.refs_9_), channel_id=1, source_target_pairs={{0,4},{1,3},{2,6},{3,1},{4,0},{5,7},{6,2},{7,5},{8,12},{9,11},{10,... | collective-permute-start | bytes 786440 | tf_op jit(solution)/shard_map/ppermute | solution.py:406
  122.1 7.2 %collective-permute-start.32 = (bf16[2,128,512]{2,1,0:T(8,128)(2,1)S(1)}, bf16[2,128,512]{2,1,0:T(8,128)(2,1)S(1)}, u32[]{:S(2)}, u32[]{:S(2)}) collective-permute-start(bf16[2,128,512]{2,1,0:T(8,128)(2,1)S(1)} %collective-permute-done.28.refs_1_), channel_id=1, source_target_pairs={{0,1},{1,0},{2,3},{3,2},{4,5},{5,4},{6,7},{7,6},{8,9},{9,8},{10,11... | collective-permute-start | bytes 786440 | tf_op jit(solution)/shard_map/ppermute | solution.py:408
  122.1 9.2 %collective-permute-start.39 = (bf16[2,128,512]{2,1,0:T(8,128)(2,1)S(1)}, bf16[2,128,512]{2,1,0:T(8,128)(2,1)S(1)}, u32[]{:S(2)}, u32[]{:S(2)}) collective-permute-start(bf16[2,128,512]{2,1,0:T(8,128)(2,1)S(1)} %collective-permute-done.35.refs_9_), channel_id=1, source_target_pairs={{0,1},{1,0},{2,3},{3,2},{4,5},{5,4},{6,7},{7,6},{8,9},{9,8},{10,11... | collective-permute-start | bytes 786440 | tf_op jit(solution)/shard_map/ppermute | solution.py:408
  122.6 8.7 %collective-permute-start.33 = (bf16[2,128,512]{2,1,0:T(8,128)(2,1)S(1)}, bf16[2,128,512]{2,1,0:T(8,128)(2,1)S(1)}, u32[]{:S(2)}, u32[]{:S(2)}) collective-permute-start(bf16[2,128,512]{2,1,0:T(8,128)(2,1)S(1)} %collective-permute-done.29.refs_2_), channel_id=1, source_target_pairs={{0,1},{1,0},{2,3},{3,2},{4,5},{5,4},{6,7},{7,6},{8,9},{9,8},{10,11... | collective-permute-start | bytes 786440 | tf_op jit(solution)/shard_map/ppermute | solution.py:408
  126.4 4.9 %collective-permute-start.40 = (bf16[2,128,512]{2,1,0:T(8,128)(2,1)S(1)}, bf16[2,128,512]{2,1,0:T(8,128)(2,1)}, u32[]{:S(2)}, u32[]{:S(2)}) collective-permute-start(bf16[2,128,512]{2,1,0:T(8,128)(2,1)S(1)} %collective-permute-done.36.refs_10_), channel_id=1, source_target_pairs={{0,1},{1,0},{2,3},{3,2},{4,5},{5,4},{6,7},{7,6},{8,9},{9,8},{10,11... | collective-permute-start | bytes 786440 | tf_op jit(solution)/shard_map/ppermute | solution.py:408
  129.2 2.1 %collective-permute-start.34 = (bf16[2,128,512]{2,1,0:T(8,128)(2,1)S(1)}, bf16[2,128,512]{2,1,0:T(8,128)(2,1)}, u32[]{:S(2)}, u32[]{:S(2)}) collective-permute-start(bf16[2,128,512]{2,1,0:T(8,128)(2,1)S(1)} %collective-permute-done.30.refs_3_), channel_id=1, source_target_pairs={{0,1},{1,0},{2,3},{3,2},{4,5},{5,4},{6,7},{7,6},{8,9},{9,8},{10,11... | collective-permute-start | bytes 786440 | tf_op jit(solution)/shard_map/ppermute | solution.py:408
  129.3 2.1 %collective-permute-start.41 = (bf16[2,128,512]{2,1,0:T(8,128)(2,1)S(1)}, bf16[2,128,512]{2,1,0:T(8,128)(2,1)}, u32[]{:S(2)}, u32[]{:S(2)}) collective-permute-start(bf16[2,128,512]{2,1,0:T(8,128)(2,1)S(1)} %collective-permute-done.37.refs_11_), channel_id=1, source_target_pairs={{0,1},{1,0},{2,3},{3,2},{4,5},{5,4},{6,7},{7,6},{8,9},{9,8},{10,11... | collective-permute-start | bytes 786440 | tf_op jit(solution)/shard_map/ppermute | solution.py:408
  140.6 19.8 %collective-permute-start.43 = (bf16[2,256,512]{2,1,0:T(8,128)(2,1)S(1)}, bf16[2,256,512]{2,1,0:T(8,128)(2,1)S(1)}, u32[]{:S(2)}, u32[]{:S(2)}) collective-permute-start(bf16[2,256,512]{2,1,0:T(8,128)(2,1)S(1)} %get-tuple-element.21), channel_id=1, source_target_pairs={{0,8},{24,16},{16,0},{8,24},{1,9},{25,17},{17,1},{9,25},{2,10},{26... | collective-permute-start | bytes 1572872 | tf_op jit(solution)/shard_map/ppermute | solution.py:450
  157.1 24.6 %collective-permute-start.42 = (bf16[2,256,512]{2,1,0:T(8,128)(2,1)S(1)}, bf16[2,256,512]{2,1,0:T(8,128)(2,1)}, u32[]{:S(2)}, u32[]{:S(2)}) collective-permute-start(bf16[2,256,512]{2,1,0:T(8,128)(2,1)S(1)} %get-tuple-element.19), channel_id=1, source_target_pairs={{0,8},{8,0},{24,16},{1,9},{9,1},{25,17},{2,10},{10,2},{26,18},{3,1... | collective-permute-start | bytes 1572872 | tf_op jit(solution)/shard_map/ppermute | solution.py:455
  159.0 22.6 %collective-permute-start.45 = (bf16[2,256,512]{2,1,0:T(8,128)(2,1)S(1)}, bf16[2,256,512]{2,1,0:T(8,128)(2,1)}, u32[]{:S(2)}, u32[]{:S(2)}) collective-permute-start(bf16[2,256,512]{2,1,0:T(8,128)(2,1)S(1)} %get-tuple-element.20), channel_id=1, source_target_pairs={{0,24},{24,0},{1,25},{25,1},{2,26},{26,2},{3,27},{27,3},{4,28},{28... | collective-permute-start | bytes 1572872 | tf_op jit(solution)/shard_map/ppermute | solution.py:452
  161.4 27.0 %collective-permute-start.44 = (bf16[2,256,512]{2,1,0:T(8,128)(2,1)}, bf16[2,256,512]{2,1,0:T(8,128)(2,1)}, u32[]{:S(2)}, u32[]{:S(2)}) collective-permute-start(bf16[2,256,512]{2,1,0:T(8,128)(2,1)} %fusion), channel_id=1, source_target_pairs={{8,16},{16,8},{9,17},{17,9},{10,18},{18,10},{11,19},{19,11},{12,20... | collective-permute-start | bytes 1572872 | tf_op jit(solution)/shard_map/ppermute | solution.py:454
  (2 other events, 2.7 us)

commit v3 on v2

--- a/solution.py
+++ b/solution.py
@@ -15,7 +15,7 @@
 HBM = pl.BlockSpec(memory_space=pltpu.HBM)
 SLOTS = 3
 CHUNKS = 2
-LIMIT = 48 * 2**20
+LIMIT = 32 * 2**20
 
 
 def plain(resid, enc, enc_bias, fire, dec, dec_bias, target):
@@ -109,6 +109,8 @@
             buffer, odd = BUFFER[g][source // 2], source % 2
             if odd and buffer:
                 rows[1].append((k, buffer - 1, slot))
+            elif buffer == 4:
+                rows[1].append((k, 4, slot))
             else:
                 rows[0].append((k, 0 if odd else buffer + 1, slot))
         early.append(rows[0])
@@ -117,18 +119,21 @@
 
 
 def gradient_tables():
-    first, rest = [], []
+    first, rest, last = [], [], []
     for g in range(GROUPS):
-        rows = ([], [])
+        rows = ([], [], [])
         for k, source, slot in pairs_of(g):
             place, odd = source // 2 ^ g, source % 2
-            if place == 2 or (place == 3 and g < 2):
+            if place == 0:
+                rows[2].append((k, odd, slot))
+            elif place == 2 or (place == 3 and g < 2):
                 rows[0].append((k, 2 * (place - 2) + odd, slot))
             else:
-                rows[1].append((k, 2 * (1, 3, 0).index(place) + odd, slot))
+                rows[1].append((k, place - 1 + odd, slot))
         first.append(sorted(rows[0], key=lambda r: r[1]))
         rest.append(sorted(rows[1], key=lambda r: r[1]))
-    return table(first), table(rest)
+        last.append(sorted(rows[2], key=lambda r: r[1]))
+    return table(first), table(rest), table(last)
 
 
 def bring(sources, places, sems):
@@ -141,14 +146,16 @@
     return copies
 
 
-def encode_kernel(layer, order, bias, *refs):
-    *blocks, enc, fire, out, held, weight, mask, acc, sems, wsems, fsem = refs
+def encode_kernel(layer, order, *refs):
+    *blocks, bias, enc, fire, out, held, weight, mask, shift, acc, sems, wsems, fsem, ssem = refs
     width = blocks[0].shape[1]
     rows = [pl.ds(pl.multiple_of(order[i] * width, width), width) for i in range(8)]
     weights = bring([enc.at[layer, r, :] for r in rows], [weight.at[i] for i in range(8)], wsems)
     values = bring(blocks, [held.at[i] for i in range(8)], sems)
     fired = pltpu.make_async_copy(fire.at[layer], mask, fsem)
     fired.start()
+    shifted = pltpu.make_async_copy(bias, shift, ssem)
+    shifted.start()
     for i in range(8):
         values[i].wait()
         weights[i].wait()
@@ -158,7 +165,8 @@
         else:
             acc[...] += term
     fired.wait()
-    value = acc[...] + bias[layer : layer + 1, :]
+    shifted.wait()
+    value = acc[...] + shift[layer : layer + 1, :]
     out[...] = (mask[...].astype(jnp.float32) * value).astype(jnp.bfloat16)
 
 
@@ -167,22 +175,24 @@
     _, depth, feats = enc.shape
     return pl.pallas_call(
         functools.partial(encode_kernel, layer),
-        in_specs=[SMEM, VMEM] + [HBM] * 10,
+        in_specs=[SMEM] + [HBM] * 11,
         out_specs=VMEM,
         out_shape=jax.ShapeDtypeStruct((tokens, feats), jnp.bfloat16),
         scratch_shapes=[
             pltpu.VMEM((8, tokens, width), jnp.bfloat16),
             pltpu.VMEM((8, width, feats), jnp.bfloat16),
             pltpu.VMEM((tokens, feats), jnp.int32),
+            pltpu.VMEM(bias.shape, jnp.float32),
             pltpu.VMEM((tokens, feats), jnp.float32),
             pltpu.SemaphoreType.DMA((8,)),
             pltpu.SemaphoreType.DMA((8,)),
+            pltpu.SemaphoreType.DMA(()),
             pltpu.SemaphoreType.DMA(()),
         ],
         compiler_params=pltpu.CompilerParams(vmem_limit_bytes=LIMIT),
         cost_estimate=cost(1),
         name="encode",
-    )(order, bias, *blocks, enc, fire)
+    )(order, *blocks, bias, enc, fire)
 
 
 def fetch(entries, dec, ring, sems, i):
@@ -359,21 +369,20 @@
     )(entries, cols, *blocks, dec)
 
 
-def rest_kernel(entries, whole, begun, dec, one, three, own, error, total, esem, tsem, ring, sems):
+def rest_kernel(entries, whole, begun, dec, one, three, error, total, esem, tsem, ring, sems):
     copy = pltpu.make_async_copy(whole, error, esem)
     copy.start()
     more = pltpu.make_async_copy(begun, total.at[2:4], tsem)
     more.start()
     open_stream(entries, dec, ring, sems)
     total[0:2] = jnp.zeros_like(total[0:2])
-    total[4:6] = jnp.zeros_like(total[4:6])
     copy.wait()
     more.wait()
     run_stream(
         entries, dec, ring, sems, lambda e, block: add_term(entries, e, error, total, block)
     )
-    for i, out in enumerate((one, three, own)):
-        out[...] = total[2 * i : 2 * i + 2].astype(out.dtype)
+    one[...] = total[:2].astype(one.dtype)
+    three[...] = total[2:].astype(three.dtype)
 
 
 def rest_gradients(entries, whole, begun, dec):
@@ -382,22 +391,50 @@
     return pl.pallas_call(
         rest_kernel,
         in_specs=[SMEM, HBM, HBM, HBM],
-        out_specs=[VMEM] * 3,
+        out_specs=[VMEM] * 2,
         scratch_shapes=[
             pltpu.VMEM((2, tokens, depth), jnp.bfloat16),
-            pltpu.VMEM((6, tokens, feats), jnp.float32),
+            pltpu.VMEM((4, tokens, feats), jnp.float32),
             pltpu.SemaphoreType.DMA(()),
             pltpu.SemaphoreType.DMA(()),
         ]
         + stream_scratch(dec),
-        out_shape=[
-            jax.ShapeDtypeStruct((2, tokens, feats), t)
-            for t in (jnp.bfloat16, jnp.bfloat16, jnp.float32)
-        ],
+        out_shape=[jax.ShapeDtypeStruct((2, tokens, feats), jnp.bfloat16)] * 2,
         compiler_params=pltpu.CompilerParams(vmem_limit_bytes=LIMIT),
         cost_estimate=cost(10),
         name="rest_gradients",
     )(entries, whole, begun, dec)
+
+
+def own_kernel(entries, whole, dec, total, error, esem, ring, sems):
+    copy = pltpu.make_async_copy(whole, error, esem)
+    copy.start()
+    open_stream(entries, dec, ring, sems)
+    total[...] = jnp.zeros_like(total)
+    copy.wait()
+    run_stream(
+        entries, dec, ring, sems, lambda e, block: add_term(entries, e, error, total, block)
+    )
+
+
+def own_gradients(entries, whole, dec):
+    _, tokens, depth = whole.shape
+    feats = dec.shape[1]
+    return pl.pallas_call(
+        own_kernel,
+        in_specs=[SMEM, HBM, HBM],
+        out_specs=VMEM,
+        scratch_shapes=[pltpu.VMEM((2, tokens, depth), jnp.bfloat16), pltpu.SemaphoreType.DMA(())]
+        + stream_scratch(dec),
+        out_shape=jax.ShapeDtypeStruct((2, tokens, feats), jnp.float32),
+        compiler_params=pltpu.CompilerParams(vmem_limit_bytes=LIMIT),
+        cost_estimate=cost(10),
+        name="own_gradients",
+    )(entries, whole, dec)
+
+
+def after(array, *others):
+    return lax.optimization_barrier((array, *others))[0]
 
 
 def gather(own):
@@ -405,7 +442,7 @@
     second = lax.ppermute(own, "feat", SECOND)
     both = lax.ppermute(first, "feat", SECOND)
     mine = [own, first, second, both]
-    return mine + [lax.ppermute(b, "feat", FLIP) for b in mine]
+    return [*mine, *(lax.ppermute(b, "feat", FLIP) for b in mine)]
 
 
 def on_device(resid, enc, enc_bias, fire, dec, dec_bias, target):
@@ -418,9 +455,11 @@
     near = jnp.stack([none, one, two, none + 6, none + 1, two ^ 1, one ^ 1, none + 7])
     columns = (me ^ near).astype(jnp.int32)
     early_table, late_table = (jnp.asarray(t)[group] for t in reconstruct_tables())
-    first_table, rest_table = (jnp.asarray(t)[group] for t in gradient_tables())
-
-    masks = pltpu.with_memory_space_constraint(fire, pltpu.HBM)
+    first_table, rest_table, own_table = (jnp.asarray(t)[group] for t in gradient_tables())
+
+    enc, enc_bias, masks = (
+        pltpu.with_memory_space_constraint(x, pltpu.HBM) for x in (enc, enc_bias, fire)
+    )
     ways = []
     for layer in range(2):
         acts = encode(columns, gather(resid[layer]), enc, enc_bias, masks, layer)
@@ -430,8 +469,8 @@
         relayed = lax.ppermute(two_away, "layer", RELAY)
         ways.append((acts, nearest, middle, two_away, relayed))
     a, b = ways
-    before = reconstruct_early(early_table, [b[0], *a], dec)
-    halves = reconstruct_late(late_table, columns, b[1:], before, dec)
+    before = reconstruct_early(early_table, [b[0], *a[:4]], dec)
+    halves = reconstruct_late(late_table, columns, [*b[1:], a[4]], before, dec)
 
     tokens = resid.shape[1] // CHUNKS
     errors, blocks = [], []
@@ -440,7 +479,10 @@
         keep, send = halves[2 * c : 2 * c + 2]
         pair = keep.astype(f32) + lax.ppermute(send, "feat", FLIP).astype(f32)
         far = lax.ppermute(pair[2:].astype(bf16), "feat", SECOND).astype(f32)
-        close = lax.ppermute((pair[1] + far[1]).astype(bf16), "feat", FIRST).astype(f32)
+        close = (pair[1] + far[1]).astype(bf16)
+        if errors:
+            close = after(close, errors[0])
+        close = lax.ppermute(close, "feat", FIRST).astype(f32)
         recon = pair[0] + far[0] + close
         error = recon + dec_bias.astype(f32)[:, None, :] - target[:, span].astype(f32)
         errors.append(error.astype(bf16))
@@ -448,14 +490,16 @@
 
     two_away, begun, whole = first_gradients(first_table, columns, blocks, dec)
     mixed = lax.ppermute(two_away, "layer", MIX)
-    one_away, three_away, own = rest_gradients(rest_table, whole, begun, dec)
+    one_away, three_away = rest_gradients(rest_table, whole, begun, dec)
     ends = lax.ppermute(three_away, "layer", ENDS)
-    middle = (three_away.astype(f32) + mixed.astype(f32)).astype(bf16)
-    middle = lax.ppermute(middle, "layer", MIDDLE)
-    one_away = lax.ppermute(one_away, "layer", BACK_ONE)
+    across = (three_away.astype(f32) + mixed.astype(f32)).astype(bf16)
+    middle = lax.ppermute(across, "layer", MIDDLE)
+    back = lax.ppermute(one_away, "layer", BACK_ONE)
+    own = own_gradients(after(own_table, across), whole, dec)
     inner = (group == 1) | (group == 2)
-    total = own + one_away.astype(f32) + middle.astype(f32)
-    total = total + jnp.where(inner, 0.0, mixed.astype(f32) + ends.astype(f32))
+    here = after(own + jnp.where(inner, 0.0, mixed.astype(f32)))
+    total = here + back.astype(f32) + middle.astype(f32) + ends.astype(f32)
+    errors[0] = after(errors[0], one_away)
     return jnp.concatenate(errors, axis=1), fire.astype(f32) * total
 
 

time: 192 us -> 180 us (0.938)
  waiting for transfers between devices: 76.9 us -> 72.8 us
  starting transfers between devices: 52.3 us -> 49.4 us
  other arithmetic: 6.28 us -> 3.86 us
  local copies, waits for them, and re-layouts: 7.08 us -> 5.1 us
    ppermute x20, waiting for transfers between devices: 30.4 us -> 24 us  [the longest x1 14.6 us: on_device(): middle = lax.ppermute(across, 'layer', MIDDLE)]
    pallas_call x2 -> x3, Pallas kernels: 6.85 us -> 12.5 us  [the longest x2 6.87 us: encode(): pl.pallas_call(functools.partial(encode_kernel, layer), in_specs=[SMEM] +...]
    ppermute x2, starting transfers between devices: 11.7 us -> 6.28 us  [on_device(): relayed = lax.ppermute(two_away, 'layer', RELAY)]
    pallas_call x1, Pallas kernels: 12 us -> 8.46 us  [rest_gradients(): pl.pallas_call(rest_kernel, in_specs=[SMEM, HBM, HBM, HBM], out_specs=[VM...]
    ppermute x2, starting transfers between devices: 6.84 us -> 9.74 us  [on_device(): middle = lax.ppermute(acts, 'layer', MIDDLE)]
    unnamed x8 -> x6, local copies, waits for them, and re-layouts: 2.68 us -> 0.02 us
    squeeze x4 -> x9, local copies, waits for them, and re-layouts: 1.56 us -> 3.8 us  [on_device(): jnp.asarray(t)[group]]
    ppermute x2, waiting for transfers between devices: 0.01 us -> 2.24 us  [on_device(): middle = lax.ppermute(acts, 'layer', MIDDLE)]
  transfers between devices with their start and end apart: 46 -> 46, of which waited for: 17 -> 18; matrix products, arithmetic and copies ran while one was open for 3% -> 4% of each run, Pallas kernels for 16% -> 18%
where the time goes in v3:
time: 180 us
  waiting for transfers between devices  72.8 us (40%)
  starting transfers between devices  49.4 us (27%)
  Pallas kernels  47.5 us (26%)
  local copies, waits for them, and re-layouts  5.1 us (3%)
  other arithmetic  3.86 us (2%)
    ppermute x4, waiting for transfers between devices, gather(): first = lax.ppermute(own, 'feat', FIRST)  17.2 us
    ppermute x1, waiting for transfers between devices, on_device(): middle = lax.ppermute(across, 'layer', MIDDLE)  14.6 us
    ppermute x2, waiting for transfers between devices, on_device(): far = lax.ppermute(pair[2:].astype(bf16), 'feat', SECOND).astype(f32)  14.5 us
    pallas_call x1, Pallas kernels, reconstruct_early(): pl.pallas_call(early_kernel, in_specs=[SMEM] + [HBM] * len(sources) + [HB...  11 us
    ppermute x2, starting transfers between devices, on_device(): middle = lax.ppermute(acts, 'layer', MIDDLE)  9.74 us
    pallas_call x1, Pallas kernels, rest_gradients(): pl.pallas_call(rest_kernel, in_specs=[SMEM, HBM, HBM, HBM], out_specs=[VM...  8.46 us
    pallas_call x1, Pallas kernels, reconstruct_late(): pl.pallas_call(late_kernel, in_specs=[SMEM] * 2 + [HBM] * len(sources) +...  8.04 us
    ppermute x4, waiting for transfers between devices, gather(): both = lax.ppermute(first, 'feat', SECOND)  7.6 us
  transfers between devices with their start and end apart: 46, of which 18 were waited for; matrix products, arithmetic and copies ran while one was open for 4% of the time, Pallas kernels for 18%

profile of v3, /device:TPU:10, one launch (start us, length us, event | category | flops | bytes accessed | tf_op | source)
XLA Modules:
  0.0 179.7 jit_solution(15804884948130854453)
XLA Ops:
  0.6 1.1 slice_bitcast_fusion
  2.3 1.5 collective-permute-start.12
  3.8 1.5 collective-permute-start
  5.3 5.5 %collective-permute-done.11.refs_1_ = bf16[256,512]{1,0:T(8,128)(2,1)S(1)} collective-permute-done((bf16[256,512]{1,0:T(8,128)(2,1)S(1)}, bf16[256,512]{1,0:T(8,128)(2,1)S(1)}, u32[]{:S(2)}, u32[]{:S(2)}) %collective-permute-start.11) | collective-permute-done | bytes 262176 | tf_op jit(solution)/shard_map/ppermute | solution.py:441
  10.8 0.7 collective-permute-start.13
  11.6 1.3 collective-permute-start.1
  13.4 3.1 %collective-permute-done.refs_1_ = bf16[256,512]{1,0:T(8,128)(2,1)S(1)} collective-permute-done((bf16[256,512]{1,0:T(8,128)(2,1)S(1)}, bf16[256,512]{1,0:T(8,128)(2,1)S(1)}, u32[]{:S(2)}, u32[]{:S(2)}) %collective-permute-start) | collective-permute-done | bytes 262176 | tf_op jit(solution)/shard_map/ppermute | solution.py:441
  16.5 0.8 collective-permute-done.13.refs_3_
  17.3 2.7 %collective-permute-done.1.refs_2_ = bf16[256,512]{1,0:T(8,128)(2,1)S(1)} collective-permute-done((bf16[256,512]{1,0:T(8,128)(2,1)S(1)}, bf16[256,512]{1,0:T(8,128)(2,1)S(1)}, u32[]{:S(2)}, u32[]{:S(2)}) %collective-permute-start.1) | collective-permute-done | bytes 262176 | tf_op jit(solution)/shard_map/ppermute | solution.py:442
  20.6 2.2 %collective-permute-done.2.refs_3_ = bf16[256,512]{1,0:T(8,128)(2,1)S(1)} collective-permute-done((bf16[256,512]{1,0:T(8,128)(2,1)S(1)}, bf16[256,512]{1,0:T(8,128)(2,1)S(1)}, u32[]{:S(2)}, u32[]{:S(2)}) %collective-permute-start.2) | collective-permute-done | bytes 262176 | tf_op jit(solution)/shard_map/ppermute | solution.py:443
  22.8 3.4 %encode.3.refs_1_ = bf16[256,512]{1,0:T(8,128)(2,1)S(1)} custom-call(s32[8]{0:T(128)S(1)} %broadcast_xor_fusion.order.cols, bf16[256,512]{1,0:T(8,128)(2,1)S(1)} %get-tuple-element.26.refs_0_, bf16[256,512]{1,0:T(8,128)(2,1)S(1)} %collective-permute-done.11.refs_1_, bf16[256,512]{1,0:T(8,128)(2,1)S(1)} %collective-permute-done.12.refs_2_, ...), custom_call_target="tpu_custom_call" | custom-call | flops 1000000000 | bytes 1048576 | tf_op jit(solution)/shard_map/encode/pallas_call | solution.py:176
  26.3 2.7 %collective-permute-start.18 = (bf16[256,512]{1,0:T(8,128)(2,1)S(1)}, bf16[256,512]{1,0:T(8,128)(2,1)S(1)}, u32[]{:S(2)}, u32[]{:S(2)}) collective-permute-start(bf16[256,512]{1,0:T(8,128)(2,1)S(1)} %encode.3.refs_1_), channel_id=1, source_target_pairs={{0,16},{16,0},{8,24},{24,8},{1,17},{17,1},{9,25},{25,9},{2,18},{18... | collective-permute-start | bytes 786440 | tf_op jit(solution)/shard_map/ppermute | solution.py:466
  28.9 2.3 %collective-permute-start.20 = (bf16[256,512]{1,0:T(8,128)(2,1)S(1)}, bf16[256,512]{1,0:T(8,128)(2,1)S(1)}, u32[]{:S(2)}, u32[]{:S(2)}) collective-permute-start(bf16[256,512]{1,0:T(8,128)(2,1)S(1)} %encode.3.refs_1_), channel_id=1, source_target_pairs={{0,8},{8,0},{16,24},{1,9},{9,1},{17,25},{2,10},{10,2},{18,26},{3,1... | collective-permute-start | bytes 786440 | tf_op jit(solution)/shard_map/ppermute | solution.py:467
  31.3 3.4 %encode.2.refs_0_ = bf16[256,512]{1,0:T(8,128)(2,1)S(1)} custom-call(s32[8]{0:T(128)S(1)} %broadcast_xor_fusion.order.cols, bf16[256,512]{1,0:T(8,128)(2,1)S(1)} %get-tuple-element.27.refs_0_, bf16[256,512]{1,0:T(8,128)(2,1)S(1)} %collective-permute-done.refs_1_, bf16[256,512]{1,0:T(8,128)(2,1)S(1)} %collective-permute-done.1.refs_2_, ...), custom_call_target="tpu_custom_call" | custom-call | flops 1000000000 | bytes 1048576 | tf_op jit(solution)/shard_map/encode/pallas_call | solution.py:176
  34.8 4.9 %collective-permute-start.21 = (bf16[256,512]{1,0:T(8,128)(2,1)S(1)}, bf16[256,512]{1,0:T(8,128)(2,1)S(1)}, u32[]{:S(2)}, u32[]{:S(2)}) collective-permute-start(bf16[256,512]{1,0:T(8,128)(2,1)S(1)} %encode.3.refs_1_), channel_id=1, source_target_pairs={{8,16},{16,8},{9,17},{17,9},{10,18},{18,10},{11,19},{19,11},{12,20... | collective-permute-start | bytes 786440 | tf_op jit(solution)/shard_map/ppermute | solution.py:468
  41.4 1.9 %collective-permute-start.7 = (bf16[256,512]{1,0:T(8,128)(2,1)S(1)}, bf16[256,512]{1,0:T(8,128)(2,1)S(1)}, u32[]{:S(2)}, u32[]{:S(2)}) collective-permute-start(bf16[256,512]{1,0:T(8,128)(2,1)S(1)} %encode.2.refs_0_), channel_id=1, source_target_pairs={{0,8},{8,0},{16,24},{1,9},{9,1},{17,25},{2,10},{10,2},{18,26},{3,1... | collective-permute-start | bytes 786440 | tf_op jit(solution)/shard_map/ppermute | solution.py:467
  43.3 4.8 %collective-permute-start.8 = (bf16[256,512]{1,0:T(8,128)(2,1)S(1)}, bf16[256,512]{1,0:T(8,128)(2,1)S(1)}, u32[]{:S(2)}, u32[]{:S(2)}) collective-permute-start(bf16[256,512]{1,0:T(8,128)(2,1)S(1)} %encode.2.refs_0_), channel_id=1, source_target_pairs={{8,16},{16,8},{9,17},{17,9},{10,18},{18,10},{11,19},{19,11},{12,20... | collective-permute-start | bytes 786440 | tf_op jit(solution)/shard_map/ppermute | solution.py:468
  48.1 2.7 %collective-permute-start.19 = (bf16[256,512]{1,0:T(8,128)(2,1)S(1)}, bf16[256,512]{1,0:T(8,128)(2,1)S(1)}, u32[]{:S(2)}, u32[]{:S(2)}) collective-permute-start(bf16[256,512]{1,0:T(8,128)(2,1)S(1)} %collective-permute-done.18.refs_4_), channel_id=1, source_target_pairs={{16,24},{8,0},{17,25},{9,1},{18,26},{10,2},{19,27},{11,3},{20,28},... | collective-permute-start | bytes 786440 | tf_op jit(solution)/shard_map/ppermute | solution.py:469
  50.8 1.2 collective-permute-done.9.refs_2_
  52.0 3.6 %collective-permute-start.10 = (bf16[256,512]{1,0:T(8,128)(2,1)S(1)}, bf16[256,512]{1,0:T(8,128)(2,1)S(1)}, u32[]{:S(2)}, u32[]{:S(2)}) collective-permute-start(bf16[256,512]{1,0:T(8,128)(2,1)S(1)} %collective-permute-done.9.refs_2_), channel_id=1, source_target_pairs={{16,24},{8,0},{17,25},{9,1},{18,26},{10,2},{19,27},{11,3},{20,28},... | collective-permute-start | bytes 786440 | tf_op jit(solution)/shard_map/ppermute | solution.py:469
  55.7 2.2 %collective-permute-done.21.refs_3_ = bf16[256,512]{1,0:T(8,128)(2,1)S(1)} collective-permute-done((bf16[256,512]{1,0:T(8,128)(2,1)S(1)}, bf16[256,512]{1,0:T(8,128)(2,1)S(1)}, u32[]{:S(2)}, u32[]{:S(2)}) %collective-permute-start.21) | collective-permute-done | bytes 262176 | tf_op jit(solution)/shard_map/ppermute | solution.py:468
  57.9 11.0 %reconstruct_early.1.refs_5_ = bf16[2,256,4096]{2,1,0:T(8,128)(2,1)S(1)} custom-call(s32[7,4]{1,0:T(8,128)S(1)} %copy.14.entries, bf16[256,512]{1,0:T(8,128)(2,1)S(1)} %encode.2.refs_0_, bf16[256,512]{1,0:T(8,128)(2,1)S(1)} %encode.3.refs_1_, bf16[256,512]{1,0:T(8,128)(2,1)S(1)} %collective-permute-done.20.refs_2_, ...), custom_call_target="tpu_custom_call" | custom-call | flops 10000000000 | bytes 10485760 | tf_op jit(solution)/shard_map/reconstruct_early/pallas_call | solution.py:260
  69.0 8.0 %reconstruct_late.1 = (bf16[4,2,128,512]{3,2,1,0:T(8,128)(2,1)S(1)}, bf16[4,2,128,512]{3,2,1,0:T(8,128)(2,1)S(1)}, bf16[4,2,128,512]{3,2,1,0:T(8,128)(2,1)S(1)}, bf16[4,2,128,512]{3,2,1,0:T(8,128)(2,1)S(1)}) custom-call(s32[7,4]{1,0:T(8,128)S(1)} %copy.15.entries, s32[8]{0:T(128)S(1)} %broadcast_xor_fusion.order.cols, ...), custom_call_target="tpu_custom_call" | custom-call | flops 10000000000 | bytes 10485760 | tf_op jit(solution)/shard_map/reconstruct_late/pallas_call | solution.py:305
  77.6 2.1 %collective-permute-done.22 = bf16[4,2,128,512]{3,2,1,0:T(8,128)(2,1)S(1)} collective-permute-done((bf16[4,2,128,512]{3,2,1,0:T(8,128)(2,1)S(1)}, bf16[4,2,128,512]{3,2,1,0:T(8,128)(2,1)S(1)}, u32[]{:S(2)}, u32[]{:S(2)}) %collective-permute-start.22) | collective-permute-done | bytes 1048608 | tf_op jit(solution)/shard_map/ppermute | solution.py:480
  80.1 0.8 collective-permute-start.23
  81.7 1.0 collective-permute-start.33
  82.7 6.7 %collective-permute-done.23 = bf16[2,2,128,512]{3,2,1,0:T(8,128)(2,1)S(1)} collective-permute-done((bf16[2,2,128,512]{3,2,1,0:T(8,128)(2,1)S(1)}, bf16[2,2,128,512]{3,2,1,0:T(8,128)(2,1)S(1)}, u32[]{:S(2)}, u32[]{:S(2)}) %collective-permute-start.23) | collective-permute-done | bytes 524320 | tf_op jit(solution)/shard_map/ppermute | solution.py:481
  90.0 7.8 %collective-permute-done.33 = bf16[2,2,128,512]{3,2,1,0:T(8,128)(2,1)S(1)} collective-permute-done((bf16[2,2,128,512]{3,2,1,0:T(8,128)(2,1)S(1)}, bf16[2,2,128,512]{3,2,1,0:T(8,128)(2,1)S(1)}, u32[]{:S(2)}, u32[]{:S(2)}) %collective-permute-start.33) | collective-permute-done | bytes 524320 | tf_op jit(solution)/shard_map/ppermute | solution.py:481
  98.6 1.7 collective-permute-start.25
  100.3 0.7 collective-permute-start.26
  101.1 6.4 %collective-permute-done.34 = bf16[2,128,512]{2,1,0:T(8,128)(2,1)S(1)} collective-permute-done((bf16[2,128,512]{2,1,0:T(8,128)(2,1)S(1)}, bf16[2,128,512]{2,1,0:T(8,128)(2,1)S(1)}, u32[]{:S(2)}, u32[]{:S(2)}) %collective-permute-start.34) | collective-permute-done | bytes 262176 | tf_op jit(solution)/shard_map/ppermute | solution.py:485
  108.0 0.8 collective-permute-start.36
  108.8 4.3 %collective-permute-done.25.refs_1_ = bf16[2,128,512]{2,1,0:T(8,128)(2,1)S(1)} collective-permute-done((bf16[2,128,512]{2,1,0:T(8,128)(2,1)S(1)}, bf16[2,128,512]{2,1,0:T(8,128)(2,1)S(1)}, u32[]{:S(2)}, u32[]{:S(2)}) %collective-permute-start.25) | collective-permute-done | bytes 262176 | tf_op jit(solution)/shard_map/ppermute | solution.py:441
  113.1 0.7 collective-permute-start.27
  114.3 4.4 %collective-permute-done.35.refs_9_ = bf16[2,128,512]{2,1,0:T(8,128)(2,1)S(1)} collective-permute-done((bf16[2,128,512]{2,1,0:T(8,128)(2,1)S(1)}, bf16[2,128,512]{2,1,0:T(8,128)(2,1)S(1)}, u32[]{:S(2)}, u32[]{:S(2)}) %collective-permute-start.35) | collective-permute-done | bytes 262176 | tf_op jit(solution)/shard_map/ppermute | solution.py:441
  118.7 0.7 collective-permute-start.37
  120.5 4.6 %collective-permute-done.37.refs_11_ = bf16[2,128,512]{2,1,0:T(8,128)(2,1)S(1)} collective-permute-done((bf16[2,128,512]{2,1,0:T(8,128)(2,1)S(1)}, bf16[2,128,512]{2,1,0:T(8,128)(2,1)S(1)}, u32[]{:S(2)}, u32[]{:S(2)}) %collective-permute-start.37) | collective-permute-done | bytes 262176 | tf_op jit(solution)/shard_map/ppermute | solution.py:443
  127.4 7.4 %first_gradients.1 = (bf16[2,256,512]{2,1,0:T(8,128)(2,1)S(1)}, f32[2,256,512]{2,1,0:T(8,128)S(1)}, bf16[2,256,4096]{2,1,0:T(8,128)(2,1)S(1)}) custom-call(s32[5,4]{1,0:T(8,128)S(1)} %copy.16.entries, s32[8]{0:T(128)S(1)} %broadcast_xor_fusion.order.cols, bf16[2,128,512]{2,1,0:T(8,128)(2,1)S(1)} %fusion.13.refs_0_, ...), custom_call_target="tpu_custom_call" | custom-call | flops 10000000000 | bytes 10485760 | tf_op jit(solution)/shard_map/first_gradients/pallas_call | solution.py:352
  134.8 3.8 %collective-permute-start.42 = (bf16[2,256,512]{2,1,0:T(8,128)(2,1)S(1)}, bf16[2,256,512]{2,1,0:T(8,128)(2,1)S(1)}, u32[]{:S(2)}, u32[]{:S(2)}) collective-permute-start(bf16[2,256,512]{2,1,0:T(8,128)(2,1)S(1)} %get-tuple-element.24), channel_id=1, source_target_pairs={{0,8},{24,16},{16,0},{8,24},{1,9},{25,17},{17,1},{9,25},{2,10},{26... | collective-permute-start | bytes 1572872 | tf_op jit(solution)/shard_map/ppermute | solution.py:492
  138.6 8.5 %rest_gradients.1 = (bf16[2,256,512]{2,1,0:T(8,128)(2,1)S(1)}, bf16[2,256,512]{2,1,0:T(8,128)(2,1)S(1)}) custom-call(s32[6,4]{1,0:T(8,128)S(1)} %copy.17.entries, bf16[2,256,4096]{2,1,0:T(8,128)(2,1)S(1)} %get-tuple-element.19.whole, f32[2,256,512]{2,1,0:T(8,128)S(1)} %get-tuple-element.20.begun, bf16[9,512,4096]{2,1,0:T(8,128)(2,1)} %dec.3), custom_call_target="tpu_custom_call" | custom-call | flops 10000000000 | bytes 10485760 | tf_op jit(solution)/shard_map/rest_gradients/pallas_call | solution.py:391
  147.1 1.9 %collective-permute-start.43 = (bf16[2,256,512]{2,1,0:T(8,128)(2,1)S(1)}, bf16[2,256,512]{2,1,0:T(8,128)(2,1)S(1)}, u32[]{:S(2)}, u32[]{:S(2)}) collective-permute-start(bf16[2,256,512]{2,1,0:T(8,128)(2,1)S(1)} %get-tuple-element.21), channel_id=1, source_target_pairs={{0,8},{8,0},{24,16},{1,9},{9,1},{25,17},{2,10},{10,2},{26,18},{3,1... | collective-permute-start | bytes 1572872 | tf_op jit(solution)/shard_map/ppermute | solution.py:497
  149.7 0.8 pad_maximum_fusion
  150.5 0.7 collective-permute-done.42
  151.4 3.5 %collective-permute-start.44 = (bf16[2,256,512]{2,1,0:T(8,128)(2,1)S(1)}, bf16[2,256,512]{2,1,0:T(8,128)(2,1)S(1)}, u32[]{:S(2)}, u32[]{:S(2)}) collective-permute-start(bf16[2,256,512]{2,1,0:T(8,128)(2,1)S(1)} %fusion), channel_id=1, source_target_pairs={{8,16},{16,8},{9,17},{17,9},{10,18},{18,10},{11,19},{19,11},{12,20... | collective-permute-start | bytes 1572872 | tf_op jit(solution)/shard_map/ppermute | solution.py:496
  154.9 5.6 %own_gradients.1 = f32[2,256,512]{2,1,0:T(8,128)S(1)} custom-call(s32[4,4]{1,0:T(4,128)S(1)} %dynamic-slice_bitcast_fusion.entries, bf16[2,256,4096]{2,1,0:T(8,128)(2,1)S(1)} %get-tuple-element.19.whole, bf16[9,512,4096]{2,1,0:T(8,128)(2,1)} %dec.3), custom_call_target="tpu_custom_call" | custom-call | flops 10000000000 | bytes 10485760 | tf_op jit(solution)/shard_map/own_gradients/pallas_call | solution.py:423
  160.7 3.0 %collective-permute-done.43 = bf16[2,256,512]{2,1,0:T(8,128)(2,1)S(1)} collective-permute-done((bf16[2,256,512]{2,1,0:T(8,128)(2,1)S(1)}, bf16[2,256,512]{2,1,0:T(8,128)(2,1)S(1)}, u32[]{:S(2)}, u32[]{:S(2)}) %collective-permute-start.43) | collective-permute-done | bytes 524320 | tf_op jit(solution)/shard_map/ppermute | solution.py:497
  163.7 14.6 %collective-permute-done.44 = bf16[2,256,512]{2,1,0:T(8,128)(2,1)S(1)} collective-permute-done((bf16[2,256,512]{2,1,0:T(8,128)(2,1)S(1)}, bf16[2,256,512]{2,1,0:T(8,128)(2,1)S(1)}, u32[]{:S(2)}, u32[]{:S(2)}) %collective-permute-start.44) | collective-permute-done | bytes 524320 | tf_op jit(solution)/shard_map/ppermute | solution.py:496
  178.3 1.4 add_multiply_fusion
  (84 shorter events, 11.8 us)
Async XLA Ops:
  1.7 9.1 %collective-permute-start.11 = (bf16[256,512]{1,0:T(8,128)(2,1)S(1)}, bf16[256,512]{1,0:T(8,128)(2,1)S(1)}, u32[]{:S(2)}, u32[]{:S(2)}) collective-permute-start(bf16[256,512]{1,0:T(8,128)(2,1)S(1)} %get-tuple-element.26.refs_0_), channel_id=1, source_target_pairs={{0,2},{1,5},{2,0},{3,7},{4,6},{5,1},{6,4},{7,3},{8,10},{9,13},{10,... | collective-permute-start | bytes 786440 | tf_op jit(solution)/shard_map/ppermute | solution.py:441
  2.3 10.6 %collective-permute-start.12 = (bf16[256,512]{1,0:T(8,128)(2,1)S(1)}, bf16[256,512]{1,0:T(8,128)(2,1)S(1)}, u32[]{:S(2)}, u32[]{:S(2)}) collective-permute-start(bf16[256,512]{1,0:T(8,128)(2,1)S(1)} %get-tuple-element.26.refs_0_), channel_id=1, source_target_pairs={{0,4},{1,3},{2,6},{3,1},{4,0},{5,7},{6,2},{7,5},{8,12},{9,11},{10,... | collective-permute-start | bytes 786440 | tf_op jit(solution)/shard_map/ppermute | solution.py:442
  3.8 9.1 %collective-permute-start.14 = (bf16[256,512]{1,0:T(8,128)(2,1)S(1)}, bf16[256,512]{1,0:T(8,128)(2,1)S(1)}, u32[]{:S(2)}, u32[]{:S(2)}) collective-permute-start(bf16[256,512]{1,0:T(8,128)(2,1)S(1)} %get-tuple-element.26.refs_0_), channel_id=1, source_target_pairs={{0,1},{1,0},{2,3},{3,2},{4,5},{5,4},{6,7},{7,6},{8,9},{9,8},{10,11... | collective-permute-start | bytes 786440 | tf_op jit(solution)/shard_map/ppermute | solution.py:445
  3.8 12.6 %collective-permute-start = (bf16[256,512]{1,0:T(8,128)(2,1)S(1)}, bf16[256,512]{1,0:T(8,128)(2,1)S(1)}, u32[]{:S(2)}, u32[]{:S(2)}) collective-permute-start(bf16[256,512]{1,0:T(8,128)(2,1)S(1)} %get-tuple-element.27.refs_0_), channel_id=1, source_target_pairs={{0,2},{1,5},{2,0},{3,7},{4,6},{5,1},{6,4},{7,3},{8,10},{9,13},{10,... | collective-permute-start | bytes 786440 | tf_op jit(solution)/shard_map/ppermute | solution.py:441
  10.8 6.4 %collective-permute-start.13 = (bf16[256,512]{1,0:T(8,128)(2,1)S(1)}, bf16[256,512]{1,0:T(8,128)(2,1)S(1)}, u32[]{:S(2)}, u32[]{:S(2)}) collective-permute-start(bf16[256,512]{1,0:T(8,128)(2,1)S(1)} %collective-permute-done.11.refs_1_), channel_id=1, source_target_pairs={{0,4},{1,3},{2,6},{3,1},{4,0},{5,7},{6,2},{7,5},{8,12},{9,11},{10,... | collective-permute-start | bytes 786440 | tf_op jit(solution)/shard_map/ppermute | solution.py:443
  11.6 8.5 %collective-permute-start.1 = (bf16[256,512]{1,0:T(8,128)(2,1)S(1)}, bf16[256,512]{1,0:T(8,128)(2,1)S(1)}, u32[]{:S(2)}, u32[]{:S(2)}) collective-permute-start(bf16[256,512]{1,0:T(8,128)(2,1)S(1)} %get-tuple-element.27.refs_0_), channel_id=1, source_target_pairs={{0,4},{1,3},{2,6},{3,1},{4,0},{5,7},{6,2},{7,5},{8,12},{9,11},{10,... | collective-permute-start | bytes 786440 | tf_op jit(solution)/shard_map/ppermute | solution.py:442
  12.9 7.2 %collective-permute-start.15 = (bf16[256,512]{1,0:T(8,128)(2,1)S(1)}, bf16[256,512]{1,0:T(8,128)(2,1)S(1)}, u32[]{:S(2)}, u32[]{:S(2)}) collective-permute-start(bf16[256,512]{1,0:T(8,128)(2,1)S(1)} %collective-permute-done.11.refs_1_), channel_id=1, source_target_pairs={{0,1},{1,0},{2,3},{3,2},{4,5},{5,4},{6,7},{7,6},{8,9},{9,8},{10,11... | collective-permute-start | bytes 786440 | tf_op jit(solution)/shard_map/ppermute | solution.py:445
  12.9 7.7 %collective-permute-start.16 = (bf16[256,512]{1,0:T(8,128)(2,1)S(1)}, bf16[256,512]{1,0:T(8,128)(2,1)S(1)}, u32[]{:S(2)}, u32[]{:S(2)}) collective-permute-start(bf16[256,512]{1,0:T(8,128)(2,1)S(1)} %collective-permute-done.12.refs_2_), channel_id=1, source_target_pairs={{0,1},{1,0},{2,3},{3,2},{4,5},{5,4},{6,7},{7,6},{8,9},{9,8},{10,11... | collective-permute-start | bytes 786440 | tf_op jit(solution)/shard_map/ppermute | solution.py:445
  16.5 6.4 %collective-permute-start.2 = (bf16[256,512]{1,0:T(8,128)(2,1)S(1)}, bf16[256,512]{1,0:T(8,128)(2,1)S(1)}, u32[]{:S(2)}, u32[]{:S(2)}) collective-permute-start(bf16[256,512]{1,0:T(8,128)(2,1)S(1)} %collective-permute-done.refs_1_), channel_id=1, source_target_pairs={{0,4},{1,3},{2,6},{3,1},{4,0},{5,7},{6,2},{7,5},{8,12},{9,11},{10,... | collective-permute-start | bytes 786440 | tf_op jit(solution)/shard_map/ppermute | solution.py:443
  17.2 5.6 %collective-permute-start.17 = (bf16[256,512]{1,0:T(8,128)(2,1)S(1)}, bf16[256,512]{1,0:T(8,128)(2,1)S(1)}, u32[]{:S(2)}, u32[]{:S(2)}) collective-permute-start(bf16[256,512]{1,0:T(8,128)(2,1)S(1)} %collective-permute-done.13.refs_3_), channel_id=1, source_target_pairs={{0,1},{1,0},{2,3},{3,2},{4,5},{5,4},{6,7},{7,6},{8,9},{9,8},{10,11... | collective-permute-start | bytes 786440 | tf_op jit(solution)/shard_map/ppermute | solution.py:445
  20.0 8.9 %collective-permute-start.3 = (bf16[256,512]{1,0:T(8,128)(2,1)S(1)}, bf16[256,512]{1,0:T(8,128)(2,1)S(1)}, u32[]{:S(2)}, u32[]{:S(2)}) collective-permute-start(bf16[256,512]{1,0:T(8,128)(2,1)S(1)} %get-tuple-element.27.refs_0_), channel_id=1, source_target_pairs={{0,1},{1,0},{2,3},{3,2},{4,5},{5,4},{6,7},{7,6},{8,9},{9,8},{10,11... | collective-permute-start | bytes 786440 | tf_op jit(solution)/shard_map/ppermute | solution.py:445
  20.0 11.3 %collective-permute-start.4 = (bf16[256,512]{1,0:T(8,128)(2,1)S(1)}, bf16[256,512]{1,0:T(8,128)(2,1)S(1)}, u32[]{:S(2)}, u32[]{:S(2)}) collective-permute-start(bf16[256,512]{1,0:T(8,128)(2,1)S(1)} %collective-permute-done.refs_1_), channel_id=1, source_target_pairs={{0,1},{1,0},{2,3},{3,2},{4,5},{5,4},{6,7},{7,6},{8,9},{9,8},{10,11... | collective-permute-start | bytes 786440 | tf_op jit(solution)/shard_map/ppermute | solution.py:445
  20.5 10.8 %collective-permute-start.5 = (bf16[256,512]{1,0:T(8,128)(2,1)S(1)}, bf16[256,512]{1,0:T(8,128)(2,1)S(1)}, u32[]{:S(2)}, u32[]{:S(2)}) collective-permute-start(bf16[256,512]{1,0:T(8,128)(2,1)S(1)} %collective-permute-done.1.refs_2_), channel_id=1, source_target_pairs={{0,1},{1,0},{2,3},{3,2},{4,5},{5,4},{6,7},{7,6},{8,9},{9,8},{10,11... | collective-permute-start | bytes 786440 | tf_op jit(solution)/shard_map/ppermute | solution.py:445
  22.8 8.5 %collective-permute-start.6 = (bf16[256,512]{1,0:T(8,128)(2,1)S(1)}, bf16[256,512]{1,0:T(8,128)(2,1)S(1)}, u32[]{:S(2)}, u32[]{:S(2)}) collective-permute-start(bf16[256,512]{1,0:T(8,128)(2,1)S(1)} %collective-permute-done.2.refs_3_), channel_id=1, source_target_pairs={{0,1},{1,0},{2,3},{3,2},{4,5},{5,4},{6,7},{7,6},{8,9},{9,8},{10,11... | collective-permute-start | bytes 786440 | tf_op jit(solution)/shard_map/ppermute | solution.py:445
  26.3 17.0 %collective-permute-start.18 = (bf16[256,512]{1,0:T(8,128)(2,1)S(1)}, bf16[256,512]{1,0:T(8,128)(2,1)S(1)}, u32[]{:S(2)}, u32[]{:S(2)}) collective-permute-start(bf16[256,512]{1,0:T(8,128)(2,1)S(1)} %encode.3.refs_1_), channel_id=1, source_target_pairs={{0,16},{16,0},{8,24},{24,8},{1,17},{17,1},{9,25},{25,9},{2,18},{18... | collective-permute-start | bytes 786440 | tf_op jit(solution)/shard_map/ppermute | solution.py:466
  28.9 19.2 %collective-permute-start.20 = (bf16[256,512]{1,0:T(8,128)(2,1)S(1)}, bf16[256,512]{1,0:T(8,128)(2,1)S(1)}, u32[]{:S(2)}, u32[]{:S(2)}) collective-permute-start(bf16[256,512]{1,0:T(8,128)(2,1)S(1)} %encode.3.refs_1_), channel_id=1, source_target_pairs={{0,8},{8,0},{16,24},{1,9},{9,1},{17,25},{2,10},{10,2},{18,26},{3,1... | collective-permute-start | bytes 786440 | tf_op jit(solution)/shard_map/ppermute | solution.py:467
  34.8 17.3 %collective-permute-start.9 = (bf16[256,512]{1,0:T(8,128)(2,1)S(1)}, bf16[256,512]{1,0:T(8,128)(2,1)S(1)}, u32[]{:S(2)}, u32[]{:S(2)}) collective-permute-start(bf16[256,512]{1,0:T(8,128)(2,1)S(1)} %encode.2.refs_0_), channel_id=1, source_target_pairs={{0,16},{16,0},{8,24},{24,8},{1,17},{17,1},{9,25},{25,9},{2,18},{18... | collective-permute-start | bytes 786440 | tf_op jit(solution)/shard_map/ppermute | solution.py:466
  34.8 23.0 %collective-permute-start.21 = (bf16[256,512]{1,0:T(8,128)(2,1)S(1)}, bf16[256,512]{1,0:T(8,128)(2,1)S(1)}, u32[]{:S(2)}, u32[]{:S(2)}) collective-permute-start(bf16[256,512]{1,0:T(8,128)(2,1)S(1)} %encode.3.refs_1_), channel_id=1, source_target_pairs={{8,16},{16,8},{9,17},{17,9},{10,18},{18,10},{11,19},{19,11},{12,20... | collective-permute-start | bytes 786440 | tf_op jit(solution)/shard_map/ppermute | solution.py:468
  41.4 27.6 %collective-permute-start.7 = (bf16[256,512]{1,0:T(8,128)(2,1)S(1)}, bf16[256,512]{1,0:T(8,128)(2,1)S(1)}, u32[]{:S(2)}, u32[]{:S(2)}) collective-permute-start(bf16[256,512]{1,0:T(8,128)(2,1)S(1)} %encode.2.refs_0_), channel_id=1, source_target_pairs={{0,8},{8,0},{16,24},{1,9},{9,1},{17,25},{2,10},{10,2},{18,26},{3,1... | collective-permute-start | bytes 786440 | tf_op jit(solution)/shard_map/ppermute | solution.py:467
  43.3 25.7 %collective-permute-start.8 = (bf16[256,512]{1,0:T(8,128)(2,1)S(1)}, bf16[256,512]{1,0:T(8,128)(2,1)S(1)}, u32[]{:S(2)}, u32[]{:S(2)}) collective-permute-start(bf16[256,512]{1,0:T(8,128)(2,1)S(1)} %encode.2.refs_0_), channel_id=1, source_target_pairs={{8,16},{16,8},{9,17},{17,9},{10,18},{18,10},{11,19},{19,11},{12,20... | collective-permute-start | bytes 786440 | tf_op jit(solution)/shard_map/ppermute | solution.py:468
  48.1 20.9 %collective-permute-start.19 = (bf16[256,512]{1,0:T(8,128)(2,1)S(1)}, bf16[256,512]{1,0:T(8,128)(2,1)S(1)}, u32[]{:S(2)}, u32[]{:S(2)}) collective-permute-start(bf16[256,512]{1,0:T(8,128)(2,1)S(1)} %collective-permute-done.18.refs_4_), channel_id=1, source_target_pairs={{16,24},{8,0},{17,25},{9,1},{18,26},{10,2},{19,27},{11,3},{20,28},... | collective-permute-start | bytes 786440 | tf_op jit(solution)/shard_map/ppermute | solution.py:469
  52.0 16.9 %collective-permute-start.10 = (bf16[256,512]{1,0:T(8,128)(2,1)S(1)}, bf16[256,512]{1,0:T(8,128)(2,1)S(1)}, u32[]{:S(2)}, u32[]{:S(2)}) collective-permute-start(bf16[256,512]{1,0:T(8,128)(2,1)S(1)} %collective-permute-done.9.refs_2_), channel_id=1, source_target_pairs={{16,24},{8,0},{17,25},{9,1},{18,26},{10,2},{19,27},{11,3},{20,28},... | collective-permute-start | bytes 786440 | tf_op jit(solution)/shard_map/ppermute | solution.py:469
  77.0 2.7 %collective-permute-start.22 = (bf16[4,2,128,512]{3,2,1,0:T(8,128)(2,1)S(1)}, bf16[4,2,128,512]{3,2,1,0:T(8,128)(2,1)S(1)}, u32[]{:S(2)}, u32[]{:S(2)}) collective-permute-start(bf16[4,2,128,512]{3,2,1,0:T(8,128)(2,1)S(1)} %get-tuple-element.15), channel_id=1, source_target_pairs={{0,1},{1,0},{2,3},{3,2},{4,5},{5,4},{6,7},{7,6},{8,9},{9,8},{10,11... | collective-permute-start | bytes 3145736 | tf_op jit(solution)/shard_map/ppermute | solution.py:480
  77.1 4.1 %collective-permute-start.32 = (bf16[4,2,128,512]{3,2,1,0:T(8,128)(2,1)S(1)}, bf16[4,2,128,512]{3,2,1,0:T(8,128)(2,1)S(1)}, u32[]{:S(2)}, u32[]{:S(2)}) collective-permute-start(bf16[4,2,128,512]{3,2,1,0:T(8,128)(2,1)S(1)} %get-tuple-element.17), channel_id=1, source_target_pairs={{0,1},{1,0},{2,3},{3,2},{4,5},{5,4},{6,7},{7,6},{8,9},{9,8},{10,11... | collective-permute-start | bytes 3145736 | tf_op jit(solution)/shard_map/ppermute | solution.py:480
  80.1 9.2 %collective-permute-start.23 = (bf16[2,2,128,512]{3,2,1,0:T(8,128)(2,1)S(1)}, bf16[2,2,128,512]{3,2,1,0:T(8,128)(2,1)S(1)}, u32[]{:S(2)}, u32[]{:S(2)}) collective-permute-start(bf16[2,2,128,512]{3,2,1,0:T(8,128)(2,1)S(1)} %slice.115), channel_id=1, source_target_pairs={{0,4},{1,3},{2,6},{3,1},{4,0},{5,7},{6,2},{7,5},{8,12},{9,11},{10,... | collective-permute-start | bytes 1572872 | tf_op jit(solution)/shard_map/ppermute | solution.py:481
  81.7 16.2 %collective-permute-start.33 = (bf16[2,2,128,512]{3,2,1,0:T(8,128)(2,1)S(1)}, bf16[2,2,128,512]{3,2,1,0:T(8,128)(2,1)S(1)}, u32[]{:S(2)}, u32[]{:S(2)}) collective-permute-start(bf16[2,2,128,512]{3,2,1,0:T(8,128)(2,1)S(1)} %slice.114), channel_id=1, source_target_pairs={{0,4},{1,3},{2,6},{3,1},{4,0},{5,7},{6,2},{7,5},{8,12},{9,11},{10,... | collective-permute-start | bytes 1572872 | tf_op jit(solution)/shard_map/ppermute | solution.py:481
  89.5 8.5 %copy-start.1 = (bf16[2,256,512]{2,1,0:T(8,128)(2,1)S(1)}, bf16[2,256,512]{2,1,0:T(8,128)(2,1)}, u32[]{:S(2)}) copy-start(bf16[2,256,512]{2,1,0:T(8,128)(2,1)} %param.18) | copy-start | bytes 1572868
  89.6 8.4 %collective-permute-start.24 = (bf16[2,128,512]{2,1,0:T(8,128)(2,1)S(1)}, bf16[2,128,512]{2,1,0:T(8,128)(2,1)S(1)}, u32[]{:S(2)}, u32[]{:S(2)}) collective-permute-start(bf16[2,128,512]{2,1,0:T(8,128)(2,1)S(1)} %fusion.14), channel_id=1, source_target_pairs={{0,2},{1,5},{2,0},{3,7},{4,6},{5,1},{6,4},{7,3},{8,10},{9,13},{10,... | collective-permute-start | bytes 786440 | tf_op jit(solution)/shard_map/ppermute | solution.py:485
  98.2 9.2 %collective-permute-start.34 = (bf16[2,128,512]{2,1,0:T(8,128)(2,1)S(1)}, bf16[2,128,512]{2,1,0:T(8,128)(2,1)S(1)}, u32[]{:S(2)}, u32[]{:S(2)}) collective-permute-start(bf16[2,128,512]{2,1,0:T(8,128)(2,1)S(1)} %fusion.15), channel_id=1, source_target_pairs={{0,2},{1,5},{2,0},{3,7},{4,6},{5,1},{6,4},{7,3},{8,10},{9,13},{10,... | collective-permute-start | bytes 786440 | tf_op jit(solution)/shard_map/ppermute | solution.py:485
  98.6 14.5 %collective-permute-start.25 = (bf16[2,128,512]{2,1,0:T(8,128)(2,1)S(1)}, bf16[2,128,512]{2,1,0:T(8,128)(2,1)S(1)}, u32[]{:S(2)}, u32[]{:S(2)}) collective-permute-start(bf16[2,128,512]{2,1,0:T(8,128)(2,1)S(1)} %fusion.13.refs_0_), channel_id=1, source_target_pairs={{0,2},{1,5},{2,0},{3,7},{4,6},{5,1},{6,4},{7,3},{8,10},{9,13},{10,... | collective-permute-start | bytes 786440 | tf_op jit(solution)/shard_map/ppermute | solution.py:441
  100.3 13.5 %collective-permute-start.26 = (bf16[2,128,512]{2,1,0:T(8,128)(2,1)S(1)}, bf16[2,128,512]{2,1,0:T(8,128)(2,1)S(1)}, u32[]{:S(2)}, u32[]{:S(2)}) collective-permute-start(bf16[2,128,512]{2,1,0:T(8,128)(2,1)S(1)} %fusion.13.refs_0_), channel_id=1, source_target_pairs={{0,4},{1,3},{2,6},{3,1},{4,0},{5,7},{6,2},{7,5},{8,12},{9,11},{10,... | collective-permute-start | bytes 786440 | tf_op jit(solution)/shard_map/ppermute | solution.py:442
  101.1 12.8 %collective-permute-start.28 = (bf16[2,128,512]{2,1,0:T(8,128)(2,1)S(1)}, bf16[2,128,512]{2,1,0:T(8,128)(2,1)S(1)}, u32[]{:S(2)}, u32[]{:S(2)}) collective-permute-start(bf16[2,128,512]{2,1,0:T(8,128)(2,1)S(1)} %fusion.13.refs_0_), channel_id=1, source_target_pairs={{0,1},{1,0},{2,3},{3,2},{4,5},{5,4},{6,7},{7,6},{8,9},{9,8},{10,11... | collective-permute-start | bytes 786440 | tf_op jit(solution)/shard_map/ppermute | solution.py:445
  107.6 11.1 %collective-permute-start.35 = (bf16[2,128,512]{2,1,0:T(8,128)(2,1)S(1)}, bf16[2,128,512]{2,1,0:T(8,128)(2,1)S(1)}, u32[]{:S(2)}, u32[]{:S(2)}) collective-permute-start(bf16[2,128,512]{2,1,0:T(8,128)(2,1)S(1)} %fusion.7.refs_8_), channel_id=1, source_target_pairs={{0,2},{1,5},{2,0},{3,7},{4,6},{5,1},{6,4},{7,3},{8,10},{9,13},{10,... | collective-permute-start | bytes 786440 | tf_op jit(solution)/shard_map/ppermute | solution.py:441
  108.0 11.4 %collective-permute-start.36 = (bf16[2,128,512]{2,1,0:T(8,128)(2,1)S(1)}, bf16[2,128,512]{2,1,0:T(8,128)(2,1)S(1)}, u32[]{:S(2)}, u32[]{:S(2)}) collective-permute-start(bf16[2,128,512]{2,1,0:T(8,128)(2,1)S(1)} %fusion.7.refs_8_), channel_id=1, source_target_pairs={{0,4},{1,3},{2,6},{3,1},{4,0},{5,7},{6,2},{7,5},{8,12},{9,11},{10,... | collective-permute-start | bytes 786440 | tf_op jit(solution)/shard_map/ppermute | solution.py:442
  113.1 6.4 %collective-permute-start.27 = (bf16[2,128,512]{2,1,0:T(8,128)(2,1)S(1)}, bf16[2,128,512]{2,1,0:T(8,128)(2,1)S(1)}, u32[]{:S(2)}, u32[]{:S(2)}) collective-permute-start(bf16[2,128,512]{2,1,0:T(8,128)(2,1)S(1)} %collective-permute-done.25.refs_1_), channel_id=1, source_target_pairs={{0,4},{1,3},{2,6},{3,1},{4,0},{5,7},{6,2},{7,5},{8,12},{9,11},{10,... | collective-permute-start | bytes 786440 | tf_op jit(solution)/shard_map/ppermute | solution.py:443
  113.8 6.1 %collective-permute-start.38 = (bf16[2,128,512]{2,1,0:T(8,128)(2,1)S(1)}, bf16[2,128,512]{2,1,0:T(8,128)(2,1)S(1)}, u32[]{:S(2)}, u32[]{:S(2)}) collective-permute-start(bf16[2,128,512]{2,1,0:T(8,128)(2,1)S(1)} %fusion.7.refs_8_), channel_id=1, source_target_pairs={{0,1},{1,0},{2,3},{3,2},{4,5},{5,4},{6,7},{7,6},{8,9},{9,8},{10,11... | collective-permute-start | bytes 786440 | tf_op jit(solution)/shard_map/ppermute | solution.py:445
  113.8 6.2 %collective-permute-start.29 = (bf16[2,128,512]{2,1,0:T(8,128)(2,1)S(1)}, bf16[2,128,512]{2,1,0:T(8,128)(2,1)S(1)}, u32[]{:S(2)}, u32[]{:S(2)}) collective-permute-start(bf16[2,128,512]{2,1,0:T(8,128)(2,1)S(1)} %collective-permute-done.25.refs_1_), channel_id=1, source_target_pairs={{0,1},{1,0},{2,3},{3,2},{4,5},{5,4},{6,7},{7,6},{8,9},{9,8},{10,11... | collective-permute-start | bytes 786440 | tf_op jit(solution)/shard_map/ppermute | solution.py:445
  118.7 6.4 %collective-permute-start.37 = (bf16[2,128,512]{2,1,0:T(8,128)(2,1)S(1)}, bf16[2,128,512]{2,1,0:T(8,128)(2,1)S(1)}, u32[]{:S(2)}, u32[]{:S(2)}) collective-permute-start(bf16[2,128,512]{2,1,0:T(8,128)(2,1)S(1)} %collective-permute-done.35.refs_9_), channel_id=1, source_target_pairs={{0,4},{1,3},{2,6},{3,1},{4,0},{5,7},{6,2},{7,5},{8,12},{9,11},{10,... | collective-permute-start | bytes 786440 | tf_op jit(solution)/shard_map/ppermute | solution.py:443
  119.4 7.9 %collective-permute-start.30 = (bf16[2,128,512]{2,1,0:T(8,128)(2,1)S(1)}, bf16[2,128,512]{2,1,0:T(8,128)(2,1)S(1)}, u32[]{:S(2)}, u32[]{:S(2)}) collective-permute-start(bf16[2,128,512]{2,1,0:T(8,128)(2,1)S(1)} %collective-permute-done.26.refs_2_), channel_id=1, source_target_pairs={{0,1},{1,0},{2,3},{3,2},{4,5},{5,4},{6,7},{7,6},{8,9},{9,8},{10,11... | collective-permute-start | bytes 786440 | tf_op jit(solution)/shard_map/ppermute | solution.py:445
  119.5 7.9 %collective-permute-start.39 = (bf16[2,128,512]{2,1,0:T(8,128)(2,1)S(1)}, bf16[2,128,512]{2,1,0:T(8,128)(2,1)S(1)}, u32[]{:S(2)}, u32[]{:S(2)}) collective-permute-start(bf16[2,128,512]{2,1,0:T(8,128)(2,1)S(1)} %collective-permute-done.35.refs_9_), channel_id=1, source_target_pairs={{0,1},{1,0},{2,3},{3,2},{4,5},{5,4},{6,7},{7,6},{8,9},{9,8},{10,11... | collective-permute-start | bytes 786440 | tf_op jit(solution)/shard_map/ppermute | solution.py:445
  120.0 7.4 %collective-permute-start.40 = (bf16[2,128,512]{2,1,0:T(8,128)(2,1)S(1)}, bf16[2,128,512]{2,1,0:T(8,128)(2,1)}, u32[]{:S(2)}, u32[]{:S(2)}) collective-permute-start(bf16[2,128,512]{2,1,0:T(8,128)(2,1)S(1)} %collective-permute-done.36.refs_10_), channel_id=1, source_target_pairs={{0,1},{1,0},{2,3},{3,2},{4,5},{5,4},{6,7},{7,6},{8,9},{9,8},{10,11... | collective-permute-start | bytes 786440 | tf_op jit(solution)/shard_map/ppermute | solution.py:445
  120.0 7.3 %collective-permute-start.31 = (bf16[2,128,512]{2,1,0:T(8,128)(2,1)S(1)}, bf16[2,128,512]{2,1,0:T(8,128)(2,1)}, u32[]{:S(2)}, u32[]{:S(2)}) collective-permute-start(bf16[2,128,512]{2,1,0:T(8,128)(2,1)S(1)} %collective-permute-done.27.refs_3_), channel_id=1, source_target_pairs={{0,1},{1,0},{2,3},{3,2},{4,5},{5,4},{6,7},{7,6},{8,9},{9,8},{10,11... | collective-permute-start | bytes 786440 | tf_op jit(solution)/shard_map/ppermute | solution.py:445
  125.1 2.3 %collective-permute-start.41 = (bf16[2,128,512]{2,1,0:T(8,128)(2,1)S(1)}, bf16[2,128,512]{2,1,0:T(8,128)(2,1)}, u32[]{:S(2)}, u32[]{:S(2)}) collective-permute-start(bf16[2,128,512]{2,1,0:T(8,128)(2,1)S(1)} %collective-permute-done.37.refs_11_), channel_id=1, source_target_pairs={{0,1},{1,0},{2,3},{3,2},{4,5},{5,4},{6,7},{7,6},{8,9},{9,8},{10,11... | collective-permute-start | bytes 786440 | tf_op jit(solution)/shard_map/ppermute | solution.py:445
  134.8 16.5 %collective-permute-start.42 = (bf16[2,256,512]{2,1,0:T(8,128)(2,1)S(1)}, bf16[2,256,512]{2,1,0:T(8,128)(2,1)S(1)}, u32[]{:S(2)}, u32[]{:S(2)}) collective-permute-start(bf16[2,256,512]{2,1,0:T(8,128)(2,1)S(1)} %get-tuple-element.24), channel_id=1, source_target_pairs={{0,8},{24,16},{16,0},{8,24},{1,9},{25,17},{17,1},{9,25},{2,10},{26... | collective-permute-start | bytes 1572872 | tf_op jit(solution)/shard_map/ppermute | solution.py:492
  147.1 16.7 %collective-permute-start.43 = (bf16[2,256,512]{2,1,0:T(8,128)(2,1)S(1)}, bf16[2,256,512]{2,1,0:T(8,128)(2,1)S(1)}, u32[]{:S(2)}, u32[]{:S(2)}) collective-permute-start(bf16[2,256,512]{2,1,0:T(8,128)(2,1)S(1)} %get-tuple-element.21), channel_id=1, source_target_pairs={{0,8},{8,0},{24,16},{1,9},{9,1},{25,17},{2,10},{10,2},{26,18},{3,1... | collective-permute-start | bytes 1572872 | tf_op jit(solution)/shard_map/ppermute | solution.py:497
  149.0 14.7 %collective-permute-start.45 = (bf16[2,256,512]{2,1,0:T(8,128)(2,1)S(1)}, bf16[2,256,512]{2,1,0:T(8,128)(2,1)S(1)}, u32[]{:S(2)}, u32[]{:S(2)}) collective-permute-start(bf16[2,256,512]{2,1,0:T(8,128)(2,1)S(1)} %get-tuple-element.23), channel_id=1, source_target_pairs={{0,24},{24,0},{1,25},{25,1},{2,26},{26,2},{3,27},{27,3},{4,28},{28... | collective-permute-start | bytes 1572872 | tf_op jit(solution)/shard_map/ppermute | solution.py:494
  151.4 26.9 %collective-permute-start.44 = (bf16[2,256,512]{2,1,0:T(8,128)(2,1)S(1)}, bf16[2,256,512]{2,1,0:T(8,128)(2,1)S(1)}, u32[]{:S(2)}, u32[]{:S(2)}) collective-permute-start(bf16[2,256,512]{2,1,0:T(8,128)(2,1)S(1)} %fusion), channel_id=1, source_target_pairs={{8,16},{16,8},{9,17},{17,9},{10,18},{18,10},{11,19},{19,11},{12,20... | collective-permute-start | bytes 1572872 | tf_op jit(solution)/shard_map/ppermute | solution.py:496
  160.6 17.7 %copy-start = (s32[2,256,512]{2,1,0:T(8,128)S(1)}, s32[2,256,512]{2,1,0:T(8,128)}, u32[]{:S(2)}) copy-start(s32[2,256,512]{2,1,0:T(8,128)} %refs_10_.3) | copy-start | bytes 3145732
  (1 other events, 8.4 us)

commit v4 on v3

--- a/solution.py
+++ b/solution.py
@@ -275,45 +275,44 @@
 
 
 def late_kernel(entries, cols, *refs):
-    *sources, before, dec, keep0, send0, keep1, send1, held, acc, earlier, hsems, ring, sems = refs
-    copies = bring([*sources, before], [held.at[i] for i in range(len(sources))] + [earlier], hsems)
+    *sources, before, dec = refs[:-13]
+    outs, (held, acc, hsems, ring, sems) = refs[-13:-5], refs[-5:]
+    copies = bring(sources, [held.at[i] for i in range(len(sources))], hsems)
     open_stream(entries, dec, ring, sems)
     acc[...] = jnp.zeros_like(acc)
-    tokens, width = keep0.shape[2:]
-    for copy in copies[:-1]:
+    tokens, width = outs[0].shape[2:]
+    for copy in copies:
         copy.wait()
 
     def use(e, block):
         add_pair(acc, entries[e, 2], held[entries[e, 1]], block)
 
     run_stream(entries, dec, ring, sems, use)
-    copies[-1].wait()
-    for c, (keep, send) in enumerate(((keep0, send0), (keep1, send1))):
+    for c in range(CHUNKS):
         rows = slice(c * tokens, (c + 1) * tokens)
         for i in range(8):
             place = pl.ds(pl.multiple_of(cols[i] * width, width), width)
-            out = keep if i < 4 else send
+            out = outs[4 * c + i // 2]
             for s in range(2):
-                value = acc[s, rows, place] + earlier[s, rows, place].astype(jnp.float32)
-                out[i % 4, s] = value.astype(jnp.bfloat16)
+                value = acc[s, rows, place] + before[s, rows, place].astype(jnp.float32)
+                out[i % 2, s] = value.astype(jnp.bfloat16)
 
 
 def reconstruct_late(entries, cols, sources, before, dec):
     tokens, feats = sources[0].shape
     depth = dec.shape[2]
-    out = jax.ShapeDtypeStruct((4, 2, tokens // CHUNKS, depth // 8), jnp.bfloat16)
+    out = jax.ShapeDtypeStruct((2, 2, tokens // CHUNKS, depth // 8), jnp.bfloat16)
     return pl.pallas_call(
         late_kernel,
-        in_specs=[SMEM] * 2 + [HBM] * len(sources) + [HBM, HBM],
-        out_specs=[VMEM] * 4,
+        in_specs=[SMEM] * 2 + [HBM] * len(sources) + [VMEM, HBM],
+        out_specs=[VMEM] * 8,
         scratch_shapes=[
             pltpu.VMEM((len(sources), tokens, feats), jnp.bfloat16),
             pltpu.VMEM((2, tokens, depth), jnp.float32),
-            pltpu.VMEM((2, tokens, depth), jnp.bfloat16),
-            pltpu.SemaphoreType.DMA((len(sources) + 1,)),
+            pltpu.SemaphoreType.DMA((len(sources),)),
         ]
         + stream_scratch(dec),
-        out_shape=[out] * 4,
+        out_shape=[out] * 8,
         compiler_params=pltpu.CompilerParams(vmem_limit_bytes=LIMIT),
         cost_estimate=cost(10),
         name="reconstruct_late",
@@ -369,34 +368,26 @@
     )(entries, cols, *blocks, dec)
 
 
-def rest_kernel(entries, whole, begun, dec, one, three, error, total, esem, tsem, ring, sems):
-    copy = pltpu.make_async_copy(whole, error, esem)
-    copy.start()
-    more = pltpu.make_async_copy(begun, total.at[2:4], tsem)
-    more.start()
+def rest_kernel(entries, whole, begun, dec, one, three, total, ring, sems):
     open_stream(entries, dec, ring, sems)
     total[0:2] = jnp.zeros_like(total[0:2])
-    copy.wait()
-    more.wait()
+    total[2:4] = begun[...]
     run_stream(
-        entries, dec, ring, sems, lambda e, block: add_term(entries, e, error, total, block)
+        entries, dec, ring, sems, lambda e, block: add_term(entries, e, whole, total, block)
     )
     one[...] = total[:2].astype(one.dtype)
     three[...] = total[2:].astype(three.dtype)
 
 
 def rest_gradients(entries, whole, begun, dec):
-    _, tokens, depth = whole.shape
+    tokens = whole.shape[1]
     feats = dec.shape[1]
     return pl.pallas_call(
         rest_kernel,
-        in_specs=[SMEM, HBM, HBM, HBM],
+        in_specs=[SMEM, VMEM, VMEM, HBM],
         out_specs=[VMEM] * 2,
         scratch_shapes=[
-            pltpu.VMEM((2, tokens, depth), jnp.bfloat16),
             pltpu.VMEM((4, tokens, feats), jnp.float32),
-            pltpu.SemaphoreType.DMA(()),
-            pltpu.SemaphoreType.DMA(()),
         ]
         + stream_scratch(dec),
         out_shape=[jax.ShapeDtypeStruct((2, tokens, feats), jnp.bfloat16)] * 2,
@@ -406,26 +397,22 @@
     )(entries, whole, begun, dec)
 
 
-def own_kernel(entries, whole, dec, total, error, esem, ring, sems):
-    copy = pltpu.make_async_copy(whole, error, esem)
-    copy.start()
+def own_kernel(entries, whole, dec, total, ring, sems):
     open_stream(entries, dec, ring, sems)
     total[...] = jnp.zeros_like(total)
-    copy.wait()
     run_stream(
-        entries, dec, ring, sems, lambda e, block: add_term(entries, e, error, total, block)
+        entries, dec, ring, sems, lambda e, block: add_term(entries, e, whole, total, block)
     )
 
 
 def own_gradients(entries, whole, dec):
-    _, tokens, depth = whole.shape
+    tokens = whole.shape[1]
     feats = dec.shape[1]
     return pl.pallas_call(
         own_kernel,
-        in_specs=[SMEM, HBM, HBM],
+        in_specs=[SMEM, VMEM, HBM],
         out_specs=VMEM,
-        scratch_shapes=[pltpu.VMEM((2, tokens, depth), jnp.bfloat16), pltpu.SemaphoreType.DMA(())]
-        + stream_scratch(dec),
+        scratch_shapes=stream_scratch(dec),
         out_shape=jax.ShapeDtypeStruct((2, tokens, feats), jnp.float32),
         compiler_params=pltpu.CompilerParams(vmem_limit_bytes=LIMIT),
         cost_estimate=cost(10),
@@ -460,9 +447,10 @@
     enc, enc_bias, masks = (
         pltpu.with_memory_space_constraint(x, pltpu.HBM) for x in (enc, enc_bias, fire)
     )
+    slabs = (resid[0], lax.optimization_barrier(resid)[1])
     ways = []
     for layer in range(2):
-        acts = encode(columns, gather(resid[layer]), enc, enc_bias, masks, layer)
+        acts = encode(columns, gather(slabs[layer]), enc, enc_bias, masks, layer)
         two_away = lax.ppermute(acts, "layer", TWO)
         nearest = lax.ppermute(acts, "layer", ONE)
         middle = lax.ppermute(acts, "layer", MIDDLE)
@@ -476,14 +464,17 @@
     errors, blocks = [], []
     for c in range(CHUNKS):
         span = slice(c * tokens, (c + 1) * tokens)
-        keep, send = halves[2 * c : 2 * c + 2]
-        pair = keep.astype(f32) + lax.ppermute(send, "feat", FLIP).astype(f32)
-        far = lax.ppermute(pair[2:].astype(bf16), "feat", SECOND).astype(f32)
+        keep_near, keep_far, send_near, send_far = halves[4 * c : 4 * c + 4]
+        far = keep_far.astype(f32) + lax.ppermute(send_far, "feat", FLIP).astype(f32)
+        far = lax.ppermute(far.astype(bf16), "feat", SECOND).astype(f32)
+        pair = keep_near.astype(f32) + lax.ppermute(send_near, "feat", FLIP).astype(f32)
         close = (pair[1] + far[1]).astype(bf16)
         if errors:
             close = after(close, errors[0])
         close = lax.ppermute(close, "feat", FIRST).astype(f32)
         recon = pair[0] + far[0] + close
+        if errors:
+            recon = after(recon, errors[0])
         error = recon + dec_bias.astype(f32)[:, None, :] - target[:, span].astype(f32)
         errors.append(error.astype(bf16))
         blocks += gather(errors[c])

time: 180 us -> 176 us (0.978)
  waiting for transfers between devices: 72.8 us -> 67.9 us
    ppermute x4, waiting for transfers between devices: 17.2 us -> 13.6 us  [gather(): first = lax.ppermute(own, 'feat', FIRST)]
    ppermute x4 -> x6, waiting for transfers between devices: 17 us -> 15.4 us  [the longest x2 14.5 us: on_device(): far = lax.ppermute(far.astype(bf16), 'feat', SECOND).astype(f32)]
  transfers between devices with their start and end apart: 46 -> 48, of which waited for: 18 -> 18; matrix products, arithmetic and copies ran while one was open for 4% -> 4% of each run, Pallas kernels for 18% -> 18%
where the time goes in v4:
time: 176 us; the launch traced here: 175 us
  waiting for transfers between devices  67.9 us (39%)
  starting transfers between devices  50.2 us (29%)
  Pallas kernels  46.6 us (26%)
  local copies, waits for them, and re-layouts  5.84 us (3%)
  other arithmetic  3.95 us (2%)
    ppermute x1, waiting for transfers between devices, on_device(): middle = lax.ppermute(across, 'layer', MIDDLE)  15.1 us
    ppermute x2, waiting for transfers between devices, on_device(): far = lax.ppermute(far.astype(bf16), 'feat', SECOND).astype(f32)  14.5 us
    ppermute x4, waiting for transfers between devices, gather(): first = lax.ppermute(own, 'feat', FIRST)  13.6 us
    pallas_call x1, Pallas kernels, reconstruct_early(): pl.pallas_call(early_kernel, in_specs=[SMEM] + [HBM] * len(sources) + [HB...  11 us
    ppermute x2, starting transfers between devices, on_device(): middle = lax.ppermute(acts, 'layer', MIDDLE)  9.74 us
    pallas_call x1, Pallas kernels, rest_gradients(): pl.pallas_call(rest_kernel, in_specs=[SMEM, VMEM, VMEM, HBM], out_specs=[...  8.1 us
    pallas_call x1, Pallas kernels, reconstruct_late(): pl.pallas_call(late_kernel, in_specs=[SMEM] * 2 + [HBM] * len(sources) +...  7.76 us
    ppermute x4, waiting for transfers between devices, gather(): both = lax.ppermute(first, 'feat', SECOND)  7.6 us
  transfers between devices with their start and end apart: 48, of which 18 were waited for; matrix products, arithmetic and copies ran while one was open for 4% of the time, Pallas kernels for 18%

profile of v4, /device:TPU:10, one launch (start us, length us, event | category | flops | bytes accessed | tf_op | source)
XLA Modules:
  0.0 175.5 jit_solution(15605980255919364754)
XLA Ops:
  0.6 1.0 slice_bitcast_fusion.1.refs_0_
  2.2 1.5 collective-permute-start.12
  3.7 1.0 slice_bitcast_fusion.refs_0_
  4.7 1.6 collective-permute-start
  6.3 4.5 %collective-permute-done.11.refs_1_ = bf16[256,512]{1,0:T(8,128)(2,1)S(1)} collective-permute-done((bf16[256,512]{1,0:T(8,128)(2,1)S(1)}, bf16[256,512]{1,0:T(8,128)(2,1)S(1)}, u32[]{:S(2)}, u32[]{:S(2)}) %collective-permute-start.11) | collective-permute-done | bytes 262176 | tf_op jit(solution)/shard_map/ppermute | solution.py:428
  10.7 0.7 collective-permute-start.13
  11.5 1.3 collective-permute-start.1
  13.3 3.1 %collective-permute-done.refs_1_ = bf16[256,512]{1,0:T(8,128)(2,1)S(1)} collective-permute-done((bf16[256,512]{1,0:T(8,128)(2,1)S(1)}, bf16[256,512]{1,0:T(8,128)(2,1)S(1)}, u32[]{:S(2)}, u32[]{:S(2)}) %collective-permute-start) | collective-permute-done | bytes 262176 | tf_op jit(solution)/shard_map/ppermute | solution.py:428
  16.4 0.8 collective-permute-done.13.refs_3_
  17.2 2.7 %collective-permute-done.1.refs_2_ = bf16[256,512]{1,0:T(8,128)(2,1)S(1)} collective-permute-done((bf16[256,512]{1,0:T(8,128)(2,1)S(1)}, bf16[256,512]{1,0:T(8,128)(2,1)S(1)}, u32[]{:S(2)}, u32[]{:S(2)}) %collective-permute-start.1) | collective-permute-done | bytes 262176 | tf_op jit(solution)/shard_map/ppermute | solution.py:429
  20.5 2.2 %collective-permute-done.2.refs_3_ = bf16[256,512]{1,0:T(8,128)(2,1)S(1)} collective-permute-done((bf16[256,512]{1,0:T(8,128)(2,1)S(1)}, bf16[256,512]{1,0:T(8,128)(2,1)S(1)}, u32[]{:S(2)}, u32[]{:S(2)}) %collective-permute-start.2) | collective-permute-done | bytes 262176 | tf_op jit(solution)/shard_map/ppermute | solution.py:430
  22.7 3.4 %encode.3.refs_1_ = bf16[256,512]{1,0:T(8,128)(2,1)S(1)} custom-call(s32[8]{0:T(128)S(1)} %broadcast_xor_fusion.order.cols, bf16[256,512]{1,0:T(8,128)(2,1)S(1)} %slice_bitcast_fusion.1.refs_0_, bf16[256,512]{1,0:T(8,128)(2,1)S(1)} %collective-permute-done.11.refs_1_, bf16[256,512]{1,0:T(8,128)(2,1)S(1)} %collective-permute-done.12.refs_2_, ...), custom_call_target="tpu_custom_call" | custom-call | flops 1000000000 | bytes 1048576 | tf_op jit(solution)/shard_map/encode/pallas_call | solution.py:176
  26.2 2.7 %collective-permute-start.18 = (bf16[256,512]{1,0:T(8,128)(2,1)S(1)}, bf16[256,512]{1,0:T(8,128)(2,1)S(1)}, u32[]{:S(2)}, u32[]{:S(2)}) collective-permute-start(bf16[256,512]{1,0:T(8,128)(2,1)S(1)} %encode.3.refs_1_), channel_id=1, source_target_pairs={{0,16},{16,0},{8,24},{24,8},{1,17},{17,1},{9,25},{25,9},{2,18},{18... | collective-permute-start | bytes 786440 | tf_op jit(solution)/shard_map/ppermute | solution.py:454
  28.8 2.3 %collective-permute-start.20 = (bf16[256,512]{1,0:T(8,128)(2,1)S(1)}, bf16[256,512]{1,0:T(8,128)(2,1)S(1)}, u32[]{:S(2)}, u32[]{:S(2)}) collective-permute-start(bf16[256,512]{1,0:T(8,128)(2,1)S(1)} %encode.3.refs_1_), channel_id=1, source_target_pairs={{0,8},{8,0},{16,24},{1,9},{9,1},{17,25},{2,10},{10,2},{18,26},{3,1... | collective-permute-start | bytes 786440 | tf_op jit(solution)/shard_map/ppermute | solution.py:455
  31.2 3.4 %encode.2.refs_0_ = bf16[256,512]{1,0:T(8,128)(2,1)S(1)} custom-call(s32[8]{0:T(128)S(1)} %broadcast_xor_fusion.order.cols, bf16[256,512]{1,0:T(8,128)(2,1)S(1)} %slice_bitcast_fusion.refs_0_, bf16[256,512]{1,0:T(8,128)(2,1)S(1)} %collective-permute-done.refs_1_, bf16[256,512]{1,0:T(8,128)(2,1)S(1)} %collective-permute-done.1.refs_2_, ...), custom_call_target="tpu_custom_call" | custom-call | flops 1000000000 | bytes 1048576 | tf_op jit(solution)/shard_map/encode/pallas_call | solution.py:176
  34.8 4.9 %collective-permute-start.21 = (bf16[256,512]{1,0:T(8,128)(2,1)S(1)}, bf16[256,512]{1,0:T(8,128)(2,1)S(1)}, u32[]{:S(2)}, u32[]{:S(2)}) collective-permute-start(bf16[256,512]{1,0:T(8,128)(2,1)S(1)} %encode.3.refs_1_), channel_id=1, source_target_pairs={{8,16},{16,8},{9,17},{17,9},{10,18},{18,10},{11,19},{19,11},{12,20... | collective-permute-start | bytes 786440 | tf_op jit(solution)/shard_map/ppermute | solution.py:456
  41.3 1.9 %collective-permute-start.7 = (bf16[256,512]{1,0:T(8,128)(2,1)S(1)}, bf16[256,512]{1,0:T(8,128)(2,1)S(1)}, u32[]{:S(2)}, u32[]{:S(2)}) collective-permute-start(bf16[256,512]{1,0:T(8,128)(2,1)S(1)} %encode.2.refs_0_), channel_id=1, source_target_pairs={{0,8},{8,0},{16,24},{1,9},{9,1},{17,25},{2,10},{10,2},{18,26},{3,1... | collective-permute-start | bytes 786440 | tf_op jit(solution)/shard_map/ppermute | solution.py:455
  43.2 4.8 %collective-permute-start.8 = (bf16[256,512]{1,0:T(8,128)(2,1)S(1)}, bf16[256,512]{1,0:T(8,128)(2,1)S(1)}, u32[]{:S(2)}, u32[]{:S(2)}) collective-permute-start(bf16[256,512]{1,0:T(8,128)(2,1)S(1)} %encode.2.refs_0_), channel_id=1, source_target_pairs={{8,16},{16,8},{9,17},{17,9},{10,18},{18,10},{11,19},{19,11},{12,20... | collective-permute-start | bytes 786440 | tf_op jit(solution)/shard_map/ppermute | solution.py:456
  48.0 2.7 %collective-permute-start.19 = (bf16[256,512]{1,0:T(8,128)(2,1)S(1)}, bf16[256,512]{1,0:T(8,128)(2,1)S(1)}, u32[]{:S(2)}, u32[]{:S(2)}) collective-permute-start(bf16[256,512]{1,0:T(8,128)(2,1)S(1)} %collective-permute-done.18.refs_4_), channel_id=1, source_target_pairs={{16,24},{8,0},{17,25},{9,1},{18,26},{10,2},{19,27},{11,3},{20,28},... | collective-permute-start | bytes 786440 | tf_op jit(solution)/shard_map/ppermute | solution.py:457
  50.7 1.2 collective-permute-done.9.refs_2_
  51.9 3.6 %collective-permute-start.10 = (bf16[256,512]{1,0:T(8,128)(2,1)S(1)}, bf16[256,512]{1,0:T(8,128)(2,1)S(1)}, u32[]{:S(2)}, u32[]{:S(2)}) collective-permute-start(bf16[256,512]{1,0:T(8,128)(2,1)S(1)} %collective-permute-done.9.refs_2_), channel_id=1, source_target_pairs={{16,24},{8,0},{17,25},{9,1},{18,26},{10,2},{19,27},{11,3},{20,28},... | collective-permute-start | bytes 786440 | tf_op jit(solution)/shard_map/ppermute | solution.py:457
  55.6 2.2 %collective-permute-done.21.refs_3_ = bf16[256,512]{1,0:T(8,128)(2,1)S(1)} collective-permute-done((bf16[256,512]{1,0:T(8,128)(2,1)S(1)}, bf16[256,512]{1,0:T(8,128)(2,1)S(1)}, u32[]{:S(2)}, u32[]{:S(2)}) %collective-permute-start.21) | collective-permute-done | bytes 262176 | tf_op jit(solution)/shard_map/ppermute | solution.py:456
  57.8 11.0 %reconstruct_early.1.refs_5_ = bf16[2,256,4096]{2,1,0:T(8,128)(2,1)S(1)} custom-call(s32[7,4]{1,0:T(8,128)S(1)} %copy.14.entries, bf16[256,512]{1,0:T(8,128)(2,1)S(1)} %encode.2.refs_0_, bf16[256,512]{1,0:T(8,128)(2,1)S(1)} %encode.3.refs_1_, bf16[256,512]{1,0:T(8,128)(2,1)S(1)} %collective-permute-done.20.refs_2_, ...), custom_call_target="tpu_custom_call" | custom-call | flops 10000000000 | bytes 10485760 | tf_op jit(solution)/shard_map/reconstruct_early/pallas_call | solution.py:260
  68.9 7.8 %reconstruct_late.1 = (bf16[2,2,128,512]{3,2,1,0:T(8,128)(2,1)S(1)}, bf16[2,2,128,512]{3,2,1,0:T(8,128)(2,1)S(1)}, bf16[2,2,128,512]{3,2,1,0:T(8,128)(2,1)S(1)},...) custom-call(s32[7,4]{1,0:T(8,128)S(1)} %copy.15.entries, ...), custom_call_target="tpu_custom_call" | custom-call | flops 10000000000 | bytes 10485760 | tf_op jit(solution)/shard_map/reconstruct_late/pallas_call | solution.py:305
  77.8 0.9 collective-permute-done.23
  78.8 0.8 collective-permute-start.24
  79.7 1.4 collective-permute-start.35
  81.3 6.8 %collective-permute-done.24 = bf16[2,2,128,512]{3,2,1,0:T(8,128)(2,1)S(1)} collective-permute-done((bf16[2,2,128,512]{3,2,1,0:T(8,128)(2,1)S(1)}, bf16[2,2,128,512]{3,2,1,0:T(8,128)(2,1)S(1)}, u32[]{:S(2)}, u32[]{:S(2)}) %collective-permute-start.24) | collective-permute-done | bytes 524320 | tf_op jit(solution)/shard_map/ppermute | solution.py:469
  88.8 7.7 %collective-permute-done.35 = bf16[2,2,128,512]{3,2,1,0:T(8,128)(2,1)S(1)} collective-permute-done((bf16[2,2,128,512]{3,2,1,0:T(8,128)(2,1)S(1)}, bf16[2,2,128,512]{3,2,1,0:T(8,128)(2,1)S(1)}, u32[]{:S(2)}, u32[]{:S(2)}) %collective-permute-start.35) | collective-permute-done | bytes 524320 | tf_op jit(solution)/shard_map/ppermute | solution.py:469
  97.2 1.7 collective-permute-start.26
  99.7 6.4 %collective-permute-done.36 = bf16[2,128,512]{2,1,0:T(8,128)(2,1)S(1)} collective-permute-done((bf16[2,128,512]{2,1,0:T(8,128)(2,1)S(1)}, bf16[2,128,512]{2,1,0:T(8,128)(2,1)S(1)}, u32[]{:S(2)}, u32[]{:S(2)}) %collective-permute-start.36) | collective-permute-done | bytes 262176 | tf_op jit(solution)/shard_map/ppermute | solution.py:474
  106.7 0.8 collective-permute-start.38
  107.5 4.0 %collective-permute-done.26.refs_1_ = bf16[2,128,512]{2,1,0:T(8,128)(2,1)S(1)} collective-permute-done((bf16[2,128,512]{2,1,0:T(8,128)(2,1)S(1)}, bf16[2,128,512]{2,1,0:T(8,128)(2,1)S(1)}, u32[]{:S(2)}, u32[]{:S(2)}) %collective-permute-start.26) | collective-permute-done | bytes 262176 | tf_op jit(solution)/shard_map/ppermute | solution.py:428
  111.6 0.7 collective-permute-start.28
  112.3 2.1 %collective-permute-done.37.refs_9_ = bf16[2,128,512]{2,1,0:T(8,128)(2,1)S(1)} collective-permute-done((bf16[2,128,512]{2,1,0:T(8,128)(2,1)S(1)}, bf16[2,128,512]{2,1,0:T(8,128)(2,1)S(1)}, u32[]{:S(2)}, u32[]{:S(2)}) %collective-permute-start.37) | collective-permute-done | bytes 262176 | tf_op jit(solution)/shard_map/ppermute | solution.py:428
  115.6 2.3 %collective-permute-done.28.refs_3_ = bf16[2,128,512]{2,1,0:T(8,128)(2,1)S(1)} collective-permute-done((bf16[2,128,512]{2,1,0:T(8,128)(2,1)S(1)}, bf16[2,128,512]{2,1,0:T(8,128)(2,1)S(1)}, u32[]{:S(2)}, u32[]{:S(2)}) %collective-permute-start.28) | collective-permute-done | bytes 262176 | tf_op jit(solution)/shard_map/ppermute | solution.py:430
  118.4 2.3 %collective-permute-done.39.refs_11_ = bf16[2,128,512]{2,1,0:T(8,128)(2,1)S(1)} collective-permute-done((bf16[2,128,512]{2,1,0:T(8,128)(2,1)S(1)}, bf16[2,128,512]{2,1,0:T(8,128)(2,1)S(1)}, u32[]{:S(2)}, u32[]{:S(2)}) %collective-permute-start.39) | collective-permute-done | bytes 262176 | tf_op jit(solution)/shard_map/ppermute | solution.py:430
  123.0 7.4 %first_gradients.1 = (bf16[2,256,512]{2,1,0:T(8,128)(2,1)S(1)}, f32[2,256,512]{2,1,0:T(8,128)S(1)}, bf16[2,256,4096]{2,1,0:T(8,128)(2,1)S(1)}) custom-call(s32[5,4]{1,0:T(8,128)S(1)} %copy.16.entries, s32[8]{0:T(128)S(1)} %broadcast_xor_fusion.order.cols, bf16[2,128,512]{2,1,0:T(8,128)(2,1)S(1)} %fusion.10.refs_0_, ...), custom_call_target="tpu_custom_call" | custom-call | flops 10000000000 | bytes 10485760 | tf_op jit(solution)/shard_map/first_gradients/pallas_call | solution.py:351
  130.4 3.8 %collective-permute-start.44 = (bf16[2,256,512]{2,1,0:T(8,128)(2,1)S(1)}, bf16[2,256,512]{2,1,0:T(8,128)(2,1)S(1)}, u32[]{:S(2)}, u32[]{:S(2)}) collective-permute-start(bf16[2,256,512]{2,1,0:T(8,128)(2,1)S(1)} %get-tuple-element.34), channel_id=1, source_target_pairs={{0,8},{24,16},{16,0},{8,24},{1,9},{25,17},{17,1},{9,25},{2,10},{26... | collective-permute-start | bytes 1572872 | tf_op jit(solution)/shard_map/ppermute | solution.py:483
  134.2 8.1 %rest_gradients.1 = (bf16[2,256,512]{2,1,0:T(8,128)(2,1)S(1)}, bf16[2,256,512]{2,1,0:T(8,128)(2,1)S(1)}) custom-call(s32[6,4]{1,0:T(8,128)S(1)} %copy.17.entries, bf16[2,256,4096]{2,1,0:T(8,128)(2,1)S(1)} %get-tuple-element.29.whole, f32[2,256,512]{2,1,0:T(8,128)S(1)} %get-tuple-element.30.begun, bf16[9,512,4096]{2,1,0:T(8,128)(2,1)} %dec.3), custom_call_target="tpu_custom_call" | custom-call | flops 10000000000 | bytes 10485760 | tf_op jit(solution)/shard_map/rest_gradients/pallas_call | solution.py:385
  142.3 1.9 %collective-permute-start.45 = (bf16[2,256,512]{2,1,0:T(8,128)(2,1)S(1)}, bf16[2,256,512]{2,1,0:T(8,128)(2,1)S(1)}, u32[]{:S(2)}, u32[]{:S(2)}) collective-permute-start(bf16[2,256,512]{2,1,0:T(8,128)(2,1)S(1)} %get-tuple-element.31), channel_id=1, source_target_pairs={{0,8},{8,0},{24,16},{1,9},{9,1},{25,17},{2,10},{10,2},{26,18},{3,1... | collective-permute-start | bytes 1572872 | tf_op jit(solution)/shard_map/ppermute | solution.py:488
  145.0 0.8 pad_maximum_fusion
  145.8 1.1 collective-permute-done.44
  147.0 3.9 %collective-permute-start.46 = (bf16[2,256,512]{2,1,0:T(8,128)(2,1)S(1)}, bf16[2,256,512]{2,1,0:T(8,128)(2,1)S(1)}, u32[]{:S(2)}, u32[]{:S(2)}) collective-permute-start(bf16[2,256,512]{2,1,0:T(8,128)(2,1)S(1)} %fusion), channel_id=1, source_target_pairs={{8,16},{16,8},{9,17},{17,9},{10,18},{18,10},{11,19},{19,11},{12,20... | collective-permute-start | bytes 1572872 | tf_op jit(solution)/shard_map/ppermute | solution.py:487
  151.0 5.4 %own_gradients.1 = f32[2,256,512]{2,1,0:T(8,128)S(1)} custom-call(s32[4,4]{1,0:T(4,128)S(1)} %dynamic-slice_bitcast_fusion.entries, bf16[2,256,4096]{2,1,0:T(8,128)(2,1)S(1)} %get-tuple-element.29.whole, bf16[9,512,4096]{2,1,0:T(8,128)(2,1)} %dec.3), custom_call_target="tpu_custom_call" | custom-call | flops 10000000000 | bytes 10485760 | tf_op jit(solution)/shard_map/own_gradients/pallas_call | solution.py:411
  156.5 2.5 %collective-permute-done.45 = bf16[2,256,512]{2,1,0:T(8,128)(2,1)S(1)} collective-permute-done((bf16[2,256,512]{2,1,0:T(8,128)(2,1)S(1)}, bf16[2,256,512]{2,1,0:T(8,128)(2,1)S(1)}, u32[]{:S(2)}, u32[]{:S(2)}) %collective-permute-start.45) | collective-permute-done | bytes 524320 | tf_op jit(solution)/shard_map/ppermute | solution.py:488
  159.0 15.1 %collective-permute-done.46 = bf16[2,256,512]{2,1,0:T(8,128)(2,1)S(1)} collective-permute-done((bf16[2,256,512]{2,1,0:T(8,128)(2,1)S(1)}, bf16[2,256,512]{2,1,0:T(8,128)(2,1)S(1)}, u32[]{:S(2)}, u32[]{:S(2)}) %collective-permute-start.46) | collective-permute-done | bytes 524320 | tf_op jit(solution)/shard_map/ppermute | solution.py:487
  174.1 1.4 add_multiply_fusion
  (90 shorter events, 12.7 us)
Async XLA Ops:
  1.6 9.1 %collective-permute-start.11 = (bf16[256,512]{1,0:T(8,128)(2,1)S(1)}, bf16[256,512]{1,0:T(8,128)(2,1)S(1)}, u32[]{:S(2)}, u32[]{:S(2)}) collective-permute-start(bf16[256,512]{1,0:T(8,128)(2,1)S(1)} %slice_bitcast_fusion.1.refs_0_), channel_id=1, source_target_pairs={{0,2},{1,5},{2,0},{3,7},{4,6},{5,1},{6,4},{7,3},{8,10},{9,13},{10,... | collective-permute-start | bytes 786440 | tf_op jit(solution)/shard_map/ppermute | solution.py:428
  2.2 10.6 %collective-permute-start.12 = (bf16[256,512]{1,0:T(8,128)(2,1)S(1)}, bf16[256,512]{1,0:T(8,128)(2,1)S(1)}, u32[]{:S(2)}, u32[]{:S(2)}) collective-permute-start(bf16[256,512]{1,0:T(8,128)(2,1)S(1)} %slice_bitcast_fusion.1.refs_0_), channel_id=1, source_target_pairs={{0,4},{1,3},{2,6},{3,1},{4,0},{5,7},{6,2},{7,5},{8,12},{9,11},{10,... | collective-permute-start | bytes 786440 | tf_op jit(solution)/shard_map/ppermute | solution.py:429
  3.7 9.1 %collective-permute-start.14 = (bf16[256,512]{1,0:T(8,128)(2,1)S(1)}, bf16[256,512]{1,0:T(8,128)(2,1)S(1)}, u32[]{:S(2)}, u32[]{:S(2)}) collective-permute-start(bf16[256,512]{1,0:T(8,128)(2,1)S(1)} %slice_bitcast_fusion.1.refs_0_), channel_id=1, source_target_pairs={{0,1},{1,0},{2,3},{3,2},{4,5},{5,4},{6,7},{7,6},{8,9},{9,8},{10,11... | collective-permute-start | bytes 786440 | tf_op jit(solution)/shard_map/ppermute | solution.py:432
  4.7 11.7 %collective-permute-start = (bf16[256,512]{1,0:T(8,128)(2,1)S(1)}, bf16[256,512]{1,0:T(8,128)(2,1)S(1)}, u32[]{:S(2)}, u32[]{:S(2)}) collective-permute-start(bf16[256,512]{1,0:T(8,128)(2,1)S(1)} %slice_bitcast_fusion.refs_0_), channel_id=1, source_target_pairs={{0,2},{1,5},{2,0},{3,7},{4,6},{5,1},{6,4},{7,3},{8,10},{9,13},{10,... | collective-permute-start | bytes 786440 | tf_op jit(solution)/shard_map/ppermute | solution.py:428
  10.7 6.4 %collective-permute-start.13 = (bf16[256,512]{1,0:T(8,128)(2,1)S(1)}, bf16[256,512]{1,0:T(8,128)(2,1)S(1)}, u32[]{:S(2)}, u32[]{:S(2)}) collective-permute-start(bf16[256,512]{1,0:T(8,128)(2,1)S(1)} %collective-permute-done.11.refs_1_), channel_id=1, source_target_pairs={{0,4},{1,3},{2,6},{3,1},{4,0},{5,7},{6,2},{7,5},{8,12},{9,11},{10,... | collective-permute-start | bytes 786440 | tf_op jit(solution)/shard_map/ppermute | solution.py:430
  11.5 8.5 %collective-permute-start.1 = (bf16[256,512]{1,0:T(8,128)(2,1)S(1)}, bf16[256,512]{1,0:T(8,128)(2,1)S(1)}, u32[]{:S(2)}, u32[]{:S(2)}) collective-permute-start(bf16[256,512]{1,0:T(8,128)(2,1)S(1)} %slice_bitcast_fusion.refs_0_), channel_id=1, source_target_pairs={{0,4},{1,3},{2,6},{3,1},{4,0},{5,7},{6,2},{7,5},{8,12},{9,11},{10,... | collective-permute-start | bytes 786440 | tf_op jit(solution)/shard_map/ppermute | solution.py:429
  12.8 7.2 %collective-permute-start.15 = (bf16[256,512]{1,0:T(8,128)(2,1)S(1)}, bf16[256,512]{1,0:T(8,128)(2,1)S(1)}, u32[]{:S(2)}, u32[]{:S(2)}) collective-permute-start(bf16[256,512]{1,0:T(8,128)(2,1)S(1)} %collective-permute-done.11.refs_1_), channel_id=1, source_target_pairs={{0,1},{1,0},{2,3},{3,2},{4,5},{5,4},{6,7},{7,6},{8,9},{9,8},{10,11... | collective-permute-start | bytes 786440 | tf_op jit(solution)/shard_map/ppermute | solution.py:432
  12.8 7.7 %collective-permute-start.16 = (bf16[256,512]{1,0:T(8,128)(2,1)S(1)}, bf16[256,512]{1,0:T(8,128)(2,1)S(1)}, u32[]{:S(2)}, u32[]{:S(2)}) collective-permute-start(bf16[256,512]{1,0:T(8,128)(2,1)S(1)} %collective-permute-done.12.refs_2_), channel_id=1, source_target_pairs={{0,1},{1,0},{2,3},{3,2},{4,5},{5,4},{6,7},{7,6},{8,9},{9,8},{10,11... | collective-permute-start | bytes 786440 | tf_op jit(solution)/shard_map/ppermute | solution.py:432
  16.4 6.4 %collective-permute-start.2 = (bf16[256,512]{1,0:T(8,128)(2,1)S(1)}, bf16[256,512]{1,0:T(8,128)(2,1)S(1)}, u32[]{:S(2)}, u32[]{:S(2)}) collective-permute-start(bf16[256,512]{1,0:T(8,128)(2,1)S(1)} %collective-permute-done.refs_1_), channel_id=1, source_target_pairs={{0,4},{1,3},{2,6},{3,1},{4,0},{5,7},{6,2},{7,5},{8,12},{9,11},{10,... | collective-permute-start | bytes 786440 | tf_op jit(solution)/shard_map/ppermute | solution.py:430
  17.1 5.6 %collective-permute-start.17 = (bf16[256,512]{1,0:T(8,128)(2,1)S(1)}, bf16[256,512]{1,0:T(8,128)(2,1)S(1)}, u32[]{:S(2)}, u32[]{:S(2)}) collective-permute-start(bf16[256,512]{1,0:T(8,128)(2,1)S(1)} %collective-permute-done.13.refs_3_), channel_id=1, source_target_pairs={{0,1},{1,0},{2,3},{3,2},{4,5},{5,4},{6,7},{7,6},{8,9},{9,8},{10,11... | collective-permute-start | bytes 786440 | tf_op jit(solution)/shard_map/ppermute | solution.py:432
  19.9 8.9 %collective-permute-start.3 = (bf16[256,512]{1,0:T(8,128)(2,1)S(1)}, bf16[256,512]{1,0:T(8,128)(2,1)S(1)}, u32[]{:S(2)}, u32[]{:S(2)}) collective-permute-start(bf16[256,512]{1,0:T(8,128)(2,1)S(1)} %slice_bitcast_fusion.refs_0_), channel_id=1, source_target_pairs={{0,1},{1,0},{2,3},{3,2},{4,5},{5,4},{6,7},{7,6},{8,9},{9,8},{10,11... | collective-permute-start | bytes 786440 | tf_op jit(solution)/shard_map/ppermute | solution.py:432
  19.9 11.3 %collective-permute-start.4 = (bf16[256,512]{1,0:T(8,128)(2,1)S(1)}, bf16[256,512]{1,0:T(8,128)(2,1)S(1)}, u32[]{:S(2)}, u32[]{:S(2)}) collective-permute-start(bf16[256,512]{1,0:T(8,128)(2,1)S(1)} %collective-permute-done.refs_1_), channel_id=1, source_target_pairs={{0,1},{1,0},{2,3},{3,2},{4,5},{5,4},{6,7},{7,6},{8,9},{9,8},{10,11... | collective-permute-start | bytes 786440 | tf_op jit(solution)/shard_map/ppermute | solution.py:432
  20.4 10.8 %collective-permute-start.5 = (bf16[256,512]{1,0:T(8,128)(2,1)S(1)}, bf16[256,512]{1,0:T(8,128)(2,1)S(1)}, u32[]{:S(2)}, u32[]{:S(2)}) collective-permute-start(bf16[256,512]{1,0:T(8,128)(2,1)S(1)} %collective-permute-done.1.refs_2_), channel_id=1, source_target_pairs={{0,1},{1,0},{2,3},{3,2},{4,5},{5,4},{6,7},{7,6},{8,9},{9,8},{10,11... | collective-permute-start | bytes 786440 | tf_op jit(solution)/shard_map/ppermute | solution.py:432
  22.7 8.5 %collective-permute-start.6 = (bf16[256,512]{1,0:T(8,128)(2,1)S(1)}, bf16[256,512]{1,0:T(8,128)(2,1)S(1)}, u32[]{:S(2)}, u32[]{:S(2)}) collective-permute-start(bf16[256,512]{1,0:T(8,128)(2,1)S(1)} %collective-permute-done.2.refs_3_), channel_id=1, source_target_pairs={{0,1},{1,0},{2,3},{3,2},{4,5},{5,4},{6,7},{7,6},{8,9},{9,8},{10,11... | collective-permute-start | bytes 786440 | tf_op jit(solution)/shard_map/ppermute | solution.py:432
  26.2 17.0 %collective-permute-start.18 = (bf16[256,512]{1,0:T(8,128)(2,1)S(1)}, bf16[256,512]{1,0:T(8,128)(2,1)S(1)}, u32[]{:S(2)}, u32[]{:S(2)}) collective-permute-start(bf16[256,512]{1,0:T(8,128)(2,1)S(1)} %encode.3.refs_1_), channel_id=1, source_target_pairs={{0,16},{16,0},{8,24},{24,8},{1,17},{17,1},{9,25},{25,9},{2,18},{18... | collective-permute-start | bytes 786440 | tf_op jit(solution)/shard_map/ppermute | solution.py:454
  28.8 19.2 %collective-permute-start.20 = (bf16[256,512]{1,0:T(8,128)(2,1)S(1)}, bf16[256,512]{1,0:T(8,128)(2,1)S(1)}, u32[]{:S(2)}, u32[]{:S(2)}) collective-permute-start(bf16[256,512]{1,0:T(8,128)(2,1)S(1)} %encode.3.refs_1_), channel_id=1, source_target_pairs={{0,8},{8,0},{16,24},{1,9},{9,1},{17,25},{2,10},{10,2},{18,26},{3,1... | collective-permute-start | bytes 786440 | tf_op jit(solution)/shard_map/ppermute | solution.py:455
  34.7 17.3 %collective-permute-start.9 = (bf16[256,512]{1,0:T(8,128)(2,1)S(1)}, bf16[256,512]{1,0:T(8,128)(2,1)S(1)}, u32[]{:S(2)}, u32[]{:S(2)}) collective-permute-start(bf16[256,512]{1,0:T(8,128)(2,1)S(1)} %encode.2.refs_0_), channel_id=1, source_target_pairs={{0,16},{16,0},{8,24},{24,8},{1,17},{17,1},{9,25},{25,9},{2,18},{18... | collective-permute-start | bytes 786440 | tf_op jit(solution)/shard_map/ppermute | solution.py:454
  34.8 23.0 %collective-permute-start.21 = (bf16[256,512]{1,0:T(8,128)(2,1)S(1)}, bf16[256,512]{1,0:T(8,128)(2,1)S(1)}, u32[]{:S(2)}, u32[]{:S(2)}) collective-permute-start(bf16[256,512]{1,0:T(8,128)(2,1)S(1)} %encode.3.refs_1_), channel_id=1, source_target_pairs={{8,16},{16,8},{9,17},{17,9},{10,18},{18,10},{11,19},{19,11},{12,20... | collective-permute-start | bytes 786440 | tf_op jit(solution)/shard_map/ppermute | solution.py:456
  41.3 27.6 %collective-permute-start.7 = (bf16[256,512]{1,0:T(8,128)(2,1)S(1)}, bf16[256,512]{1,0:T(8,128)(2,1)S(1)}, u32[]{:S(2)}, u32[]{:S(2)}) collective-permute-start(bf16[256,512]{1,0:T(8,128)(2,1)S(1)} %encode.2.refs_0_), channel_id=1, source_target_pairs={{0,8},{8,0},{16,24},{1,9},{9,1},{17,25},{2,10},{10,2},{18,26},{3,1... | collective-permute-start | bytes 786440 | tf_op jit(solution)/shard_map/ppermute | solution.py:455
  43.2 25.7 %collective-permute-start.8 = (bf16[256,512]{1,0:T(8,128)(2,1)S(1)}, bf16[256,512]{1,0:T(8,128)(2,1)S(1)}, u32[]{:S(2)}, u32[]{:S(2)}) collective-permute-start(bf16[256,512]{1,0:T(8,128)(2,1)S(1)} %encode.2.refs_0_), channel_id=1, source_target_pairs={{8,16},{16,8},{9,17},{17,9},{10,18},{18,10},{11,19},{19,11},{12,20... | collective-permute-start | bytes 786440 | tf_op jit(solution)/shard_map/ppermute | solution.py:456
  48.0 20.9 %collective-permute-start.19 = (bf16[256,512]{1,0:T(8,128)(2,1)S(1)}, bf16[256,512]{1,0:T(8,128)(2,1)S(1)}, u32[]{:S(2)}, u32[]{:S(2)}) collective-permute-start(bf16[256,512]{1,0:T(8,128)(2,1)S(1)} %collective-permute-done.18.refs_4_), channel_id=1, source_target_pairs={{16,24},{8,0},{17,25},{9,1},{18,26},{10,2},{19,27},{11,3},{20,28},... | collective-permute-start | bytes 786440 | tf_op jit(solution)/shard_map/ppermute | solution.py:457
  51.9 17.0 %collective-permute-start.10 = (bf16[256,512]{1,0:T(8,128)(2,1)S(1)}, bf16[256,512]{1,0:T(8,128)(2,1)S(1)}, u32[]{:S(2)}, u32[]{:S(2)}) collective-permute-start(bf16[256,512]{1,0:T(8,128)(2,1)S(1)} %collective-permute-done.9.refs_2_), channel_id=1, source_target_pairs={{16,24},{8,0},{17,25},{9,1},{18,26},{10,2},{19,27},{11,3},{20,28},... | collective-permute-start | bytes 786440 | tf_op jit(solution)/shard_map/ppermute | solution.py:457
  76.7 2.0 %collective-permute-start.23 = (bf16[2,2,128,512]{3,2,1,0:T(8,128)(2,1)S(1)}, bf16[2,2,128,512]{3,2,1,0:T(8,128)(2,1)S(1)}, u32[]{:S(2)}, u32[]{:S(2)}) collective-permute-start(bf16[2,2,128,512]{3,2,1,0:T(8,128)(2,1)S(1)} %get-tuple-element.22), channel_id=1, source_target_pairs={{0,1},{1,0},{2,3},{3,2},{4,5},{5,4},{6,7},{7,6},{8,9},{9,8},{10,11... | collective-permute-start | bytes 1572872 | tf_op jit(solution)/shard_map/ppermute | solution.py:468
  76.8 2.8 %collective-permute-start.34 = (bf16[2,2,128,512]{3,2,1,0:T(8,128)(2,1)S(1)}, bf16[2,2,128,512]{3,2,1,0:T(8,128)(2,1)S(1)}, u32[]{:S(2)}, u32[]{:S(2)}) collective-permute-start(bf16[2,2,128,512]{3,2,1,0:T(8,128)(2,1)S(1)} %get-tuple-element.26), channel_id=1, source_target_pairs={{0,1},{1,0},{2,3},{3,2},{4,5},{5,4},{6,7},{7,6},{8,9},{9,8},{10,11... | collective-permute-start | bytes 1572872 | tf_op jit(solution)/shard_map/ppermute | solution.py:468
  77.3 3.8 %collective-permute-start.22 = (bf16[2,2,128,512]{3,2,1,0:T(8,128)(2,1)S(1)}, bf16[2,2,128,512]{3,2,1,0:T(8,128)(2,1)S(1)}, u32[]{:S(2)}, u32[]{:S(2)}) collective-permute-start(bf16[2,2,128,512]{3,2,1,0:T(8,128)(2,1)S(1)} %get-tuple-element.20), channel_id=1, source_target_pairs={{0,1},{1,0},{2,3},{3,2},{4,5},{5,4},{6,7},{7,6},{8,9},{9,8},{10,11... | collective-permute-start | bytes 1572872 | tf_op jit(solution)/shard_map/ppermute | solution.py:470
  77.4 11.3 %collective-permute-start.33 = (bf16[2,2,128,512]{3,2,1,0:T(8,128)(2,1)S(1)}, bf16[2,2,128,512]{3,2,1,0:T(8,128)(2,1)S(1)}, u32[]{:S(2)}, u32[]{:S(2)}) collective-permute-start(bf16[2,2,128,512]{3,2,1,0:T(8,128)(2,1)S(1)} %get-tuple-element.24), channel_id=1, source_target_pairs={{0,1},{1,0},{2,3},{3,2},{4,5},{5,4},{6,7},{7,6},{8,9},{9,8},{10,11... | collective-permute-start | bytes 1572872 | tf_op jit(solution)/shard_map/ppermute | solution.py:470
  78.8 9.2 %collective-permute-start.24 = (bf16[2,2,128,512]{3,2,1,0:T(8,128)(2,1)S(1)}, bf16[2,2,128,512]{3,2,1,0:T(8,128)(2,1)S(1)}, u32[]{:S(2)}, u32[]{:S(2)}) collective-permute-start(bf16[2,2,128,512]{3,2,1,0:T(8,128)(2,1)S(1)} %add_convert_fusion.1), channel_id=1, source_target_pairs={{0,4},{1,3},{2,6},{3,1},{4,0},{5,7},{6,2},{7,5},{8,12},{9,11},{10,... | collective-permute-start | bytes 1572872 | tf_op jit(solution)/shard_map/ppermute | solution.py:469
  79.7 16.7 %collective-permute-start.35 = (bf16[2,2,128,512]{3,2,1,0:T(8,128)(2,1)S(1)}, bf16[2,2,128,512]{3,2,1,0:T(8,128)(2,1)S(1)}, u32[]{:S(2)}, u32[]{:S(2)}) collective-permute-start(bf16[2,2,128,512]{3,2,1,0:T(8,128)(2,1)S(1)} %add_convert_fusion), channel_id=1, source_target_pairs={{0,4},{1,3},{2,6},{3,1},{4,0},{5,7},{6,2},{7,5},{8,12},{9,11},{10,... | collective-permute-start | bytes 1572872 | tf_op jit(solution)/shard_map/ppermute | solution.py:469
  88.3 8.4 %collective-permute-start.25 = (bf16[2,128,512]{2,1,0:T(8,128)(2,1)S(1)}, bf16[2,128,512]{2,1,0:T(8,128)(2,1)S(1)}, u32[]{:S(2)}, u32[]{:S(2)}) collective-permute-start(bf16[2,128,512]{2,1,0:T(8,128)(2,1)S(1)} %fusion.11), channel_id=1, source_target_pairs={{0,2},{1,5},{2,0},{3,7},{4,6},{5,1},{6,4},{7,3},{8,10},{9,13},{10,... | collective-permute-start | bytes 786440 | tf_op jit(solution)/shard_map/ppermute | solution.py:474
  96.9 9.2 %collective-permute-start.36 = (bf16[2,128,512]{2,1,0:T(8,128)(2,1)S(1)}, bf16[2,128,512]{2,1,0:T(8,128)(2,1)S(1)}, u32[]{:S(2)}, u32[]{:S(2)}) collective-permute-start(bf16[2,128,512]{2,1,0:T(8,128)(2,1)S(1)} %fusion.12), channel_id=1, source_target_pairs={{0,2},{1,5},{2,0},{3,7},{4,6},{5,1},{6,4},{7,3},{8,10},{9,13},{10,... | collective-permute-start | bytes 786440 | tf_op jit(solution)/shard_map/ppermute | solution.py:474
  97.2 14.3 %collective-permute-start.26 = (bf16[2,128,512]{2,1,0:T(8,128)(2,1)S(1)}, bf16[2,128,512]{2,1,0:T(8,128)(2,1)S(1)}, u32[]{:S(2)}, u32[]{:S(2)}) collective-permute-start(bf16[2,128,512]{2,1,0:T(8,128)(2,1)S(1)} %fusion.10.refs_0_), channel_id=1, source_target_pairs={{0,2},{1,5},{2,0},{3,7},{4,6},{5,1},{6,4},{7,3},{8,10},{9,13},{10,... | collective-permute-start | bytes 786440 | tf_op jit(solution)/shard_map/ppermute | solution.py:428
  99.0 12.6 %collective-permute-start.27 = (bf16[2,128,512]{2,1,0:T(8,128)(2,1)S(1)}, bf16[2,128,512]{2,1,0:T(8,128)(2,1)S(1)}, u32[]{:S(2)}, u32[]{:S(2)}) collective-permute-start(bf16[2,128,512]{2,1,0:T(8,128)(2,1)S(1)} %fusion.10.refs_0_), channel_id=1, source_target_pairs={{0,4},{1,3},{2,6},{3,1},{4,0},{5,7},{6,2},{7,5},{8,12},{9,11},{10,... | collective-permute-start | bytes 786440 | tf_op jit(solution)/shard_map/ppermute | solution.py:429
  99.7 12.6 %collective-permute-start.29 = (bf16[2,128,512]{2,1,0:T(8,128)(2,1)S(1)}, bf16[2,128,512]{2,1,0:T(8,128)(2,1)S(1)}, u32[]{:S(2)}, u32[]{:S(2)}) collective-permute-start(bf16[2,128,512]{2,1,0:T(8,128)(2,1)S(1)} %fusion.10.refs_0_), channel_id=1, source_target_pairs={{0,1},{1,0},{2,3},{3,2},{4,5},{5,4},{6,7},{7,6},{8,9},{9,8},{10,11... | collective-permute-start | bytes 786440 | tf_op jit(solution)/shard_map/ppermute | solution.py:432
  106.4 8.0 %collective-permute-start.37 = (bf16[2,128,512]{2,1,0:T(8,128)(2,1)S(1)}, bf16[2,128,512]{2,1,0:T(8,128)(2,1)S(1)}, u32[]{:S(2)}, u32[]{:S(2)}) collective-permute-start(bf16[2,128,512]{2,1,0:T(8,128)(2,1)S(1)} %subtract_convert_fusion.refs_8_), channel_id=1, source_target_pairs={{0,2},{1,5},{2,0},{3,7},{4,6},{5,1},{6,4},{7,3},{8,10},{9,13},{10,... | collective-permute-start | bytes 786440 | tf_op jit(solution)/shard_map/ppermute | solution.py:428
  106.7 8.4 %collective-permute-start.38 = (bf16[2,128,512]{2,1,0:T(8,128)(2,1)S(1)}, bf16[2,128,512]{2,1,0:T(8,128)(2,1)S(1)}, u32[]{:S(2)}, u32[]{:S(2)}) collective-permute-start(bf16[2,128,512]{2,1,0:T(8,128)(2,1)S(1)} %subtract_convert_fusion.refs_8_), channel_id=1, source_target_pairs={{0,4},{1,3},{2,6},{3,1},{4,0},{5,7},{6,2},{7,5},{8,12},{9,11},{10,... | collective-permute-start | bytes 786440 | tf_op jit(solution)/shard_map/ppermute | solution.py:429
  111.5 3.5 %collective-permute-start.40 = (bf16[2,128,512]{2,1,0:T(8,128)(2,1)S(1)}, bf16[2,128,512]{2,1,0:T(8,128)(2,1)S(1)}, u32[]{:S(2)}, u32[]{:S(2)}) collective-permute-start(bf16[2,128,512]{2,1,0:T(8,128)(2,1)S(1)} %subtract_convert_fusion.refs_8_), channel_id=1, source_target_pairs={{0,1},{1,0},{2,3},{3,2},{4,5},{5,4},{6,7},{7,6},{8,9},{9,8},{10,11... | collective-permute-start | bytes 786440 | tf_op jit(solution)/shard_map/ppermute | solution.py:432
  111.6 6.4 %collective-permute-start.28 = (bf16[2,128,512]{2,1,0:T(8,128)(2,1)S(1)}, bf16[2,128,512]{2,1,0:T(8,128)(2,1)S(1)}, u32[]{:S(2)}, u32[]{:S(2)}) collective-permute-start(bf16[2,128,512]{2,1,0:T(8,128)(2,1)S(1)} %collective-permute-done.26.refs_1_), channel_id=1, source_target_pairs={{0,4},{1,3},{2,6},{3,1},{4,0},{5,7},{6,2},{7,5},{8,12},{9,11},{10,... | collective-permute-start | bytes 786440 | tf_op jit(solution)/shard_map/ppermute | solution.py:430
  112.3 5.7 %collective-permute-start.30 = (bf16[2,128,512]{2,1,0:T(8,128)(2,1)S(1)}, bf16[2,128,512]{2,1,0:T(8,128)(2,1)S(1)}, u32[]{:S(2)}, u32[]{:S(2)}) collective-permute-start(bf16[2,128,512]{2,1,0:T(8,128)(2,1)S(1)} %collective-permute-done.26.refs_1_), channel_id=1, source_target_pairs={{0,1},{1,0},{2,3},{3,2},{4,5},{5,4},{6,7},{7,6},{8,9},{9,8},{10,11... | collective-permute-start | bytes 786440 | tf_op jit(solution)/shard_map/ppermute | solution.py:432
  114.4 6.4 %collective-permute-start.39 = (bf16[2,128,512]{2,1,0:T(8,128)(2,1)S(1)}, bf16[2,128,512]{2,1,0:T(8,128)(2,1)S(1)}, u32[]{:S(2)}, u32[]{:S(2)}) collective-permute-start(bf16[2,128,512]{2,1,0:T(8,128)(2,1)S(1)} %collective-permute-done.37.refs_9_), channel_id=1, source_target_pairs={{0,4},{1,3},{2,6},{3,1},{4,0},{5,7},{6,2},{7,5},{8,12},{9,11},{10,... | collective-permute-start | bytes 786440 | tf_op jit(solution)/shard_map/ppermute | solution.py:430
  115.1 7.9 %collective-permute-start.31 = (bf16[2,128,512]{2,1,0:T(8,128)(2,1)S(1)}, bf16[2,128,512]{2,1,0:T(8,128)(2,1)S(1)}, u32[]{:S(2)}, u32[]{:S(2)}) collective-permute-start(bf16[2,128,512]{2,1,0:T(8,128)(2,1)S(1)} %collective-permute-done.27.refs_2_), channel_id=1, source_target_pairs={{0,1},{1,0},{2,3},{3,2},{4,5},{5,4},{6,7},{7,6},{8,9},{9,8},{10,11... | collective-permute-start | bytes 786440 | tf_op jit(solution)/shard_map/ppermute | solution.py:432
  115.1 7.9 %collective-permute-start.41 = (bf16[2,128,512]{2,1,0:T(8,128)(2,1)S(1)}, bf16[2,128,512]{2,1,0:T(8,128)(2,1)S(1)}, u32[]{:S(2)}, u32[]{:S(2)}) collective-permute-start(bf16[2,128,512]{2,1,0:T(8,128)(2,1)S(1)} %collective-permute-done.37.refs_9_), channel_id=1, source_target_pairs={{0,1},{1,0},{2,3},{3,2},{4,5},{5,4},{6,7},{7,6},{8,9},{9,8},{10,11... | collective-permute-start | bytes 786440 | tf_op jit(solution)/shard_map/ppermute | solution.py:432
  117.9 5.1 %collective-permute-start.42 = (bf16[2,128,512]{2,1,0:T(8,128)(2,1)S(1)}, bf16[2,128,512]{2,1,0:T(8,128)(2,1)}, u32[]{:S(2)}, u32[]{:S(2)}) collective-permute-start(bf16[2,128,512]{2,1,0:T(8,128)(2,1)S(1)} %collective-permute-done.38.refs_10_), channel_id=1, source_target_pairs={{0,1},{1,0},{2,3},{3,2},{4,5},{5,4},{6,7},{7,6},{8,9},{9,8},{10,11... | collective-permute-start | bytes 786440 | tf_op jit(solution)/shard_map/ppermute | solution.py:432
  117.9 5.1 %collective-permute-start.32 = (bf16[2,128,512]{2,1,0:T(8,128)(2,1)S(1)}, bf16[2,128,512]{2,1,0:T(8,128)(2,1)}, u32[]{:S(2)}, u32[]{:S(2)}) collective-permute-start(bf16[2,128,512]{2,1,0:T(8,128)(2,1)S(1)} %collective-permute-done.28.refs_3_), channel_id=1, source_target_pairs={{0,1},{1,0},{2,3},{3,2},{4,5},{5,4},{6,7},{7,6},{8,9},{9,8},{10,11... | collective-permute-start | bytes 786440 | tf_op jit(solution)/shard_map/ppermute | solution.py:432
  120.7 2.3 %collective-permute-start.43 = (bf16[2,128,512]{2,1,0:T(8,128)(2,1)S(1)}, bf16[2,128,512]{2,1,0:T(8,128)(2,1)}, u32[]{:S(2)}, u32[]{:S(2)}) collective-permute-start(bf16[2,128,512]{2,1,0:T(8,128)(2,1)S(1)} %collective-permute-done.39.refs_11_), channel_id=1, source_target_pairs={{0,1},{1,0},{2,3},{3,2},{4,5},{5,4},{6,7},{7,6},{8,9},{9,8},{10,11... | collective-permute-start | bytes 786440 | tf_op jit(solution)/shard_map/ppermute | solution.py:432
  130.4 16.4 %collective-permute-start.44 = (bf16[2,256,512]{2,1,0:T(8,128)(2,1)S(1)}, bf16[2,256,512]{2,1,0:T(8,128)(2,1)S(1)}, u32[]{:S(2)}, u32[]{:S(2)}) collective-permute-start(bf16[2,256,512]{2,1,0:T(8,128)(2,1)S(1)} %get-tuple-element.34), channel_id=1, source_target_pairs={{0,8},{24,16},{16,0},{8,24},{1,9},{25,17},{17,1},{9,25},{2,10},{26... | collective-permute-start | bytes 1572872 | tf_op jit(solution)/shard_map/ppermute | solution.py:483
  142.3 16.7 %collective-permute-start.45 = (bf16[2,256,512]{2,1,0:T(8,128)(2,1)S(1)}, bf16[2,256,512]{2,1,0:T(8,128)(2,1)S(1)}, u32[]{:S(2)}, u32[]{:S(2)}) collective-permute-start(bf16[2,256,512]{2,1,0:T(8,128)(2,1)S(1)} %get-tuple-element.31), channel_id=1, source_target_pairs={{0,8},{8,0},{24,16},{1,9},{9,1},{25,17},{2,10},{10,2},{26,18},{3,1... | collective-permute-start | bytes 1572872 | tf_op jit(solution)/shard_map/ppermute | solution.py:488
  144.3 14.7 %collective-permute-start.47 = (bf16[2,256,512]{2,1,0:T(8,128)(2,1)S(1)}, bf16[2,256,512]{2,1,0:T(8,128)(2,1)S(1)}, u32[]{:S(2)}, u32[]{:S(2)}) collective-permute-start(bf16[2,256,512]{2,1,0:T(8,128)(2,1)S(1)} %get-tuple-element.33), channel_id=1, source_target_pairs={{0,24},{24,0},{1,25},{25,1},{2,26},{26,2},{3,27},{27,3},{4,28},{28... | collective-permute-start | bytes 1572872 | tf_op jit(solution)/shard_map/ppermute | solution.py:485
  147.0 27.0 %collective-permute-start.46 = (bf16[2,256,512]{2,1,0:T(8,128)(2,1)S(1)}, bf16[2,256,512]{2,1,0:T(8,128)(2,1)S(1)}, u32[]{:S(2)}, u32[]{:S(2)}) collective-permute-start(bf16[2,256,512]{2,1,0:T(8,128)(2,1)S(1)} %fusion), channel_id=1, source_target_pairs={{8,16},{16,8},{9,17},{17,9},{10,18},{18,10},{11,19},{19,11},{12,20... | collective-permute-start | bytes 1572872 | tf_op jit(solution)/shard_map/ppermute | solution.py:487
  (3 other events, 55.5 us)

commit v5 on v4

--- a/solution.py
+++ b/solution.py
@@ -150,8 +150,10 @@
     *blocks, bias, enc, fire, out, held, weight, mask, shift, acc, sems, wsems, fsem, ssem = refs
     width = blocks[0].shape[1]
     rows = [pl.ds(pl.multiple_of(order[i] * width, width), width) for i in range(8)]
-    weights = bring([enc.at[layer, r, :] for r in rows], [weight.at[i] for i in range(8)], wsems)
-    values = bring(blocks, [held.at[i] for i in range(8)], sems)
+    values, weights = [], []
+    for i, block in enumerate(blocks):
+        values += bring([block], [held.at[i]], sems.at[pl.ds(i, 1)])
+        weights += bring([enc.at[layer, rows[i], :]], [weight.at[i]], wsems.at[pl.ds(i, 1)])
     fired = pltpu.make_async_copy(fire.at[layer], mask, fsem)
     fired.start()
     shifted = pltpu.make_async_copy(bias, shift, ssem)

time: 176 us -> 176 us (level)
  no operation moved by 1% of the time
where the time goes in v5:
time: 176 us
  waiting for transfers between devices  67.9 us (39%)
  starting transfers between devices  50.2 us (29%)
  Pallas kernels  46.6 us (26%)
  local copies, waits for them, and re-layouts  5.84 us (3%)
  other arithmetic  3.95 us (2%)
    ppermute x1, waiting for transfers between devices, on_device(): middle = lax.ppermute(across, 'layer', MIDDLE)  15 us
    ppermute x2, waiting for transfers between devices, on_device(): far = lax.ppermute(far.astype(bf16), 'feat', SECOND).astype(f32)  14.5 us
    ppermute x4, waiting for transfers between devices, gather(): first = lax.ppermute(own, 'feat', FIRST)  13.6 us
    pallas_call x1, Pallas kernels, reconstruct_early(): pl.pallas_call(early_kernel, in_specs=[SMEM] + [HBM] * len(sources) + [HB...  11 us
    ppermute x2, starting transfers between devices, on_device(): middle = lax.ppermute(acts, 'layer', MIDDLE)  9.73 us
    pallas_call x1, Pallas kernels, rest_gradients(): pl.pallas_call(rest_kernel, in_specs=[SMEM, VMEM, VMEM, HBM], out_specs=[...  8.1 us
    pallas_call x1, Pallas kernels, reconstruct_late(): pl.pallas_call(late_kernel, in_specs=[SMEM] * 2 + [HBM] * len(sources) +...  7.76 us
    ppermute x4, waiting for transfers between devices, gather(): both = lax.ppermute(first, 'feat', SECOND)  7.59 us
  transfers between devices with their start and end apart: 48, of which 18 were waited for; matrix products, arithmetic and copies ran while one was open for 4% of the time, Pallas kernels for 18%

profile of v5, /device:TPU:10, one launch (start us, length us, event | category | flops | bytes accessed | tf_op | source)
XLA Modules:
  0.0 175.5 jit_solution(8934576334886140070)
XLA Ops:
  0.6 1.0 slice_bitcast_fusion.1.refs_0_
  2.2 1.5 collective-permute-start.12
  3.7 1.0 slice_bitcast_fusion.refs_0_
  4.7 1.6 collective-permute-start
  6.3 4.5 %collective-permute-done.11.refs_1_ = bf16[256,512]{1,0:T(8,128)(2,1)S(1)} collective-permute-done((bf16[256,512]{1,0:T(8,128)(2,1)S(1)}, bf16[256,512]{1,0:T(8,128)(2,1)S(1)}, u32[]{:S(2)}, u32[]{:S(2)}) %collective-permute-start.11) | collective-permute-done | bytes 262176 | tf_op jit(solution)/shard_map/ppermute | solution.py:430
  11.5 1.3 collective-permute-start.1
  13.3 3.1 %collective-permute-done.refs_1_ = bf16[256,512]{1,0:T(8,128)(2,1)S(1)} collective-permute-done((bf16[256,512]{1,0:T(8,128)(2,1)S(1)}, bf16[256,512]{1,0:T(8,128)(2,1)S(1)}, u32[]{:S(2)}, u32[]{:S(2)}) %collective-permute-start) | collective-permute-done | bytes 262176 | tf_op jit(solution)/shard_map/ppermute | solution.py:430
  16.4 0.8 collective-permute-done.13.refs_3_
  17.2 2.7 %collective-permute-done.1.refs_2_ = bf16[256,512]{1,0:T(8,128)(2,1)S(1)} collective-permute-done((bf16[256,512]{1,0:T(8,128)(2,1)S(1)}, bf16[256,512]{1,0:T(8,128)(2,1)S(1)}, u32[]{:S(2)}, u32[]{:S(2)}) %collective-permute-start.1) | collective-permute-done | bytes 262176 | tf_op jit(solution)/shard_map/ppermute | solution.py:431
  20.5 2.2 %collective-permute-done.2.refs_3_ = bf16[256,512]{1,0:T(8,128)(2,1)S(1)} collective-permute-done((bf16[256,512]{1,0:T(8,128)(2,1)S(1)}, bf16[256,512]{1,0:T(8,128)(2,1)S(1)}, u32[]{:S(2)}, u32[]{:S(2)}) %collective-permute-start.2) | collective-permute-done | bytes 262176 | tf_op jit(solution)/shard_map/ppermute | solution.py:432
  22.7 3.5 %encode.3.refs_1_ = bf16[256,512]{1,0:T(8,128)(2,1)S(1)} custom-call(s32[8]{0:T(128)S(1)} %broadcast_xor_fusion.order.cols, bf16[256,512]{1,0:T(8,128)(2,1)S(1)} %slice_bitcast_fusion.1.refs_0_, bf16[256,512]{1,0:T(8,128)(2,1)S(1)} %collective-permute-done.11.refs_1_, bf16[256,512]{1,0:T(8,128)(2,1)S(1)} %collective-permute-done.12.refs_2_, ...), custom_call_target="tpu_custom_call" | custom-call | flops 1000000000 | bytes 1048576 | tf_op jit(solution)/shard_map/encode/pallas_call | solution.py:178
  26.2 2.7 %collective-permute-start.18 = (bf16[256,512]{1,0:T(8,128)(2,1)S(1)}, bf16[256,512]{1,0:T(8,128)(2,1)S(1)}, u32[]{:S(2)}, u32[]{:S(2)}) collective-permute-start(bf16[256,512]{1,0:T(8,128)(2,1)S(1)} %encode.3.refs_1_), channel_id=1, source_target_pairs={{0,16},{16,0},{8,24},{24,8},{1,17},{17,1},{9,25},{25,9},{2,18},{18... | collective-permute-start | bytes 786440 | tf_op jit(solution)/shard_map/ppermute | solution.py:456
  28.9 2.3 %collective-permute-start.20 = (bf16[256,512]{1,0:T(8,128)(2,1)S(1)}, bf16[256,512]{1,0:T(8,128)(2,1)S(1)}, u32[]{:S(2)}, u32[]{:S(2)}) collective-permute-start(bf16[256,512]{1,0:T(8,128)(2,1)S(1)} %encode.3.refs_1_), channel_id=1, source_target_pairs={{0,8},{8,0},{16,24},{1,9},{9,1},{17,25},{2,10},{10,2},{18,26},{3,1... | collective-permute-start | bytes 786440 | tf_op jit(solution)/shard_map/ppermute | solution.py:457
  31.2 3.5 %encode.2.refs_0_ = bf16[256,512]{1,0:T(8,128)(2,1)S(1)} custom-call(s32[8]{0:T(128)S(1)} %broadcast_xor_fusion.order.cols, bf16[256,512]{1,0:T(8,128)(2,1)S(1)} %slice_bitcast_fusion.refs_0_, bf16[256,512]{1,0:T(8,128)(2,1)S(1)} %collective-permute-done.refs_1_, bf16[256,512]{1,0:T(8,128)(2,1)S(1)} %collective-permute-done.1.refs_2_, ...), custom_call_target="tpu_custom_call" | custom-call | flops 1000000000 | bytes 1048576 | tf_op jit(solution)/shard_map/encode/pallas_call | solution.py:178
  34.8 4.9 %collective-permute-start.21 = (bf16[256,512]{1,0:T(8,128)(2,1)S(1)}, bf16[256,512]{1,0:T(8,128)(2,1)S(1)}, u32[]{:S(2)}, u32[]{:S(2)}) collective-permute-start(bf16[256,512]{1,0:T(8,128)(2,1)S(1)} %encode.3.refs_1_), channel_id=1, source_target_pairs={{8,16},{16,8},{9,17},{17,9},{10,18},{18,10},{11,19},{19,11},{12,20... | collective-permute-start | bytes 786440 | tf_op jit(solution)/shard_map/ppermute | solution.py:458
  41.3 1.9 %collective-permute-start.7 = (bf16[256,512]{1,0:T(8,128)(2,1)S(1)}, bf16[256,512]{1,0:T(8,128)(2,1)S(1)}, u32[]{:S(2)}, u32[]{:S(2)}) collective-permute-start(bf16[256,512]{1,0:T(8,128)(2,1)S(1)} %encode.2.refs_0_), channel_id=1, source_target_pairs={{0,8},{8,0},{16,24},{1,9},{9,1},{17,25},{2,10},{10,2},{18,26},{3,1... | collective-permute-start | bytes 786440 | tf_op jit(solution)/shard_map/ppermute | solution.py:457
  43.2 4.8 %collective-permute-start.8 = (bf16[256,512]{1,0:T(8,128)(2,1)S(1)}, bf16[256,512]{1,0:T(8,128)(2,1)S(1)}, u32[]{:S(2)}, u32[]{:S(2)}) collective-permute-start(bf16[256,512]{1,0:T(8,128)(2,1)S(1)} %encode.2.refs_0_), channel_id=1, source_target_pairs={{8,16},{16,8},{9,17},{17,9},{10,18},{18,10},{11,19},{19,11},{12,20... | collective-permute-start | bytes 786440 | tf_op jit(solution)/shard_map/ppermute | solution.py:458
  48.0 2.7 %collective-permute-start.19 = (bf16[256,512]{1,0:T(8,128)(2,1)S(1)}, bf16[256,512]{1,0:T(8,128)(2,1)S(1)}, u32[]{:S(2)}, u32[]{:S(2)}) collective-permute-start(bf16[256,512]{1,0:T(8,128)(2,1)S(1)} %collective-permute-done.18.refs_4_), channel_id=1, source_target_pairs={{16,24},{8,0},{17,25},{9,1},{18,26},{10,2},{19,27},{11,3},{20,28},... | collective-permute-start | bytes 786440 | tf_op jit(solution)/shard_map/ppermute | solution.py:459
  50.7 1.2 collective-permute-done.9.refs_2_
  52.0 3.6 %collective-permute-start.10 = (bf16[256,512]{1,0:T(8,128)(2,1)S(1)}, bf16[256,512]{1,0:T(8,128)(2,1)S(1)}, u32[]{:S(2)}, u32[]{:S(2)}) collective-permute-start(bf16[256,512]{1,0:T(8,128)(2,1)S(1)} %collective-permute-done.9.refs_2_), channel_id=1, source_target_pairs={{16,24},{8,0},{17,25},{9,1},{18,26},{10,2},{19,27},{11,3},{20,28},... | collective-permute-start | bytes 786440 | tf_op jit(solution)/shard_map/ppermute | solution.py:459
  55.6 2.2 %collective-permute-done.21.refs_3_ = bf16[256,512]{1,0:T(8,128)(2,1)S(1)} collective-permute-done((bf16[256,512]{1,0:T(8,128)(2,1)S(1)}, bf16[256,512]{1,0:T(8,128)(2,1)S(1)}, u32[]{:S(2)}, u32[]{:S(2)}) %collective-permute-start.21) | collective-permute-done | bytes 262176 | tf_op jit(solution)/shard_map/ppermute | solution.py:458
  57.8 11.0 %reconstruct_early.1.refs_5_ = bf16[2,256,4096]{2,1,0:T(8,128)(2,1)S(1)} custom-call(s32[7,4]{1,0:T(8,128)S(1)} %copy.14.entries, bf16[256,512]{1,0:T(8,128)(2,1)S(1)} %encode.2.refs_0_, bf16[256,512]{1,0:T(8,128)(2,1)S(1)} %encode.3.refs_1_, bf16[256,512]{1,0:T(8,128)(2,1)S(1)} %collective-permute-done.20.refs_2_, ...), custom_call_target="tpu_custom_call" | custom-call | flops 10000000000 | bytes 10485760 | tf_op jit(solution)/shard_map/reconstruct_early/pallas_call | solution.py:262
  68.9 7.8 %reconstruct_late.1 = (bf16[2,2,128,512]{3,2,1,0:T(8,128)(2,1)S(1)}, bf16[2,2,128,512]{3,2,1,0:T(8,128)(2,1)S(1)}, bf16[2,2,128,512]{3,2,1,0:T(8,128)(2,1)S(1)},...) custom-call(s32[7,4]{1,0:T(8,128)S(1)} %copy.15.entries, ...), custom_call_target="tpu_custom_call" | custom-call | flops 10000000000 | bytes 10485760 | tf_op jit(solution)/shard_map/reconstruct_late/pallas_call | solution.py:307
  77.8 0.9 collective-permute-done.23
  78.8 0.8 collective-permute-start.24
  79.8 1.4 collective-permute-start.35
  81.3 6.8 %collective-permute-done.24 = bf16[2,2,128,512]{3,2,1,0:T(8,128)(2,1)S(1)} collective-permute-done((bf16[2,2,128,512]{3,2,1,0:T(8,128)(2,1)S(1)}, bf16[2,2,128,512]{3,2,1,0:T(8,128)(2,1)S(1)}, u32[]{:S(2)}, u32[]{:S(2)}) %collective-permute-start.24) | collective-permute-done | bytes 524320 | tf_op jit(solution)/shard_map/ppermute | solution.py:471
  88.8 7.7 %collective-permute-done.35 = bf16[2,2,128,512]{3,2,1,0:T(8,128)(2,1)S(1)} collective-permute-done((bf16[2,2,128,512]{3,2,1,0:T(8,128)(2,1)S(1)}, bf16[2,2,128,512]{3,2,1,0:T(8,128)(2,1)S(1)}, u32[]{:S(2)}, u32[]{:S(2)}) %collective-permute-start.35) | collective-permute-done | bytes 524320 | tf_op jit(solution)/shard_map/ppermute | solution.py:471
  97.3 1.7 collective-permute-start.26
  99.0 0.7 collective-permute-start.27
  99.7 6.4 %collective-permute-done.36 = bf16[2,128,512]{2,1,0:T(8,128)(2,1)S(1)} collective-permute-done((bf16[2,128,512]{2,1,0:T(8,128)(2,1)S(1)}, bf16[2,128,512]{2,1,0:T(8,128)(2,1)S(1)}, u32[]{:S(2)}, u32[]{:S(2)}) %collective-permute-start.36) | collective-permute-done | bytes 262176 | tf_op jit(solution)/shard_map/ppermute | solution.py:476
  106.7 0.8 collective-permute-start.38
  107.5 4.0 %collective-permute-done.26.refs_1_ = bf16[2,128,512]{2,1,0:T(8,128)(2,1)S(1)} collective-permute-done((bf16[2,128,512]{2,1,0:T(8,128)(2,1)S(1)}, bf16[2,128,512]{2,1,0:T(8,128)(2,1)S(1)}, u32[]{:S(2)}, u32[]{:S(2)}) %collective-permute-start.26) | collective-permute-done | bytes 262176 | tf_op jit(solution)/shard_map/ppermute | solution.py:430
  111.6 0.7 collective-permute-start.28
  112.3 2.1 %collective-permute-done.37.refs_9_ = bf16[2,128,512]{2,1,0:T(8,128)(2,1)S(1)} collective-permute-done((bf16[2,128,512]{2,1,0:T(8,128)(2,1)S(1)}, bf16[2,128,512]{2,1,0:T(8,128)(2,1)S(1)}, u32[]{:S(2)}, u32[]{:S(2)}) %collective-permute-start.37) | collective-permute-done | bytes 262176 | tf_op jit(solution)/shard_map/ppermute | solution.py:430
  115.6 2.3 %collective-permute-done.28.refs_3_ = bf16[2,128,512]{2,1,0:T(8,128)(2,1)S(1)} collective-permute-done((bf16[2,128,512]{2,1,0:T(8,128)(2,1)S(1)}, bf16[2,128,512]{2,1,0:T(8,128)(2,1)S(1)}, u32[]{:S(2)}, u32[]{:S(2)}) %collective-permute-start.28) | collective-permute-done | bytes 262176 | tf_op jit(solution)/shard_map/ppermute | solution.py:432
  118.5 2.3 %collective-permute-done.39.refs_11_ = bf16[2,128,512]{2,1,0:T(8,128)(2,1)S(1)} collective-permute-done((bf16[2,128,512]{2,1,0:T(8,128)(2,1)S(1)}, bf16[2,128,512]{2,1,0:T(8,128)(2,1)S(1)}, u32[]{:S(2)}, u32[]{:S(2)}) %collective-permute-start.39) | collective-permute-done | bytes 262176 | tf_op jit(solution)/shard_map/ppermute | solution.py:432
  123.0 7.4 %first_gradients.1 = (bf16[2,256,512]{2,1,0:T(8,128)(2,1)S(1)}, f32[2,256,512]{2,1,0:T(8,128)S(1)}, bf16[2,256,4096]{2,1,0:T(8,128)(2,1)S(1)}) custom-call(s32[5,4]{1,0:T(8,128)S(1)} %copy.16.entries, s32[8]{0:T(128)S(1)} %broadcast_xor_fusion.order.cols, bf16[2,128,512]{2,1,0:T(8,128)(2,1)S(1)} %fusion.10.refs_0_, ...), custom_call_target="tpu_custom_call" | custom-call | flops 10000000000 | bytes 10485760 | tf_op jit(solution)/shard_map/first_gradients/pallas_call | solution.py:353
  130.5 3.8 %collective-permute-start.44 = (bf16[2,256,512]{2,1,0:T(8,128)(2,1)S(1)}, bf16[2,256,512]{2,1,0:T(8,128)(2,1)S(1)}, u32[]{:S(2)}, u32[]{:S(2)}) collective-permute-start(bf16[2,256,512]{2,1,0:T(8,128)(2,1)S(1)} %get-tuple-element.34), channel_id=1, source_target_pairs={{0,8},{24,16},{16,0},{8,24},{1,9},{25,17},{17,1},{9,25},{2,10},{26... | collective-permute-start | bytes 1572872 | tf_op jit(solution)/shard_map/ppermute | solution.py:485
  134.3 8.1 %rest_gradients.1 = (bf16[2,256,512]{2,1,0:T(8,128)(2,1)S(1)}, bf16[2,256,512]{2,1,0:T(8,128)(2,1)S(1)}) custom-call(s32[6,4]{1,0:T(8,128)S(1)} %copy.17.entries, bf16[2,256,4096]{2,1,0:T(8,128)(2,1)S(1)} %get-tuple-element.29.whole, f32[2,256,512]{2,1,0:T(8,128)S(1)} %get-tuple-element.30.begun, bf16[9,512,4096]{2,1,0:T(8,128)(2,1)} %dec.3), custom_call_target="tpu_custom_call" | custom-call | flops 10000000000 | bytes 10485760 | tf_op jit(solution)/shard_map/rest_gradients/pallas_call | solution.py:387
  142.4 1.9 %collective-permute-start.45 = (bf16[2,256,512]{2,1,0:T(8,128)(2,1)S(1)}, bf16[2,256,512]{2,1,0:T(8,128)(2,1)S(1)}, u32[]{:S(2)}, u32[]{:S(2)}) collective-permute-start(bf16[2,256,512]{2,1,0:T(8,128)(2,1)S(1)} %get-tuple-element.31), channel_id=1, source_target_pairs={{0,8},{8,0},{24,16},{1,9},{9,1},{25,17},{2,10},{10,2},{26,18},{3,1... | collective-permute-start | bytes 1572872 | tf_op jit(solution)/shard_map/ppermute | solution.py:490
  145.0 0.8 pad_maximum_fusion
  145.8 1.1 collective-permute-done.44
  147.1 3.9 %collective-permute-start.46 = (bf16[2,256,512]{2,1,0:T(8,128)(2,1)S(1)}, bf16[2,256,512]{2,1,0:T(8,128)(2,1)S(1)}, u32[]{:S(2)}, u32[]{:S(2)}) collective-permute-start(bf16[2,256,512]{2,1,0:T(8,128)(2,1)S(1)} %fusion), channel_id=1, source_target_pairs={{8,16},{16,8},{9,17},{17,9},{10,18},{18,10},{11,19},{19,11},{12,20... | collective-permute-start | bytes 1572872 | tf_op jit(solution)/shard_map/ppermute | solution.py:489
  151.0 5.4 %own_gradients.1 = f32[2,256,512]{2,1,0:T(8,128)S(1)} custom-call(s32[4,4]{1,0:T(4,128)S(1)} %dynamic-slice_bitcast_fusion.entries, bf16[2,256,4096]{2,1,0:T(8,128)(2,1)S(1)} %get-tuple-element.29.whole, bf16[9,512,4096]{2,1,0:T(8,128)(2,1)} %dec.3), custom_call_target="tpu_custom_call" | custom-call | flops 10000000000 | bytes 10485760 | tf_op jit(solution)/shard_map/own_gradients/pallas_call | solution.py:413
  156.5 2.5 %collective-permute-done.45 = bf16[2,256,512]{2,1,0:T(8,128)(2,1)S(1)} collective-permute-done((bf16[2,256,512]{2,1,0:T(8,128)(2,1)S(1)}, bf16[2,256,512]{2,1,0:T(8,128)(2,1)S(1)}, u32[]{:S(2)}, u32[]{:S(2)}) %collective-permute-start.45) | collective-permute-done | bytes 524320 | tf_op jit(solution)/shard_map/ppermute | solution.py:490
  159.0 15.0 %collective-permute-done.46 = bf16[2,256,512]{2,1,0:T(8,128)(2,1)S(1)} collective-permute-done((bf16[2,256,512]{2,1,0:T(8,128)(2,1)S(1)}, bf16[2,256,512]{2,1,0:T(8,128)(2,1)S(1)}, u32[]{:S(2)}, u32[]{:S(2)}) %collective-permute-start.46) | collective-permute-done | bytes 524320 | tf_op jit(solution)/shard_map/ppermute | solution.py:489
  174.1 1.4 add_multiply_fusion
  (90 shorter events, 12.7 us)
Async XLA Ops:
  1.6 9.1 %collective-permute-start.11 = (bf16[256,512]{1,0:T(8,128)(2,1)S(1)}, bf16[256,512]{1,0:T(8,128)(2,1)S(1)}, u32[]{:S(2)}, u32[]{:S(2)}) collective-permute-start(bf16[256,512]{1,0:T(8,128)(2,1)S(1)} %slice_bitcast_fusion.1.refs_0_), channel_id=1, source_target_pairs={{0,2},{1,5},{2,0},{3,7},{4,6},{5,1},{6,4},{7,3},{8,10},{9,13},{10,... | collective-permute-start | bytes 786440 | tf_op jit(solution)/shard_map/ppermute | solution.py:430
  2.2 10.6 %collective-permute-start.12 = (bf16[256,512]{1,0:T(8,128)(2,1)S(1)}, bf16[256,512]{1,0:T(8,128)(2,1)S(1)}, u32[]{:S(2)}, u32[]{:S(2)}) collective-permute-start(bf16[256,512]{1,0:T(8,128)(2,1)S(1)} %slice_bitcast_fusion.1.refs_0_), channel_id=1, source_target_pairs={{0,4},{1,3},{2,6},{3,1},{4,0},{5,7},{6,2},{7,5},{8,12},{9,11},{10,... | collective-permute-start | bytes 786440 | tf_op jit(solution)/shard_map/ppermute | solution.py:431
  3.7 9.1 %collective-permute-start.14 = (bf16[256,512]{1,0:T(8,128)(2,1)S(1)}, bf16[256,512]{1,0:T(8,128)(2,1)S(1)}, u32[]{:S(2)}, u32[]{:S(2)}) collective-permute-start(bf16[256,512]{1,0:T(8,128)(2,1)S(1)} %slice_bitcast_fusion.1.refs_0_), channel_id=1, source_target_pairs={{0,1},{1,0},{2,3},{3,2},{4,5},{5,4},{6,7},{7,6},{8,9},{9,8},{10,11... | collective-permute-start | bytes 786440 | tf_op jit(solution)/shard_map/ppermute | solution.py:434
  4.7 11.7 %collective-permute-start = (bf16[256,512]{1,0:T(8,128)(2,1)S(1)}, bf16[256,512]{1,0:T(8,128)(2,1)S(1)}, u32[]{:S(2)}, u32[]{:S(2)}) collective-permute-start(bf16[256,512]{1,0:T(8,128)(2,1)S(1)} %slice_bitcast_fusion.refs_0_), channel_id=1, source_target_pairs={{0,2},{1,5},{2,0},{3,7},{4,6},{5,1},{6,4},{7,3},{8,10},{9,13},{10,... | collective-permute-start | bytes 786440 | tf_op jit(solution)/shard_map/ppermute | solution.py:430
  10.7 6.4 %collective-permute-start.13 = (bf16[256,512]{1,0:T(8,128)(2,1)S(1)}, bf16[256,512]{1,0:T(8,128)(2,1)S(1)}, u32[]{:S(2)}, u32[]{:S(2)}) collective-permute-start(bf16[256,512]{1,0:T(8,128)(2,1)S(1)} %collective-permute-done.11.refs_1_), channel_id=1, source_target_pairs={{0,4},{1,3},{2,6},{3,1},{4,0},{5,7},{6,2},{7,5},{8,12},{9,11},{10,... | collective-permute-start | bytes 786440 | tf_op jit(solution)/shard_map/ppermute | solution.py:432
  11.5 8.5 %collective-permute-start.1 = (bf16[256,512]{1,0:T(8,128)(2,1)S(1)}, bf16[256,512]{1,0:T(8,128)(2,1)S(1)}, u32[]{:S(2)}, u32[]{:S(2)}) collective-permute-start(bf16[256,512]{1,0:T(8,128)(2,1)S(1)} %slice_bitcast_fusion.refs_0_), channel_id=1, source_target_pairs={{0,4},{1,3},{2,6},{3,1},{4,0},{5,7},{6,2},{7,5},{8,12},{9,11},{10,... | collective-permute-start | bytes 786440 | tf_op jit(solution)/shard_map/ppermute | solution.py:431
  12.8 7.2 %collective-permute-start.15 = (bf16[256,512]{1,0:T(8,128)(2,1)S(1)}, bf16[256,512]{1,0:T(8,128)(2,1)S(1)}, u32[]{:S(2)}, u32[]{:S(2)}) collective-permute-start(bf16[256,512]{1,0:T(8,128)(2,1)S(1)} %collective-permute-done.11.refs_1_), channel_id=1, source_target_pairs={{0,1},{1,0},{2,3},{3,2},{4,5},{5,4},{6,7},{7,6},{8,9},{9,8},{10,11... | collective-permute-start | bytes 786440 | tf_op jit(solution)/shard_map/ppermute | solution.py:434
  12.8 7.7 %collective-permute-start.16 = (bf16[256,512]{1,0:T(8,128)(2,1)S(1)}, bf16[256,512]{1,0:T(8,128)(2,1)S(1)}, u32[]{:S(2)}, u32[]{:S(2)}) collective-permute-start(bf16[256,512]{1,0:T(8,128)(2,1)S(1)} %collective-permute-done.12.refs_2_), channel_id=1, source_target_pairs={{0,1},{1,0},{2,3},{3,2},{4,5},{5,4},{6,7},{7,6},{8,9},{9,8},{10,11... | collective-permute-start | bytes 786440 | tf_op jit(solution)/shard_map/ppermute | solution.py:434
  16.4 6.4 %collective-permute-start.2 = (bf16[256,512]{1,0:T(8,128)(2,1)S(1)}, bf16[256,512]{1,0:T(8,128)(2,1)S(1)}, u32[]{:S(2)}, u32[]{:S(2)}) collective-permute-start(bf16[256,512]{1,0:T(8,128)(2,1)S(1)} %collective-permute-done.refs_1_), channel_id=1, source_target_pairs={{0,4},{1,3},{2,6},{3,1},{4,0},{5,7},{6,2},{7,5},{8,12},{9,11},{10,... | collective-permute-start | bytes 786440 | tf_op jit(solution)/shard_map/ppermute | solution.py:432
  17.1 5.6 %collective-permute-start.17 = (bf16[256,512]{1,0:T(8,128)(2,1)S(1)}, bf16[256,512]{1,0:T(8,128)(2,1)S(1)}, u32[]{:S(2)}, u32[]{:S(2)}) collective-permute-start(bf16[256,512]{1,0:T(8,128)(2,1)S(1)} %collective-permute-done.13.refs_3_), channel_id=1, source_target_pairs={{0,1},{1,0},{2,3},{3,2},{4,5},{5,4},{6,7},{7,6},{8,9},{9,8},{10,11... | collective-permute-start | bytes 786440 | tf_op jit(solution)/shard_map/ppermute | solution.py:434
  19.9 8.9 %collective-permute-start.3 = (bf16[256,512]{1,0:T(8,128)(2,1)S(1)}, bf16[256,512]{1,0:T(8,128)(2,1)S(1)}, u32[]{:S(2)}, u32[]{:S(2)}) collective-permute-start(bf16[256,512]{1,0:T(8,128)(2,1)S(1)} %slice_bitcast_fusion.refs_0_), channel_id=1, source_target_pairs={{0,1},{1,0},{2,3},{3,2},{4,5},{5,4},{6,7},{7,6},{8,9},{9,8},{10,11... | collective-permute-start | bytes 786440 | tf_op jit(solution)/shard_map/ppermute | solution.py:434
  19.9 11.3 %collective-permute-start.4 = (bf16[256,512]{1,0:T(8,128)(2,1)S(1)}, bf16[256,512]{1,0:T(8,128)(2,1)S(1)}, u32[]{:S(2)}, u32[]{:S(2)}) collective-permute-start(bf16[256,512]{1,0:T(8,128)(2,1)S(1)} %collective-permute-done.refs_1_), channel_id=1, source_target_pairs={{0,1},{1,0},{2,3},{3,2},{4,5},{5,4},{6,7},{7,6},{8,9},{9,8},{10,11... | collective-permute-start | bytes 786440 | tf_op jit(solution)/shard_map/ppermute | solution.py:434
  20.4 10.8 %collective-permute-start.5 = (bf16[256,512]{1,0:T(8,128)(2,1)S(1)}, bf16[256,512]{1,0:T(8,128)(2,1)S(1)}, u32[]{:S(2)}, u32[]{:S(2)}) collective-permute-start(bf16[256,512]{1,0:T(8,128)(2,1)S(1)} %collective-permute-done.1.refs_2_), channel_id=1, source_target_pairs={{0,1},{1,0},{2,3},{3,2},{4,5},{5,4},{6,7},{7,6},{8,9},{9,8},{10,11... | collective-permute-start | bytes 786440 | tf_op jit(solution)/shard_map/ppermute | solution.py:434
  22.7 8.5 %collective-permute-start.6 = (bf16[256,512]{1,0:T(8,128)(2,1)S(1)}, bf16[256,512]{1,0:T(8,128)(2,1)S(1)}, u32[]{:S(2)}, u32[]{:S(2)}) collective-permute-start(bf16[256,512]{1,0:T(8,128)(2,1)S(1)} %collective-permute-done.2.refs_3_), channel_id=1, source_target_pairs={{0,1},{1,0},{2,3},{3,2},{4,5},{5,4},{6,7},{7,6},{8,9},{9,8},{10,11... | collective-permute-start | bytes 786440 | tf_op jit(solution)/shard_map/ppermute | solution.py:434
  26.2 17.0 %collective-permute-start.18 = (bf16[256,512]{1,0:T(8,128)(2,1)S(1)}, bf16[256,512]{1,0:T(8,128)(2,1)S(1)}, u32[]{:S(2)}, u32[]{:S(2)}) collective-permute-start(bf16[256,512]{1,0:T(8,128)(2,1)S(1)} %encode.3.refs_1_), channel_id=1, source_target_pairs={{0,16},{16,0},{8,24},{24,8},{1,17},{17,1},{9,25},{25,9},{2,18},{18... | collective-permute-start | bytes 786440 | tf_op jit(solution)/shard_map/ppermute | solution.py:456
  28.9 19.2 %collective-permute-start.20 = (bf16[256,512]{1,0:T(8,128)(2,1)S(1)}, bf16[256,512]{1,0:T(8,128)(2,1)S(1)}, u32[]{:S(2)}, u32[]{:S(2)}) collective-permute-start(bf16[256,512]{1,0:T(8,128)(2,1)S(1)} %encode.3.refs_1_), channel_id=1, source_target_pairs={{0,8},{8,0},{16,24},{1,9},{9,1},{17,25},{2,10},{10,2},{18,26},{3,1... | collective-permute-start | bytes 786440 | tf_op jit(solution)/shard_map/ppermute | solution.py:457
  34.7 17.2 %collective-permute-start.9 = (bf16[256,512]{1,0:T(8,128)(2,1)S(1)}, bf16[256,512]{1,0:T(8,128)(2,1)S(1)}, u32[]{:S(2)}, u32[]{:S(2)}) collective-permute-start(bf16[256,512]{1,0:T(8,128)(2,1)S(1)} %encode.2.refs_0_), channel_id=1, source_target_pairs={{0,16},{16,0},{8,24},{24,8},{1,17},{17,1},{9,25},{25,9},{2,18},{18... | collective-permute-start | bytes 786440 | tf_op jit(solution)/shard_map/ppermute | solution.py:456
  34.8 23.0 %collective-permute-start.21 = (bf16[256,512]{1,0:T(8,128)(2,1)S(1)}, bf16[256,512]{1,0:T(8,128)(2,1)S(1)}, u32[]{:S(2)}, u32[]{:S(2)}) collective-permute-start(bf16[256,512]{1,0:T(8,128)(2,1)S(1)} %encode.3.refs_1_), channel_id=1, source_target_pairs={{8,16},{16,8},{9,17},{17,9},{10,18},{18,10},{11,19},{19,11},{12,20... | collective-permute-start | bytes 786440 | tf_op jit(solution)/shard_map/ppermute | solution.py:458
  41.3 27.6 %collective-permute-start.7 = (bf16[256,512]{1,0:T(8,128)(2,1)S(1)}, bf16[256,512]{1,0:T(8,128)(2,1)S(1)}, u32[]{:S(2)}, u32[]{:S(2)}) collective-permute-start(bf16[256,512]{1,0:T(8,128)(2,1)S(1)} %encode.2.refs_0_), channel_id=1, source_target_pairs={{0,8},{8,0},{16,24},{1,9},{9,1},{17,25},{2,10},{10,2},{18,26},{3,1... | collective-permute-start | bytes 786440 | tf_op jit(solution)/shard_map/ppermute | solution.py:457
  43.2 25.7 %collective-permute-start.8 = (bf16[256,512]{1,0:T(8,128)(2,1)S(1)}, bf16[256,512]{1,0:T(8,128)(2,1)S(1)}, u32[]{:S(2)}, u32[]{:S(2)}) collective-permute-start(bf16[256,512]{1,0:T(8,128)(2,1)S(1)} %encode.2.refs_0_), channel_id=1, source_target_pairs={{8,16},{16,8},{9,17},{17,9},{10,18},{18,10},{11,19},{19,11},{12,20... | collective-permute-start | bytes 786440 | tf_op jit(solution)/shard_map/ppermute | solution.py:458
  48.0 20.9 %collective-permute-start.19 = (bf16[256,512]{1,0:T(8,128)(2,1)S(1)}, bf16[256,512]{1,0:T(8,128)(2,1)S(1)}, u32[]{:S(2)}, u32[]{:S(2)}) collective-permute-start(bf16[256,512]{1,0:T(8,128)(2,1)S(1)} %collective-permute-done.18.refs_4_), channel_id=1, source_target_pairs={{16,24},{8,0},{17,25},{9,1},{18,26},{10,2},{19,27},{11,3},{20,28},... | collective-permute-start | bytes 786440 | tf_op jit(solution)/shard_map/ppermute | solution.py:459
  52.0 17.0 %collective-permute-start.10 = (bf16[256,512]{1,0:T(8,128)(2,1)S(1)}, bf16[256,512]{1,0:T(8,128)(2,1)S(1)}, u32[]{:S(2)}, u32[]{:S(2)}) collective-permute-start(bf16[256,512]{1,0:T(8,128)(2,1)S(1)} %collective-permute-done.9.refs_2_), channel_id=1, source_target_pairs={{16,24},{8,0},{17,25},{9,1},{18,26},{10,2},{19,27},{11,3},{20,28},... | collective-permute-start | bytes 786440 | tf_op jit(solution)/shard_map/ppermute | solution.py:459
  76.7 2.0 %collective-permute-start.23 = (bf16[2,2,128,512]{3,2,1,0:T(8,128)(2,1)S(1)}, bf16[2,2,128,512]{3,2,1,0:T(8,128)(2,1)S(1)}, u32[]{:S(2)}, u32[]{:S(2)}) collective-permute-start(bf16[2,2,128,512]{3,2,1,0:T(8,128)(2,1)S(1)} %get-tuple-element.22), channel_id=1, source_target_pairs={{0,1},{1,0},{2,3},{3,2},{4,5},{5,4},{6,7},{7,6},{8,9},{9,8},{10,11... | collective-permute-start | bytes 1572872 | tf_op jit(solution)/shard_map/ppermute | solution.py:470
  76.8 2.8 %collective-permute-start.34 = (bf16[2,2,128,512]{3,2,1,0:T(8,128)(2,1)S(1)}, bf16[2,2,128,512]{3,2,1,0:T(8,128)(2,1)S(1)}, u32[]{:S(2)}, u32[]{:S(2)}) collective-permute-start(bf16[2,2,128,512]{3,2,1,0:T(8,128)(2,1)S(1)} %get-tuple-element.26), channel_id=1, source_target_pairs={{0,1},{1,0},{2,3},{3,2},{4,5},{5,4},{6,7},{7,6},{8,9},{9,8},{10,11... | collective-permute-start | bytes 1572872 | tf_op jit(solution)/shard_map/ppermute | solution.py:470
  77.3 3.8 %collective-permute-start.22 = (bf16[2,2,128,512]{3,2,1,0:T(8,128)(2,1)S(1)}, bf16[2,2,128,512]{3,2,1,0:T(8,128)(2,1)S(1)}, u32[]{:S(2)}, u32[]{:S(2)}) collective-permute-start(bf16[2,2,128,512]{3,2,1,0:T(8,128)(2,1)S(1)} %get-tuple-element.20), channel_id=1, source_target_pairs={{0,1},{1,0},{2,3},{3,2},{4,5},{5,4},{6,7},{7,6},{8,9},{9,8},{10,11... | collective-permute-start | bytes 1572872 | tf_op jit(solution)/shard_map/ppermute | solution.py:472
  77.4 11.3 %collective-permute-start.33 = (bf16[2,2,128,512]{3,2,1,0:T(8,128)(2,1)S(1)}, bf16[2,2,128,512]{3,2,1,0:T(8,128)(2,1)S(1)}, u32[]{:S(2)}, u32[]{:S(2)}) collective-permute-start(bf16[2,2,128,512]{3,2,1,0:T(8,128)(2,1)S(1)} %get-tuple-element.24), channel_id=1, source_target_pairs={{0,1},{1,0},{2,3},{3,2},{4,5},{5,4},{6,7},{7,6},{8,9},{9,8},{10,11... | collective-permute-start | bytes 1572872 | tf_op jit(solution)/shard_map/ppermute | solution.py:472
  78.8 9.2 %collective-permute-start.24 = (bf16[2,2,128,512]{3,2,1,0:T(8,128)(2,1)S(1)}, bf16[2,2,128,512]{3,2,1,0:T(8,128)(2,1)S(1)}, u32[]{:S(2)}, u32[]{:S(2)}) collective-permute-start(bf16[2,2,128,512]{3,2,1,0:T(8,128)(2,1)S(1)} %add_convert_fusion.1), channel_id=1, source_target_pairs={{0,4},{1,3},{2,6},{3,1},{4,0},{5,7},{6,2},{7,5},{8,12},{9,11},{10,... | collective-permute-start | bytes 1572872 | tf_op jit(solution)/shard_map/ppermute | solution.py:471
  79.8 16.7 %collective-permute-start.35 = (bf16[2,2,128,512]{3,2,1,0:T(8,128)(2,1)S(1)}, bf16[2,2,128,512]{3,2,1,0:T(8,128)(2,1)S(1)}, u32[]{:S(2)}, u32[]{:S(2)}) collective-permute-start(bf16[2,2,128,512]{3,2,1,0:T(8,128)(2,1)S(1)} %add_convert_fusion), channel_id=1, source_target_pairs={{0,4},{1,3},{2,6},{3,1},{4,0},{5,7},{6,2},{7,5},{8,12},{9,11},{10,... | collective-permute-start | bytes 1572872 | tf_op jit(solution)/shard_map/ppermute | solution.py:471
  88.3 8.4 %collective-permute-start.25 = (bf16[2,128,512]{2,1,0:T(8,128)(2,1)S(1)}, bf16[2,128,512]{2,1,0:T(8,128)(2,1)S(1)}, u32[]{:S(2)}, u32[]{:S(2)}) collective-permute-start(bf16[2,128,512]{2,1,0:T(8,128)(2,1)S(1)} %fusion.11), channel_id=1, source_target_pairs={{0,2},{1,5},{2,0},{3,7},{4,6},{5,1},{6,4},{7,3},{8,10},{9,13},{10,... | collective-permute-start | bytes 786440 | tf_op jit(solution)/shard_map/ppermute | solution.py:476
  96.9 9.2 %collective-permute-start.36 = (bf16[2,128,512]{2,1,0:T(8,128)(2,1)S(1)}, bf16[2,128,512]{2,1,0:T(8,128)(2,1)S(1)}, u32[]{:S(2)}, u32[]{:S(2)}) collective-permute-start(bf16[2,128,512]{2,1,0:T(8,128)(2,1)S(1)} %fusion.12), channel_id=1, source_target_pairs={{0,2},{1,5},{2,0},{3,7},{4,6},{5,1},{6,4},{7,3},{8,10},{9,13},{10,... | collective-permute-start | bytes 786440 | tf_op jit(solution)/shard_map/ppermute | solution.py:476
  97.3 14.3 %collective-permute-start.26 = (bf16[2,128,512]{2,1,0:T(8,128)(2,1)S(1)}, bf16[2,128,512]{2,1,0:T(8,128)(2,1)S(1)}, u32[]{:S(2)}, u32[]{:S(2)}) collective-permute-start(bf16[2,128,512]{2,1,0:T(8,128)(2,1)S(1)} %fusion.10.refs_0_), channel_id=1, source_target_pairs={{0,2},{1,5},{2,0},{3,7},{4,6},{5,1},{6,4},{7,3},{8,10},{9,13},{10,... | collective-permute-start | bytes 786440 | tf_op jit(solution)/shard_map/ppermute | solution.py:430
  99.0 12.6 %collective-permute-start.27 = (bf16[2,128,512]{2,1,0:T(8,128)(2,1)S(1)}, bf16[2,128,512]{2,1,0:T(8,128)(2,1)S(1)}, u32[]{:S(2)}, u32[]{:S(2)}) collective-permute-start(bf16[2,128,512]{2,1,0:T(8,128)(2,1)S(1)} %fusion.10.refs_0_), channel_id=1, source_target_pairs={{0,4},{1,3},{2,6},{3,1},{4,0},{5,7},{6,2},{7,5},{8,12},{9,11},{10,... | collective-permute-start | bytes 786440 | tf_op jit(solution)/shard_map/ppermute | solution.py:431
  99.7 12.6 %collective-permute-start.29 = (bf16[2,128,512]{2,1,0:T(8,128)(2,1)S(1)}, bf16[2,128,512]{2,1,0:T(8,128)(2,1)S(1)}, u32[]{:S(2)}, u32[]{:S(2)}) collective-permute-start(bf16[2,128,512]{2,1,0:T(8,128)(2,1)S(1)} %fusion.10.refs_0_), channel_id=1, source_target_pairs={{0,1},{1,0},{2,3},{3,2},{4,5},{5,4},{6,7},{7,6},{8,9},{9,8},{10,11... | collective-permute-start | bytes 786440 | tf_op jit(solution)/shard_map/ppermute | solution.py:434
  106.4 8.0 %collective-permute-start.37 = (bf16[2,128,512]{2,1,0:T(8,128)(2,1)S(1)}, bf16[2,128,512]{2,1,0:T(8,128)(2,1)S(1)}, u32[]{:S(2)}, u32[]{:S(2)}) collective-permute-start(bf16[2,128,512]{2,1,0:T(8,128)(2,1)S(1)} %subtract_convert_fusion.refs_8_), channel_id=1, source_target_pairs={{0,2},{1,5},{2,0},{3,7},{4,6},{5,1},{6,4},{7,3},{8,10},{9,13},{10,... | collective-permute-start | bytes 786440 | tf_op jit(solution)/shard_map/ppermute | solution.py:430
  106.7 8.4 %collective-permute-start.38 = (bf16[2,128,512]{2,1,0:T(8,128)(2,1)S(1)}, bf16[2,128,512]{2,1,0:T(8,128)(2,1)S(1)}, u32[]{:S(2)}, u32[]{:S(2)}) collective-permute-start(bf16[2,128,512]{2,1,0:T(8,128)(2,1)S(1)} %subtract_convert_fusion.refs_8_), channel_id=1, source_target_pairs={{0,4},{1,3},{2,6},{3,1},{4,0},{5,7},{6,2},{7,5},{8,12},{9,11},{10,... | collective-permute-start | bytes 786440 | tf_op jit(solution)/shard_map/ppermute | solution.py:431
  111.6 3.5 %collective-permute-start.40 = (bf16[2,128,512]{2,1,0:T(8,128)(2,1)S(1)}, bf16[2,128,512]{2,1,0:T(8,128)(2,1)S(1)}, u32[]{:S(2)}, u32[]{:S(2)}) collective-permute-start(bf16[2,128,512]{2,1,0:T(8,128)(2,1)S(1)} %subtract_convert_fusion.refs_8_), channel_id=1, source_target_pairs={{0,1},{1,0},{2,3},{3,2},{4,5},{5,4},{6,7},{7,6},{8,9},{9,8},{10,11... | collective-permute-start | bytes 786440 | tf_op jit(solution)/shard_map/ppermute | solution.py:434
  111.6 6.4 %collective-permute-start.28 = (bf16[2,128,512]{2,1,0:T(8,128)(2,1)S(1)}, bf16[2,128,512]{2,1,0:T(8,128)(2,1)S(1)}, u32[]{:S(2)}, u32[]{:S(2)}) collective-permute-start(bf16[2,128,512]{2,1,0:T(8,128)(2,1)S(1)} %collective-permute-done.26.refs_1_), channel_id=1, source_target_pairs={{0,4},{1,3},{2,6},{3,1},{4,0},{5,7},{6,2},{7,5},{8,12},{9,11},{10,... | collective-permute-start | bytes 786440 | tf_op jit(solution)/shard_map/ppermute | solution.py:432
  112.3 5.6 %collective-permute-start.30 = (bf16[2,128,512]{2,1,0:T(8,128)(2,1)S(1)}, bf16[2,128,512]{2,1,0:T(8,128)(2,1)S(1)}, u32[]{:S(2)}, u32[]{:S(2)}) collective-permute-start(bf16[2,128,512]{2,1,0:T(8,128)(2,1)S(1)} %collective-permute-done.26.refs_1_), channel_id=1, source_target_pairs={{0,1},{1,0},{2,3},{3,2},{4,5},{5,4},{6,7},{7,6},{8,9},{9,8},{10,11... | collective-permute-start | bytes 786440 | tf_op jit(solution)/shard_map/ppermute | solution.py:434
  114.4 6.4 %collective-permute-start.39 = (bf16[2,128,512]{2,1,0:T(8,128)(2,1)S(1)}, bf16[2,128,512]{2,1,0:T(8,128)(2,1)S(1)}, u32[]{:S(2)}, u32[]{:S(2)}) collective-permute-start(bf16[2,128,512]{2,1,0:T(8,128)(2,1)S(1)} %collective-permute-done.37.refs_9_), channel_id=1, source_target_pairs={{0,4},{1,3},{2,6},{3,1},{4,0},{5,7},{6,2},{7,5},{8,12},{9,11},{10,... | collective-permute-start | bytes 786440 | tf_op jit(solution)/shard_map/ppermute | solution.py:432
  115.1 7.9 %collective-permute-start.31 = (bf16[2,128,512]{2,1,0:T(8,128)(2,1)S(1)}, bf16[2,128,512]{2,1,0:T(8,128)(2,1)S(1)}, u32[]{:S(2)}, u32[]{:S(2)}) collective-permute-start(bf16[2,128,512]{2,1,0:T(8,128)(2,1)S(1)} %collective-permute-done.27.refs_2_), channel_id=1, source_target_pairs={{0,1},{1,0},{2,3},{3,2},{4,5},{5,4},{6,7},{7,6},{8,9},{9,8},{10,11... | collective-permute-start | bytes 786440 | tf_op jit(solution)/shard_map/ppermute | solution.py:434
  115.1 7.9 %collective-permute-start.41 = (bf16[2,128,512]{2,1,0:T(8,128)(2,1)S(1)}, bf16[2,128,512]{2,1,0:T(8,128)(2,1)S(1)}, u32[]{:S(2)}, u32[]{:S(2)}) collective-permute-start(bf16[2,128,512]{2,1,0:T(8,128)(2,1)S(1)} %collective-permute-done.37.refs_9_), channel_id=1, source_target_pairs={{0,1},{1,0},{2,3},{3,2},{4,5},{5,4},{6,7},{7,6},{8,9},{9,8},{10,11... | collective-permute-start | bytes 786440 | tf_op jit(solution)/shard_map/ppermute | solution.py:434
  117.9 5.1 %collective-permute-start.42 = (bf16[2,128,512]{2,1,0:T(8,128)(2,1)S(1)}, bf16[2,128,512]{2,1,0:T(8,128)(2,1)}, u32[]{:S(2)}, u32[]{:S(2)}) collective-permute-start(bf16[2,128,512]{2,1,0:T(8,128)(2,1)S(1)} %collective-permute-done.38.refs_10_), channel_id=1, source_target_pairs={{0,1},{1,0},{2,3},{3,2},{4,5},{5,4},{6,7},{7,6},{8,9},{9,8},{10,11... | collective-permute-start | bytes 786440 | tf_op jit(solution)/shard_map/ppermute | solution.py:434
  118.0 5.1 %collective-permute-start.32 = (bf16[2,128,512]{2,1,0:T(8,128)(2,1)S(1)}, bf16[2,128,512]{2,1,0:T(8,128)(2,1)}, u32[]{:S(2)}, u32[]{:S(2)}) collective-permute-start(bf16[2,128,512]{2,1,0:T(8,128)(2,1)S(1)} %collective-permute-done.28.refs_3_), channel_id=1, source_target_pairs={{0,1},{1,0},{2,3},{3,2},{4,5},{5,4},{6,7},{7,6},{8,9},{9,8},{10,11... | collective-permute-start | bytes 786440 | tf_op jit(solution)/shard_map/ppermute | solution.py:434
  120.8 2.3 %collective-permute-start.43 = (bf16[2,128,512]{2,1,0:T(8,128)(2,1)S(1)}, bf16[2,128,512]{2,1,0:T(8,128)(2,1)}, u32[]{:S(2)}, u32[]{:S(2)}) collective-permute-start(bf16[2,128,512]{2,1,0:T(8,128)(2,1)S(1)} %collective-permute-done.39.refs_11_), channel_id=1, source_target_pairs={{0,1},{1,0},{2,3},{3,2},{4,5},{5,4},{6,7},{7,6},{8,9},{9,8},{10,11... | collective-permute-start | bytes 786440 | tf_op jit(solution)/shard_map/ppermute | solution.py:434
  130.5 16.4 %collective-permute-start.44 = (bf16[2,256,512]{2,1,0:T(8,128)(2,1)S(1)}, bf16[2,256,512]{2,1,0:T(8,128)(2,1)S(1)}, u32[]{:S(2)}, u32[]{:S(2)}) collective-permute-start(bf16[2,256,512]{2,1,0:T(8,128)(2,1)S(1)} %get-tuple-element.34), channel_id=1, source_target_pairs={{0,8},{24,16},{16,0},{8,24},{1,9},{25,17},{17,1},{9,25},{2,10},{26... | collective-permute-start | bytes 1572872 | tf_op jit(solution)/shard_map/ppermute | solution.py:485
  142.4 16.7 %collective-permute-start.45 = (bf16[2,256,512]{2,1,0:T(8,128)(2,1)S(1)}, bf16[2,256,512]{2,1,0:T(8,128)(2,1)S(1)}, u32[]{:S(2)}, u32[]{:S(2)}) collective-permute-start(bf16[2,256,512]{2,1,0:T(8,128)(2,1)S(1)} %get-tuple-element.31), channel_id=1, source_target_pairs={{0,8},{8,0},{24,16},{1,9},{9,1},{25,17},{2,10},{10,2},{26,18},{3,1... | collective-permute-start | bytes 1572872 | tf_op jit(solution)/shard_map/ppermute | solution.py:490
  144.3 14.7 %collective-permute-start.47 = (bf16[2,256,512]{2,1,0:T(8,128)(2,1)S(1)}, bf16[2,256,512]{2,1,0:T(8,128)(2,1)S(1)}, u32[]{:S(2)}, u32[]{:S(2)}) collective-permute-start(bf16[2,256,512]{2,1,0:T(8,128)(2,1)S(1)} %get-tuple-element.33), channel_id=1, source_target_pairs={{0,24},{24,0},{1,25},{25,1},{2,26},{26,2},{3,27},{27,3},{4,28},{28... | collective-permute-start | bytes 1572872 | tf_op jit(solution)/shard_map/ppermute | solution.py:487
  147.1 27.0 %collective-permute-start.46 = (bf16[2,256,512]{2,1,0:T(8,128)(2,1)S(1)}, bf16[2,256,512]{2,1,0:T(8,128)(2,1)S(1)}, u32[]{:S(2)}, u32[]{:S(2)}) collective-permute-start(bf16[2,256,512]{2,1,0:T(8,128)(2,1)S(1)} %fusion), channel_id=1, source_target_pairs={{8,16},{16,8},{9,17},{17,9},{10,18},{18,10},{11,19},{19,11},{12,20... | collective-permute-start | bytes 1572872 | tf_op jit(solution)/shard_map/ppermute | solution.py:489
  (3 other events, 55.5 us)
